TPU v7x, 32 devices: a whole 2x2x4 slice. The times are simulated.
32 devices in a mesh: grp: 2 (over x), lat: 16 (over z, y, core).
Axes of the slice: x: 2, y: 2, z: 4, core: 2. Of those that a mesh axis runs over, the one named last changes fastest.
Arguments:
- noisy_state: bfloat16 [160, 128, 1024], P('grp', 'lat'), parts along dimension 0, may hold values from -6 to 6
- w_first: bfloat16 [3, 3, 80, 80], replicated, may hold values from -0.21875 to 0.21875
- w_second: bfloat16 [3, 3, 80, 80], replicated, may hold values from -0.21875 to 0.21875
- prior_weight: float32 [80], replicated, may hold values from 0.5 to 2
- obs_weight: float32 [80], replicated, may hold values from 0.5 to 2
- block_route: int32 [32, 9], P(('grp', 'lat')), parts along dimension 0, may hold values from 0 to 31
- counts: int32 [32, 9], P(('grp', 'lat')), parts along dimension 0, may hold values from 0 to 128, as said below
- tile_weights: bfloat16 [32, 9, 128, 256], P(('grp', 'lat')), parts along dimension 0, may hold values from -0.375 to 0.375
- observations: bfloat16 [32, 9, 80, 128], P(('grp', 'lat')), parts along dimension 0, may hold values from -6 to 6
Outputs:
- posterior_score: bfloat16 [160, 128, 1024], P('grp', 'lat'), parts along dimension 0
There are 2 independent parts, one for each index of `grp`. A program takes and returns all parts, laid end to end along the dimension named above; an argument that names none is the same for every part. Nothing has to cross between parts.
Inputs may be any that keep to these rules, and one draw needn't show every extreme that they name: counts[o, k] tells how many of tile k's first retrievals are live; it is 0 where band o - k + 4 lies outside the grid; owners carry uneven numbers of live tiles.
All inputs are finite; a program needn't handle non-finite values.
Results may differ from a plain program's by a relative error of at most 0.0058.
Values may be sent and summed in bfloat16 or wider, within the bound.
No kernel may reach another device: no remote copies, remote signals or barrier semaphores. Data moves between devices by JAX's collectives and lax.ppermute only.
A program may use at most 64 MiB of HBM per device.

v0:
```python
import functools

import jax
import jax.numpy as jnp
from jax import lax
from jax.experimental import pallas as pl
from jax.experimental.pallas import tpu as pltpu
from jax.sharding import PartitionSpec as P

BLK_LAT = 2
BLK_LON = 128
HALO = 2
F32 = jnp.float32
BF16 = jnp.bfloat16

VM = pl.BlockSpec(memory_space=pltpu.VMEM)
SM = pl.BlockSpec(memory_space=pltpu.SMEM)


def params(mib=40):
    return pltpu.CompilerParams(vmem_limit_bytes=mib << 20)


def rows(index, count, channels):
    return pl.ds(pl.multiple_of(index * channels, 16), count * channels)


def permutation(height, group):
    n = height * group
    out = lax.broadcasted_iota(jnp.int32, (n, n), 0)
    src = lax.broadcasted_iota(jnp.int32, (n, n), 1)
    want = (out % group) * height + out // group
    return jnp.where(src == want, 1.0, 0.0).astype(BF16)


def back_permutation(height, group):
    n = height * group
    out = lax.broadcasted_iota(jnp.int32, (n, n), 0)
    src = lax.broadcasted_iota(jnp.int32, (n, n), 1)
    want = (out % height) * group + out // height
    return jnp.where(src == want, 1.0, 0.0).astype(BF16)


def channel_groups(channels):
    groups, start = [], 0
    while start < channels:
        size = min(32, channels - start)
        groups.append((start, size))
        start += size
    return groups


def pack_tile(k, dst, w_ref, obs_ref, count_ref, slots, channels):
    live = lax.broadcasted_iota(jnp.int32, (slots, BLK_LON), 0) < count_ref[k]
    zero = jnp.zeros((slots, BLK_LON), BF16)
    for i in range(BLK_LAT):
        half = w_ref[k, :, i * BLK_LON : (i + 1) * BLK_LON]
        dst[i * slots : (i + 1) * slots, :] = jnp.where(live, half, zero)
    dst[BLK_LAT * slots : BLK_LAT * slots + channels, :] = obs_ref[k]


def prepare_kernel(
    channels, height, span,
    where_ref, count_ref, x_ref, w_ref, obs_ref,
    xt_ref, ha_ref, hb_ref, za_ref, zb_ref, own_ref,
):
    for start, size in channel_groups(channels):
        n = size * height
        moved = jnp.dot(
            permutation(height, size),
            x_ref[start * height : start * height + n, :],
            preferred_element_type=F32,
        ).astype(BF16)
        for r in range(height):
            xt_ref[r * channels + start : r * channels + start + size, :] = (
                moved[r * size : (r + 1) * size, :]
            )
    odd = where_ref[0] % 2
    last = height - HALO
    ha_ref[...] = xt_ref[rows(last * (1 - odd), HALO, channels), :]
    hb_ref[...] = xt_ref[rows(last * odd, HALO, channels), :]
    slots = w_ref.shape[1]
    p = where_ref[0] % span
    z_odd = (where_ref[0] // span) % 2
    pack = functools.partial(
        pack_tile, w_ref=w_ref, obs_ref=obs_ref, count_ref=count_ref, slots=slots, channels=channels
    )
    for j in range(span):
        up = jnp.maximum(p - j, 0)
        down = jnp.minimum(2 * span + p - j, 2 * span)
        pack(jnp.where(z_odd == 1, down, up), za_ref.at[j])
        pack(jnp.where(z_odd == 1, up, down), zb_ref.at[j])
        if j == 0:
            pack(span, own_ref.at[0])
        else:
            pack(span + p - lax.bitwise_xor(p, j), own_ref.at[j])


def relay_kernel(span, where_ref, za_ref, zb_ref, own_ref, *outs):
    p = where_ref[0] % span
    z_odd = (where_ref[0] // span) % 2
    for m in range(1, span):
        to = lax.bitwise_xor(p, m)
        below = jnp.where(to < p, 1, 0)
        outs[m - 1][0] = own_ref[m]

        @pl.when(below == z_odd)
        def _():
            outs[m - 1][1] = za_ref[to]

        @pl.when(below != z_odd)
        def _():
            outs[m - 1][1] = zb_ref[to]


def conv_row(w_ref, src_ref, index, channels):
    depth = w_ref.shape[1]
    window = src_ref[pl.ds(pl.multiple_of(index * channels, 16), depth), :]
    taps = jnp.dot(w_ref[...], window, preferred_element_type=F32)
    width = taps.shape[1]
    return (
        pltpu.roll(taps[0:channels], 1, 1)
        + taps[channels : 2 * channels]
        + pltpu.roll(taps[2 * channels : 3 * channels], width - 1, 1)
    )


def fill(ext, mid, a_ref, b_ref, where_ref, channels, height):
    odd = where_ref[0] % 2
    ext[HALO * channels : (HALO + height) * channels, :] = mid
    top = jnp.where(odd == 1, 0, HALO + height)
    ext[rows(top, HALO, channels), :] = a_ref[...]
    ext[rows(HALO + height - top, HALO, channels), :] = b_ref[...]
    tail = (2 * HALO + height) * channels
    if ext.shape[0] > tail:
        ext[tail:, :] = jnp.zeros((ext.shape[0] - tail, ext.shape[1]), BF16)


def forward_kernel(
    channels, height,
    where_ref, xt_ref, a_ref, b_ref, w1_ref, w2_ref,
    res_ref, slope_ref,
    ext, hid,
):
    fill(ext, xt_ref[...], a_ref, b_ref, where_ref, channels, height)
    me, count = where_ref[0], where_ref[1]
    tail = (height + 2) * channels
    hid[tail:, :] = jnp.zeros((hid.shape[0] - tail, hid.shape[1]), BF16)

    def first(e, _):
        act = conv_row(w1_ref, ext, e, channels)
        off = ((e == 0) & (me == 0)) | ((e == height + 1) & (me == count - 1))
        keep = jnp.where(off, 0.0, 1.0)
        gate = keep / (1.0 + jnp.exp(-act))
        hid[rows(e, 1, channels), :] = (act * gate).astype(BF16)
        slope_ref[rows(e, 1, channels), :] = gate * (1.0 + act * (1.0 - gate))
        return 0

    lax.fori_loop(0, height + 2, first, 0)

    def second(r, _):
        res_ref[rows(r, 1, channels), :] = conv_row(w2_ref, hid, r, channels)
        return 0

    lax.fori_loop(0, height, second, 0)


def tile_kernel(
    channels, height, columns, span,
    where_ref, route_ref, xt_ref, res_ref, ow_ref, own_ref, za_ref, zb_ref, p1_ref, p2_ref, p3_ref,
    guide_ref, ga_ref, gb_ref,
):
    slots = BLK_LON
    across = columns // BLK_LON
    p = where_ref[0] % span
    z_odd = (where_ref[0] // span) % 2
    odd = where_ref[0] % 2
    guide_ref[...] = jnp.zeros_like(guide_ref)
    jobs = [
        (span, own_ref.at[0]),
        (jnp.where(z_odd == 1, 0, 2 * span), za_ref.at[p]),
        (jnp.where(z_odd == 1, 2 * span, 0), zb_ref.at[p]),
    ]
    for m, ref in ((1, p1_ref), (2, p2_ref), (3, p3_ref)):
        other = lax.bitwise_xor(p, m)
        step = other - p
        jobs.append((span + step, ref.at[0]))
        jobs.append((jnp.where(step > 0, step, 2 * span + step), ref.at[1]))
    obs_weight = ow_ref[...]
    places = []
    terms = []
    for k, ref in jobs:
        n = route_ref[k]
        r, q = n // across, n % across
        place = [
            (rows(r * BLK_LAT + i, 1, channels), pl.ds(pl.multiple_of(q * BLK_LON, BLK_LON), BLK_LON))
            for i in range(BLK_LAT)
        ]
        predicted = jnp.zeros((channels, slots), F32)
        for i in range(BLK_LAT):
            block = (xt_ref[place[i]].astype(F32) + res_ref[place[i]]).astype(BF16)
            predicted += lax.dot_general(
                block,
                ref[i * slots : (i + 1) * slots, :],
                (((1,), (1,)), ((), ())),
                preferred_element_type=F32,
            )
        obs = ref[BLK_LAT * slots : BLK_LAT * slots + channels, :].astype(F32)
        misfit = ((obs - predicted) * obs_weight).astype(BF16)
        places.append(place)
        terms.append(
            [
                jnp.dot(misfit, ref[i * slots : (i + 1) * slots, :], preferred_element_type=F32)
                .astype(BF16)
                .astype(F32)
                for i in range(BLK_LAT)
            ]
        )
    for place, term in zip(places, terms):
        for i in range(BLK_LAT):
            guide_ref[place[i]] += term[i]
    last = height - HALO
    ga_ref[...] = guide_ref[rows(last * (1 - odd), HALO, channels), :].astype(BF16)
    gb_ref[...] = guide_ref[rows(last * odd, HALO, channels), :].astype(BF16)


def backward_kernel(
    channels, height,
    where_ref, guide_ref, a_ref, b_ref, slope_ref, res_ref, prior_ref, w2_ref, w1_ref,
    out_ref,
    ext, adj, score,
):
    fill(ext, guide_ref[...].astype(BF16), a_ref, b_ref, where_ref, channels, height)
    tail = (height + 2) * channels
    adj[tail:, :] = jnp.zeros((adj.shape[0] - tail, adj.shape[1]), BF16)

    def first(e, _):
        back = conv_row(w2_ref, ext, e, channels)
        adj[rows(e, 1, channels), :] = (slope_ref[rows(e, 1, channels), :] * back).astype(BF16)
        return 0

    lax.fori_loop(0, height + 2, first, 0)

    def second(r, _):
        here = rows(r, 1, channels)
        back = conv_row(w1_ref, adj, r, channels)
        score[here, :] = (prior_ref[...] * res_ref[here, :] + guide_ref[here, :] + back).astype(BF16)
        return 0

    lax.fori_loop(0, height, second, 0)
    for start, size in channel_groups(channels):
        n = size * height
        picked = jnp.concatenate(
            [score[r * channels + start : r * channels + start + size, :] for r in range(height)], axis=0
        )
        out_ref[start * height : start * height + n, :] = jnp.dot(
            back_permutation(height, size), picked, preferred_element_type=F32
        ).astype(BF16)


def stacked(weights, flip):
    if flip:
        weights = weights[::-1, ::-1].transpose(1, 3, 0, 2)
    else:
        weights = weights.transpose(1, 2, 0, 3)
    taps, outs, row_taps, ins = weights.shape
    matrix = weights.reshape(taps * outs, row_taps * ins)
    depth = matrix.shape[1]
    return jnp.pad(matrix, ((0, 0), (0, -depth % 256)))


def pairs(count, step, parity):
    found = []
    for i in range(count):
        other = i + step if (i // step) % 2 == parity else i - step
        if 0 <= other < count:
            found.append((i, other))
    return found


def local(
    noisy_state, w_first, w_second, prior_weight, obs_weight, block_route, counts, tile_weights, observations
):
    channels, height, columns = noisy_state.shape
    tile_total = block_route.shape[1]
    span = tile_total // 2
    slots = tile_weights.shape[2]
    count = lax.axis_size("lat")
    where = jnp.stack([lax.axis_index("lat"), jnp.int32(count)]).astype(jnp.int32)
    pack_rows = BLK_LAT * slots + channels
    field = (height * channels, columns)

    def swap(x, step, parity):
        return lax.ppermute(x, "lat", pairs(count, step, parity))

    def shape(dims, dtype=BF16):
        return jax.ShapeDtypeStruct(dims, dtype)

    xt, ha, hb, za, zb, own = pl.pallas_call(
        functools.partial(prepare_kernel, channels, height, span),
        out_shape=(
            shape(field),
            shape((HALO * channels, columns)),
            shape((HALO * channels, columns)),
            shape((span, pack_rows, BLK_LON)),
            shape((span, pack_rows, BLK_LON)),
            shape((span, pack_rows, BLK_LON)),
        ),
        in_specs=[SM, SM, VM, VM, VM],
        out_specs=[VM] * 6,
        compiler_params=params(),
    )(where, counts[0], noisy_state.reshape(channels * height, columns), tile_weights[0], observations[0])
    ha, hb = swap(ha, 1, 0), swap(hb, 1, 1)
    za, zb = swap(za, span, 0), swap(zb, span, 1)
    relayed = pl.pallas_call(
        functools.partial(relay_kernel, span),
        out_shape=tuple(shape((2, pack_rows, BLK_LON)) for _ in range(span - 1)),
        in_specs=[SM, VM, VM, VM],
        out_specs=[VM] * (span - 1),
        compiler_params=params(),
    )(where, za, zb, own)
    arrived = [
        lax.ppermute(relayed[m - 1], "lat", [(i, i ^ m) for i in range(count)]) for m in range(1, span)
    ]
    w1, w2 = stacked(w_first, False), stacked(w_second, False)
    w1t, w2t = stacked(w_first, True), stacked(w_second, True)
    pad = w1.shape[1] - 3 * channels
    ext_rows = (height + 2 * HALO) * channels + pad
    mid_rows = (height + 2) * channels + pad
    res, slope = pl.pallas_call(
        functools.partial(forward_kernel, channels, height),
        out_shape=(shape(field, F32), shape(((height + 2) * channels, columns), F32)),
        in_specs=[SM] + [VM] * 5,
        out_specs=[VM] * 2,
        scratch_shapes=[pltpu.VMEM((ext_rows, columns), BF16), pltpu.VMEM((mid_rows, columns), BF16)],
        compiler_params=params(),
    )(where, xt, ha, hb, w1, w2)
    guide, ga, gb = pl.pallas_call(
        functools.partial(tile_kernel, channels, height, columns, span),
        out_shape=(
            shape(field, F32),
            shape((HALO * channels, columns)),
            shape((HALO * channels, columns)),
        ),
        in_specs=[SM, SM] + [VM] * 9,
        out_specs=[VM] * 3,
        compiler_params=params(),
    )(where, block_route[0], xt, res, obs_weight[:, None], own, za, zb, *arrived)
    ga, gb = swap(ga, 1, 0), swap(gb, 1, 1)
    out = pl.pallas_call(
        functools.partial(backward_kernel, channels, height),
        out_shape=shape(field),
        in_specs=[SM] + [VM] * 8,
        out_specs=VM,
        scratch_shapes=[
            pltpu.VMEM((ext_rows, columns), BF16),
            pltpu.VMEM((mid_rows, columns), BF16),
            pltpu.VMEM(field, BF16),
        ],
        compiler_params=params(),
    )(where, guide, ga, gb, slope, res, prior_weight[:, None], w2t, w1t)
    return out.reshape(channels, height, columns)


def solution(mesh):
    in_specs = (
        P("grp", "lat", None),
        P(),
        P(),
        P(),
        P(),
        P(("grp", "lat"), None),
        P(("grp", "lat"), None),
        P(("grp", "lat"), None, None, None),
        P(("grp", "lat"), None, None, None),
    )
    out_specs = P("grp", "lat", None)
    return jax.shard_map(local, mesh=mesh, in_specs=in_specs, out_specs=out_specs, check_vma=False)
```

profile of v0, /device:TPU:17, one launch (start us, length us, event | category | flops | bytes accessed | tf_op | source)
XLA Modules:
  0.0 78.3 jit_solution(15864583339805038838)
XLA Ops:
  0.0 0.1 pad_add_fusion.where_ref
  0.1 1.3 %copy-done.8 = bf16[80,8,1024]{2,1,0:T(8,128)(2,1)S(1)} copy-done((bf16[80,8,1024]{2,1,0:T(8,128)(2,1)S(1)}, bf16[80,8,1024]{2,1,0:T(8,128)(2,1)}, u32[]{:S(2)}) %copy-start.8) | copy-done | bytes 1310744
  1.4 1.1 %copy-done.9 = bf16[1,9,128,256]{3,2,1,0:T(8,128)(2,1)S(1)} copy-done((bf16[1,9,128,256]{3,2,1,0:T(8,128)(2,1)S(1)}, bf16[1,9,128,256]{3,2,1,0:T(8,128)(2,1)}, u32[]{:S(2)}) %copy-start.9) | copy-done | bytes 589848
  2.5 0.9 %copy-done.14 = bf16[1,9,80,128]{3,2,1,0:T(8,128)(2,1)S(1)} copy-done((bf16[1,9,80,128]{3,2,1,0:T(8,128)(2,1)S(1)}, bf16[1,9,80,128]{3,2,1,0:T(8,128)(2,1)}, u32[]{:S(2)}) %copy-start.14) | copy-done | bytes 184344
  3.4 0.7 copy-done.21
  4.0 1.2 %shard_map.91 = (bf16[640,1024]{1,0:T(8,128)(2,1)S(1)}, bf16[160,1024]{1,0:T(8,128)(2,1)S(1)}, bf16[160,1024]{1,0:T(8,128)(2,1)S(1)}, bf16[4,336,128]{2,1,0:T(8,...) custom-call(s32[2]{0:T(128)S(1)} %pad_add_fusion.where_ref, s32[9]{0:T(128)S(1)} %bitcast.19, ...), custom_call_target="tpu_custom_call" | custom-call | tf_op jit(solution)/shard_map/pallas_call | solution.py:299
  5.3 0.0 copy-start
  5.3 1.0 %copy-done = bf16[640,1024]{1,0:T(8,128)(2,1)} copy-done((bf16[640,1024]{1,0:T(8,128)(2,1)}, bf16[640,1024]{1,0:T(8,128)(2,1)S(1)}, u32[]{:S(2)}) %copy-start) | copy-done | bytes 1310744
  6.3 1.3 %collective-permute-start.2 = (bf16[4,336,128]{2,1,0:T(8,128)(2,1)S(1)}, bf16[4,336,128]{2,1,0:T(8,128)(2,1)S(1)}, u32[]{:S(2)}, u32[]{:S(2)}) collective-permute-start(bf16[4,336,128]{2,1,0:T(8,128)(2,1)S(1)} %get-tuple-element.24), channel_id=1, source_target_pairs={{0,4},{1,5},{2,6},{3,7},{4,0},{5,1},{6,2},{7,3},{8,12},{9,13},{10,... | collective-permute-start | bytes 1032200 | tf_op jit(solution)/shard_map/ppermute | solution.py:294
  7.6 1.9 %collective-permute-start.3 = (bf16[4,336,128]{2,1,0:T(8,128)(2,1)S(1)}, bf16[4,336,128]{2,1,0:T(8,128)(2,1)S(1)}, u32[]{:S(2)}, u32[]{:S(2)}) collective-permute-start(bf16[4,336,128]{2,1,0:T(8,128)(2,1)S(1)} %get-tuple-element.25), channel_id=1, source_target_pairs={{4,8},{5,9},{6,10},{7,11},{8,4},{9,5},{10,6},{11,7},{20,24},{21,25... | collective-permute-start | bytes 1032200 | tf_op jit(solution)/shard_map/ppermute | solution.py:294
  9.6 1.0 %collective-permute-start = (bf16[160,1024]{1,0:T(8,128)(2,1)S(1)}, bf16[160,1024]{1,0:T(8,128)(2,1)S(1)}, u32[]{:S(2)}, u32[]{:S(2)}) collective-permute-start(bf16[160,1024]{1,0:T(8,128)(2,1)S(1)} %get-tuple-element.20), channel_id=1, source_target_pairs={{0,1},{1,0},{2,3},{3,2},{4,5},{5,4},{6,7},{7,6},{8,9},{9,8},{10,11... | collective-permute-start | bytes 983048 | tf_op jit(solution)/shard_map/ppermute | solution.py:294
  10.6 3.0 %collective-permute-start.1 = (bf16[160,1024]{1,0:T(8,128)(2,1)S(1)}, bf16[160,1024]{1,0:T(8,128)(2,1)S(1)}, u32[]{:S(2)}, u32[]{:S(2)}) collective-permute-start(bf16[160,1024]{1,0:T(8,128)(2,1)S(1)} %get-tuple-element.21), channel_id=1, source_target_pairs={{1,2},{2,1},{3,4},{4,3},{5,6},{6,5},{7,8},{8,7},{9,10},{10,9},{11,... | collective-permute-start | bytes 983048 | tf_op jit(solution)/shard_map/ppermute | solution.py:294
  13.6 1.7 %collective-permute-done.2.za_ref = bf16[4,336,128]{2,1,0:T(8,128)(2,1)S(1)} collective-permute-done((bf16[4,336,128]{2,1,0:T(8,128)(2,1)S(1)}, bf16[4,336,128]{2,1,0:T(8,128)(2,1)S(1)}, u32[]{:S(2)}, u32[]{:S(2)}) %collective-permute-start.2) | collective-permute-done | bytes 344096 | tf_op jit(solution)/shard_map/ppermute | solution.py:294
  15.3 2.9 %collective-permute-done.3.zb_ref = bf16[4,336,128]{2,1,0:T(8,128)(2,1)S(1)} collective-permute-done((bf16[4,336,128]{2,1,0:T(8,128)(2,1)S(1)}, bf16[4,336,128]{2,1,0:T(8,128)(2,1)S(1)}, u32[]{:S(2)}, u32[]{:S(2)}) %collective-permute-start.3) | collective-permute-done | bytes 344096 | tf_op jit(solution)/shard_map/ppermute | solution.py:294
  18.1 1.4 %shard_map.93 = (bf16[2,336,128]{2,1,0:T(8,128)(2,1)}, bf16[2,336,128]{2,1,0:T(8,128)(2,1)}, bf16[2,336,128]{2,1,0:T(8,128)(2,1)}) custom-call(s32[2]{0:T(128)S(1)} %pad_add_fusion.where_ref, bf16[4,336,128]{2,1,0:T(8,128)(2,1)S(1)} %collective-permute-done.2.za_ref, bf16[4,336,128]{2,1,0:T(8,128)(2,1)S(1)} %collective-permute-done.3.zb_ref, ...), custom_call_target="tpu_custom_call" | custom-call | tf_op jit(solution)/shard_map/pallas_call | solution.py:315
  19.5 0.7 copy-done.6
  20.3 1.9 %collective-permute-start.4 = (bf16[2,336,128]{2,1,0:T(8,128)(2,1)}, bf16[2,336,128]{2,1,0:T(8,128)(2,1)}, u32[]{:S(2)}, u32[]{:S(2)}) collective-permute-start(bf16[2,336,128]{2,1,0:T(8,128)(2,1)} %get-tuple-element.26), channel_id=1, source_target_pairs={{0,1},{1,0},{2,3},{3,2},{4,5},{5,4},{6,7},{7,6},{8,9},{9,8},{10,11... | collective-permute-start | bytes 516104 | tf_op jit(solution)/shard_map/ppermute | solution.py:323
  22.1 2.7 %collective-permute-start.5 = (bf16[2,336,128]{2,1,0:T(8,128)(2,1)}, bf16[2,336,128]{2,1,0:T(8,128)(2,1)}, u32[]{:S(2)}, u32[]{:S(2)}) collective-permute-start(bf16[2,336,128]{2,1,0:T(8,128)(2,1)} %get-tuple-element.27), channel_id=1, source_target_pairs={{0,2},{1,3},{2,0},{3,1},{4,6},{5,7},{6,4},{7,5},{8,10},{9,11},{10,... | collective-permute-start | bytes 516104 | tf_op jit(solution)/shard_map/ppermute | solution.py:323
  24.8 0.0 collective-permute-start.6
  24.8 0.0 copy-done.24
  24.8 0.1 copy.16
  24.9 0.2 reshape.19
  25.1 0.1 copy.17
  25.2 0.2 reshape.20
  25.4 0.7 copy.18.ow_ref
  26.2 0.0 collective-permute-done.a_ref
  26.2 0.7 copy-done.10
  26.9 0.0 collective-permute-done.1.b_ref
  26.9 0.7 copy-done.12
  27.6 1.3 %copy-done.1 = bf16[640,1024]{1,0:T(8,128)(2,1)S(1)} copy-done((bf16[640,1024]{1,0:T(8,128)(2,1)S(1)}, bf16[640,1024]{1,0:T(8,128)(2,1)}, u32[]{:S(2)}) %copy-start.1) | copy-done | bytes 1310744
  28.9 1.0 %copy-done.11 = bf16[160,1024]{1,0:T(8,128)(2,1)S(1)} copy-done((bf16[160,1024]{1,0:T(8,128)(2,1)S(1)}, bf16[160,1024]{1,0:T(8,128)(2,1)}, u32[]{:S(2)}) %copy-start.11) | copy-done | bytes 327704
  29.9 1.0 %copy-done.13 = bf16[160,1024]{1,0:T(8,128)(2,1)S(1)} copy-done((bf16[160,1024]{1,0:T(8,128)(2,1)S(1)}, bf16[160,1024]{1,0:T(8,128)(2,1)}, u32[]{:S(2)}) %copy-start.13) | copy-done | bytes 327704
  30.9 0.6 copy-done.18
  31.5 8.7 %shard_map.92 = (f32[640,1024]{1,0:T(8,128)S(1)}, f32[800,1024]{1,0:T(8,128)S(1)}) custom-call(s32[2]{0:T(128)S(1)} %copy-done.18, bf16[640,1024]{1,0:T(8,128)(2,1)S(1)} %copy-done.1, bf16[160,1024]{1,0:T(8,128)(2,1)S(1)} %copy-done.11, bf16[160,1024]{1,0:T(8,128)(2,1)S(1)} %copy-done.13, bf16[240,256]{1,0:T(8,128)(2,1)S(1)} %pad.13.w1_ref, ...), custom_call_target="tpu_custom_call" | custom-call | tf_op jit(solution)/shard_map/pallas_call | solution.py:330
  40.2 0.0 copy-start.2
  40.2 1.7 %copy-done.2 = f32[800,1024]{1,0:T(8,128)} copy-done((f32[800,1024]{1,0:T(8,128)}, f32[800,1024]{1,0:T(8,128)S(1)}, u32[]{:S(2)}) %copy-start.2) | copy-done | bytes 3276824
  41.9 0.0 collective-permute-done.4.p1_ref
  41.9 0.0 collective-permute-done.5.p2_ref
  41.9 0.0 collective-permute-done.6.p3_ref
  41.9 0.0 copy-start.7
  41.9 1.0 %copy-done.7 = bf16[4,336,128]{2,1,0:T(8,128)(2,1)S(1)} copy-done((bf16[4,336,128]{2,1,0:T(8,128)(2,1)S(1)}, bf16[4,336,128]{2,1,0:T(8,128)(2,1)}, u32[]{:S(2)}) %copy-start.7) | copy-done | bytes 344088
  42.9 0.8 copy-done.15
  43.7 0.7 copy-done.20
  44.3 4.0 %shard_map.94 = (f32[640,1024]{1,0:T(8,128)S(1)}, bf16[160,1024]{1,0:T(8,128)(2,1)}, bf16[160,1024]{1,0:T(8,128)(2,1)}) custom-call(s32[2]{0:T(128)S(1)} %copy-done.18, s32[9]{0:T(128)S(1)} %bitcast.18, bf16[640,1024]{1,0:T(8,128)(2,1)S(1)} %copy-done.1, f32[640,1024]{1,0:T(8,128)S(1)} %get-tuple-element.22.res_ref, f32[80,1]{1,0:T(8,128)S(1)} %copy-done.15, ...), custom_call_target="tpu_custom_call" | custom-call | tf_op jit(solution)/shard_map/pallas_call | solution.py:338
  48.3 1.5 %copy-done.4 = f32[640,1024]{1,0:T(8,128)} copy-done((f32[640,1024]{1,0:T(8,128)}, f32[640,1024]{1,0:T(8,128)S(1)}, u32[]{:S(2)}) %copy-start.4) | copy-done | bytes 2621464
  49.8 0.4 collective-permute-start.7
  50.2 3.5 %collective-permute-start.8 = (bf16[160,1024]{1,0:T(8,128)(2,1)}, bf16[160,1024]{1,0:T(8,128)(2,1)S(1)}, u32[]{:S(2)}, u32[]{:S(2)}) collective-permute-start(bf16[160,1024]{1,0:T(8,128)(2,1)} %get-tuple-element.31), channel_id=1, source_target_pairs={{1,2},{2,1},{3,4},{4,3},{5,6},{6,5},{7,8},{8,7},{9,10},{10,9},{11,... | collective-permute-start | bytes 983048 | tf_op jit(solution)/shard_map/ppermute | solution.py:294
  53.7 0.7 reverse_bitcast_fusion.1
  54.4 1.1 %copy.19 = bf16[3,80,3,80]{3,2,1,0:T(4,128)(2,1)S(1)} copy(bf16[3,80,3,80]{1,3,0,2:T(8,128)(2,1)} %reverse_bitcast_fusion.1) | data formatting | bytes 230400 | tf_op jit(solution)/shard_map/transpose | solution.py:263
  55.5 0.8 %reshape.21 = bf16[240,240]{1,0:T(8,128)(2,1)} reshape(bf16[3,80,3,80]{3,2,1,0:T(4,128)(2,1)S(1)} %copy.19) | data formatting | bytes 230400 | tf_op jit(solution)/shard_map/reshape | solution.py:267
  56.4 0.9 %pad.15.w2_ref = bf16[240,256]{1,0:T(8,128)(2,1)S(1)} pad(bf16[240,240]{1,0:T(8,128)(2,1)} %reshape.21, bf16[]{:T(256)} %constant.8.clone.1), padding=0_0x0_16 | pad | bytes 238082 | tf_op jit(solution)/shard_map/jit(_pad)/pad | solution.py:269
  57.3 1.6 %reverse_bitcast_fusion = bf16[3,80,3,80]{1,3,0,2:T(8,128)(2,1)} fusion(bf16[3,3,80,80]{3,2,1,0:T(8,128)(2,1)} %param.10), kind=kLoop, calls=%fused_computation | loop fusion | bytes 230400 | tf_op jit(solution)/shard_map/transpose | solution.py:263
  58.9 1.8 %copy.20 = bf16[3,80,3,80]{3,2,1,0:T(4,128)(2,1)} copy(bf16[3,80,3,80]{1,3,0,2:T(8,128)(2,1)} %reverse_bitcast_fusion) | data formatting | bytes 230400 | tf_op jit(solution)/shard_map/transpose | solution.py:263
  60.7 1.8 %reshape.22 = bf16[240,240]{1,0:T(8,128)(2,1)} reshape(bf16[3,80,3,80]{3,2,1,0:T(4,128)(2,1)} %copy.20) | data formatting | bytes 230400 | tf_op jit(solution)/shard_map/reshape | solution.py:267
  62.5 0.9 %pad.16.w1_ref = bf16[240,256]{1,0:T(8,128)(2,1)S(1)} pad(bf16[240,240]{1,0:T(8,128)(2,1)} %reshape.22, bf16[]{:T(256)} %constant.8.clone.1), padding=0_0x0_16 | pad | bytes 238082 | tf_op jit(solution)/shard_map/jit(_pad)/pad | solution.py:269
  63.4 0.0 copy-done.26
  63.4 0.7 copy.21.prior_ref
  64.1 0.0 collective-permute-done.7.a_ref
  64.1 0.0 collective-permute-done.8.b_ref
  64.1 0.0 copy-start.3
  64.1 1.9 %copy-done.3 = f32[800,1024]{1,0:T(8,128)S(1)} copy-done((f32[800,1024]{1,0:T(8,128)S(1)}, f32[800,1024]{1,0:T(8,128)}, u32[]{:S(2)}) %copy-start.3) | copy-done | bytes 3276824
  66.1 1.7 %copy-done.5 = f32[640,1024]{1,0:T(8,128)S(1)} copy-done((f32[640,1024]{1,0:T(8,128)S(1)}, f32[640,1024]{1,0:T(8,128)}, u32[]{:S(2)}) %copy-start.5) | copy-done | bytes 2621464
  67.8 0.8 copy-done.16
  68.6 9.8 %shard_map.95 = bf16[640,1024]{1,0:T(8,128)(2,1)} custom-call(s32[2]{0:T(128)S(1)} %copy-done.19, f32[640,1024]{1,0:T(8,128)S(1)} %copy-done.5, bf16[160,1024]{1,0:T(8,128)(2,1)S(1)} %collective-permute-done.7.a_ref, bf16[160,1024]{1,0:T(8,128)(2,1)S(1)} %collective-permute-done.8.b_ref, f32[800,1024]{1,0:T(8,128)S(1)} %copy-done.3, ...), custom_call_target="tpu_custom_call" | custom-call | tf_op jit(solution)/shard_map/pallas_call | solution.py:350
  (30 shorter events, 0.1 us)
Async XLA Ops:
  0.0 25.4 %copy-start.25 = (f32[80]{0:T(128)S(1)}, f32[80]{0:T(128)}, u32[]{:S(2)}) copy-start(f32[80]{0:T(128)} %param.13) | copy-start | bytes 964
  0.1 26.1 %copy-start.17 = (s32[2]{0:T(128)}, s32[2]{0:T(128)S(1)}, u32[]{:S(2)}) copy-start(s32[2]{0:T(128)S(1)} %pad_add_fusion.where_ref) | copy-start | bytes 28
  0.1 1.3 %copy-start.8 = (bf16[80,8,1024]{2,1,0:T(8,128)(2,1)S(1)}, bf16[80,8,1024]{2,1,0:T(8,128)(2,1)}, u32[]{:S(2)}) copy-start(bf16[80,8,1024]{2,1,0:T(8,128)(2,1)} %param.9) | copy-start | bytes 3932164
  1.4 1.1 %copy-start.9 = (bf16[1,9,128,256]{3,2,1,0:T(8,128)(2,1)S(1)}, bf16[1,9,128,256]{3,2,1,0:T(8,128)(2,1)}, u32[]{:S(2)}) copy-start(bf16[1,9,128,256]{3,2,1,0:T(8,128)(2,1)} %param.16) | copy-start | bytes 1769476
  2.5 0.9 %copy-start.14 = (bf16[1,9,80,128]{3,2,1,0:T(8,128)(2,1)S(1)}, bf16[1,9,80,128]{3,2,1,0:T(8,128)(2,1)}, u32[]{:S(2)}) copy-start(bf16[1,9,80,128]{3,2,1,0:T(8,128)(2,1)} %param.17) | copy-start | bytes 552964
  3.4 0.7 copy-start.21
  4.0 20.8 %copy-start.24 = (bf16[3,3,80,80]{3,2,1,0:T(8,128)(2,1)S(1)}, bf16[3,3,80,80]{3,2,1,0:T(8,128)(2,1)}, u32[]{:S(2)}) copy-start(bf16[3,3,80,80]{3,2,1,0:T(8,128)(2,1)} %param.10) | copy-start | bytes 345604
  4.0 21.1 %copy-start.22 = (bf16[3,3,80,80]{3,2,1,0:T(8,128)(2,1)S(1)}, bf16[3,3,80,80]{3,2,1,0:T(8,128)(2,1)}, u32[]{:S(2)}) copy-start(bf16[3,3,80,80]{3,2,1,0:T(8,128)(2,1)} %param.11) | copy-start | bytes 345604
  5.3 1.1 %copy-start = (bf16[640,1024]{1,0:T(8,128)(2,1)}, bf16[640,1024]{1,0:T(8,128)(2,1)S(1)}, u32[]{:S(2)}) copy-start(bf16[640,1024]{1,0:T(8,128)(2,1)S(1)} %get-tuple-element.19.xt_ref) | copy-start | bytes 3932164
  6.3 8.9 %collective-permute-start.2 = (bf16[4,336,128]{2,1,0:T(8,128)(2,1)S(1)}, bf16[4,336,128]{2,1,0:T(8,128)(2,1)S(1)}, u32[]{:S(2)}, u32[]{:S(2)}) collective-permute-start(bf16[4,336,128]{2,1,0:T(8,128)(2,1)S(1)} %get-tuple-element.24), channel_id=1, source_target_pairs={{0,4},{1,5},{2,6},{3,7},{4,0},{5,1},{6,2},{7,3},{8,12},{9,13},{10,... | collective-permute-start | bytes 1032200 | tf_op jit(solution)/shard_map/ppermute | solution.py:294
  7.6 10.5 %collective-permute-start.3 = (bf16[4,336,128]{2,1,0:T(8,128)(2,1)S(1)}, bf16[4,336,128]{2,1,0:T(8,128)(2,1)S(1)}, u32[]{:S(2)}, u32[]{:S(2)}) collective-permute-start(bf16[4,336,128]{2,1,0:T(8,128)(2,1)S(1)} %get-tuple-element.25), channel_id=1, source_target_pairs={{4,8},{5,9},{6,10},{7,11},{8,4},{9,5},{10,6},{11,7},{20,24},{21,25... | collective-permute-start | bytes 1032200 | tf_op jit(solution)/shard_map/ppermute | solution.py:294
  9.6 16.6 %collective-permute-start = (bf16[160,1024]{1,0:T(8,128)(2,1)S(1)}, bf16[160,1024]{1,0:T(8,128)(2,1)S(1)}, u32[]{:S(2)}, u32[]{:S(2)}) collective-permute-start(bf16[160,1024]{1,0:T(8,128)(2,1)S(1)} %get-tuple-element.20), channel_id=1, source_target_pairs={{0,1},{1,0},{2,3},{3,2},{4,5},{5,4},{6,7},{7,6},{8,9},{9,8},{10,11... | collective-permute-start | bytes 983048 | tf_op jit(solution)/shard_map/ppermute | solution.py:294
  10.6 16.3 %collective-permute-start.1 = (bf16[160,1024]{1,0:T(8,128)(2,1)S(1)}, bf16[160,1024]{1,0:T(8,128)(2,1)S(1)}, u32[]{:S(2)}, u32[]{:S(2)}) collective-permute-start(bf16[160,1024]{1,0:T(8,128)(2,1)S(1)} %get-tuple-element.21), channel_id=1, source_target_pairs={{1,2},{2,1},{3,4},{4,3},{5,6},{6,5},{7,8},{8,7},{9,10},{10,9},{11,... | collective-permute-start | bytes 983048 | tf_op jit(solution)/shard_map/ppermute | solution.py:294
  19.5 0.7 copy-start.6
  20.3 21.6 %collective-permute-start.4 = (bf16[2,336,128]{2,1,0:T(8,128)(2,1)}, bf16[2,336,128]{2,1,0:T(8,128)(2,1)}, u32[]{:S(2)}, u32[]{:S(2)}) collective-permute-start(bf16[2,336,128]{2,1,0:T(8,128)(2,1)} %get-tuple-element.26), channel_id=1, source_target_pairs={{0,1},{1,0},{2,3},{3,2},{4,5},{5,4},{6,7},{7,6},{8,9},{9,8},{10,11... | collective-permute-start | bytes 516104 | tf_op jit(solution)/shard_map/ppermute | solution.py:323
  22.1 19.8 %collective-permute-start.5 = (bf16[2,336,128]{2,1,0:T(8,128)(2,1)}, bf16[2,336,128]{2,1,0:T(8,128)(2,1)}, u32[]{:S(2)}, u32[]{:S(2)}) collective-permute-start(bf16[2,336,128]{2,1,0:T(8,128)(2,1)} %get-tuple-element.27), channel_id=1, source_target_pairs={{0,2},{1,3},{2,0},{3,1},{4,6},{5,7},{6,4},{7,5},{8,10},{9,11},{10,... | collective-permute-start | bytes 516104 | tf_op jit(solution)/shard_map/ppermute | solution.py:323
  24.8 17.1 %collective-permute-start.6 = (bf16[2,336,128]{2,1,0:T(8,128)(2,1)}, bf16[2,336,128]{2,1,0:T(8,128)(2,1)}, u32[]{:S(2)}, u32[]{:S(2)}) collective-permute-start(bf16[2,336,128]{2,1,0:T(8,128)(2,1)} %get-tuple-element.28), channel_id=1, source_target_pairs={{0,3},{1,2},{2,1},{3,0},{4,7},{5,6},{6,5},{7,4},{8,11},{9,10},{10,... | collective-permute-start | bytes 516104 | tf_op jit(solution)/shard_map/ppermute | solution.py:323
  26.2 0.7 copy-start.10
  26.9 0.7 copy-start.12
  27.6 1.3 %copy-start.1 = (bf16[640,1024]{1,0:T(8,128)(2,1)S(1)}, bf16[640,1024]{1,0:T(8,128)(2,1)}, u32[]{:S(2)}) copy-start(bf16[640,1024]{1,0:T(8,128)(2,1)} %copy-done) | copy-start | bytes 3932164
  28.9 1.0 %copy-start.11 = (bf16[160,1024]{1,0:T(8,128)(2,1)S(1)}, bf16[160,1024]{1,0:T(8,128)(2,1)}, u32[]{:S(2)}) copy-start(bf16[160,1024]{1,0:T(8,128)(2,1)} %copy-done.10) | copy-start | bytes 983044
  29.9 1.0 %copy-start.13 = (bf16[160,1024]{1,0:T(8,128)(2,1)S(1)}, bf16[160,1024]{1,0:T(8,128)(2,1)}, u32[]{:S(2)}) copy-start(bf16[160,1024]{1,0:T(8,128)(2,1)} %copy-done.12) | copy-start | bytes 983044
  30.9 0.6 copy-start.18
  40.2 1.7 %copy-start.2 = (f32[800,1024]{1,0:T(8,128)}, f32[800,1024]{1,0:T(8,128)S(1)}, u32[]{:S(2)}) copy-start(f32[800,1024]{1,0:T(8,128)S(1)} %get-tuple-element.32.slope_ref) | copy-start | bytes 9830404
  41.9 1.0 %copy-start.7 = (bf16[4,336,128]{2,1,0:T(8,128)(2,1)S(1)}, bf16[4,336,128]{2,1,0:T(8,128)(2,1)}, u32[]{:S(2)}) copy-start(bf16[4,336,128]{2,1,0:T(8,128)(2,1)} %copy-done.6) | copy-start | bytes 1032196
  42.9 0.8 copy-start.15
  43.7 0.7 copy-start.20
  44.3 9.4 %copy-start.23 = (bf16[3,3,80,80]{3,2,1,0:T(8,128)(2,1)S(1)}, bf16[3,3,80,80]{3,2,1,0:T(8,128)(2,1)}, u32[]{:S(2)}) copy-start(bf16[3,3,80,80]{3,2,1,0:T(8,128)(2,1)} %param.11) | copy-start | bytes 345604
  48.3 1.5 %copy-start.4 = (f32[640,1024]{1,0:T(8,128)}, f32[640,1024]{1,0:T(8,128)S(1)}, u32[]{:S(2)}) copy-start(f32[640,1024]{1,0:T(8,128)S(1)} %get-tuple-element.29.guide_ref) | copy-start | bytes 7864324
  49.8 13.6 %copy-start.26 = (f32[80]{0:T(128)S(1)}, f32[80]{0:T(128)}, u32[]{:S(2)}) copy-start(f32[80]{0:T(128)} %param.12) | copy-start | bytes 964
  49.8 14.3 %copy-start.19 = (s32[2]{0:T(128)S(1)}, s32[2]{0:T(128)}, u32[]{:S(2)}) copy-start(s32[2]{0:T(128)} %copy-done.17) | copy-start | bytes 28
  49.8 14.3 %collective-permute-start.7 = (bf16[160,1024]{1,0:T(8,128)(2,1)}, bf16[160,1024]{1,0:T(8,128)(2,1)S(1)}, u32[]{:S(2)}, u32[]{:S(2)}) collective-permute-start(bf16[160,1024]{1,0:T(8,128)(2,1)} %get-tuple-element.30), channel_id=1, source_target_pairs={{0,1},{1,0},{2,3},{3,2},{4,5},{5,4},{6,7},{7,6},{8,9},{9,8},{10,11... | collective-permute-start | bytes 983048 | tf_op jit(solution)/shard_map/ppermute | solution.py:294
  50.2 13.9 %collective-permute-start.8 = (bf16[160,1024]{1,0:T(8,128)(2,1)}, bf16[160,1024]{1,0:T(8,128)(2,1)S(1)}, u32[]{:S(2)}, u32[]{:S(2)}) collective-permute-start(bf16[160,1024]{1,0:T(8,128)(2,1)} %get-tuple-element.31), channel_id=1, source_target_pairs={{1,2},{2,1},{3,4},{4,3},{5,6},{6,5},{7,8},{8,7},{9,10},{10,9},{11,... | collective-permute-start | bytes 983048 | tf_op jit(solution)/shard_map/ppermute | solution.py:294
  64.1 1.9 %copy-start.3 = (f32[800,1024]{1,0:T(8,128)S(1)}, f32[800,1024]{1,0:T(8,128)}, u32[]{:S(2)}) copy-start(f32[800,1024]{1,0:T(8,128)} %copy-done.2) | copy-start | bytes 9830404
  66.0 1.7 %copy-start.5 = (f32[640,1024]{1,0:T(8,128)S(1)}, f32[640,1024]{1,0:T(8,128)}, u32[]{:S(2)}) copy-start(f32[640,1024]{1,0:T(8,128)} %copy-done.4) | copy-start | bytes 7864324
  67.8 0.8 copy-start.16
where the time goes:
time: 79.1 us; the launch traced here: 78.3 us
  local copies, waits for them, and re-layouts  32.7 us (41%)
  Pallas kernels  25.1 us (32%)
  starting transfers between devices  15.8 us (20%)
  waiting for transfers between devices  4.53 us (6%)
    unnamed x54, local copies, waits for them, and re-layouts  21.1 us
    ppermute x6, starting transfers between devices, swap(): return lax.ppermute(x, 'lat', pairs(count, step, parity))  11.2 us
    pallas_call x1, Pallas kernels, local(): pl.pallas_call(functools.partial(backward_kernel, channels, height), out_...  9.76 us
    pallas_call x1, Pallas kernels, local(): pl.pallas_call(functools.partial(forward_kernel, channels, height), out_s...  8.74 us
    transpose x4, local copies, waits for them, and re-layouts, stacked(): weights = weights[::-1, ::-1].transpose(1, 3, 0, 2)  5.2 us
    ppermute x3, starting transfers between devices, local(): lax.ppermute(relayed[m - 1], 'lat', [(i, i ^ m) for i in range(count)])  4.57 us
    ppermute x6, waiting for transfers between devices, swap(): return lax.ppermute(x, 'lat', pairs(count, step, parity))  4.52 us
    pallas_call x1, Pallas kernels, local(): pl.pallas_call(functools.partial(tile_kernel, channels, height, columns,...  3.99 us
  transfers between devices with their start and end apart: 9, of which 2 were waited for; matrix products, arithmetic and copies ran while one was open for 15% of the time, Pallas kernels for 13%

commit v1 on v0

v1 whole, which is shorter than its diff:
```python
import functools

import jax
import jax.numpy as jnp
from jax import lax
from jax.experimental import pallas as pl
from jax.experimental.pallas import tpu as pltpu
from jax.sharding import PartitionSpec as P

BLK_LAT = 2
BLK_LON = 128
HALO = 2
F32 = jnp.float32
BF16 = jnp.bfloat16

VM = pl.BlockSpec(memory_space=pltpu.VMEM)
SM = pl.BlockSpec(memory_space=pltpu.SMEM)
HB = pl.BlockSpec(memory_space=pltpu.HBM)


def params(mib=16):
    return pltpu.CompilerParams(vmem_limit_bytes=mib << 20)


def shape(dims, dtype=BF16):
    return jax.ShapeDtypeStruct(dims, dtype)


def rows(index, count, channels):
    start = index * channels
    if not isinstance(start, int):
        start = pl.multiple_of(start, 16)
    return pl.ds(start, count * channels)


def permutation(height, group, back):
    n = height * group
    out = lax.broadcasted_iota(jnp.int32, (n, n), 0)
    src = lax.broadcasted_iota(jnp.int32, (n, n), 1)
    if back:
        want = (out % height) * group + out // height
    else:
        want = (out % group) * height + out // group
    return jnp.where(src == want, 1.0, 0.0).astype(BF16)


def channel_groups(channels):
    return [(start, min(32, channels - start)) for start in range(0, channels, 32)]


def as_column(row):
    n = row.shape[1]
    here = lax.broadcasted_iota(jnp.int32, (n, n), 0) == lax.broadcasted_iota(jnp.int32, (n, n), 1)
    return jnp.sum(jnp.where(here, jnp.broadcast_to(row, (n, n)), 0.0), axis=1, keepdims=True)


def place_in_plane(span):
    me = lax.axis_index("lat")
    return me % span, (me // span) % 2, me % 2


def pack_tile(k, dst, w_ref, obs_ref, count_ref, slots, channels):
    live = lax.broadcasted_iota(jnp.int32, (slots, BLK_LON), 0) < count_ref[0, k]
    zero = jnp.zeros((slots, BLK_LON), BF16)
    for i in range(BLK_LAT):
        half = w_ref[k, :, i * BLK_LON : (i + 1) * BLK_LON]
        dst[i * slots : (i + 1) * slots, :] = jnp.where(live, half, zero)
    dst[BLK_LAT * slots : BLK_LAT * slots + channels, :] = obs_ref[k]


def prepare_kernel(
    channels, height, span,
    count_ref, x_hbm, w_hbm, obs_hbm,
    xt_ref, ha_ref, hb_ref, za_ref, zb_ref, own_ref,
    x_ref, w_ref, obs_ref, sems,
):
    copies = []
    for index, (start, size) in enumerate(channel_groups(channels)):
        part = pl.ds(start * height, size * height)
        copies.append(pltpu.make_async_copy(x_hbm.at[part], x_ref.at[part], sems.at[index]))
    copies.append(pltpu.make_async_copy(w_hbm.at[0], w_ref, sems.at[len(copies)]))
    copies.append(pltpu.make_async_copy(obs_hbm.at[0], obs_ref, sems.at[len(copies)]))
    for copy in copies:
        copy.start()
    p, z_odd, odd = place_in_plane(span)
    for index, (start, size) in enumerate(channel_groups(channels)):
        copies[index].wait()
        n = size * height
        moved = jnp.dot(
            permutation(height, size, False),
            x_ref[start * height : start * height + n, :],
            preferred_element_type=F32,
        ).astype(BF16)
        for r in range(height):
            xt_ref[r * channels + start : r * channels + start + size, :] = (
                moved[r * size : (r + 1) * size, :]
            )
    last = height - HALO
    ha_ref[...] = xt_ref[rows(last * (1 - odd), HALO, channels), :]
    hb_ref[...] = xt_ref[rows(last * odd, HALO, channels), :]
    copies[-2].wait()
    copies[-1].wait()
    slots = w_ref.shape[1]
    pack = functools.partial(
        pack_tile, w_ref=w_ref, obs_ref=obs_ref, count_ref=count_ref, slots=slots, channels=channels
    )
    for j in range(span):
        up = jnp.maximum(p - j, 0)
        down = jnp.minimum(2 * span + p - j, 2 * span)
        pack(jnp.where(z_odd == 1, down, up), za_ref.at[j])
        pack(jnp.where(z_odd == 1, up, down), zb_ref.at[j])
        if j == 0:
            pack(span, own_ref.at[0])
        else:
            pack(span + p - lax.bitwise_xor(p, j), own_ref.at[j])


def relay_kernel(span, za_ref, zb_ref, own_ref, *outs):
    p, z_odd, _ = place_in_plane(span)
    for m in range(1, span):
        to = lax.bitwise_xor(p, m)
        below = jnp.where(to < p, 1, 0)
        outs[m - 1][0] = own_ref[m]

        @pl.when(below == z_odd)
        def _():
            outs[m - 1][1] = za_ref[to]

        @pl.when(below != z_odd)
        def _():
            outs[m - 1][1] = zb_ref[to]


def stack_forward(raw_ref, dst):
    taps, _, outs, ins = raw_ref.shape
    total = jnp.zeros(dst.shape, F32)
    for a in range(taps):
        block = raw_ref[a].reshape(taps * outs, ins)
        to = lax.broadcasted_iota(jnp.int32, (ins, taps * ins), 1)
        pick = jnp.where(to == lax.broadcasted_iota(jnp.int32, to.shape, 0) + a * ins, 1.0, 0.0)
        total += jnp.dot(block, pick.astype(BF16), preferred_element_type=F32)
    dst[...] = total.astype(BF16)


def stack_backward(raw_ref, dst):
    taps, _, outs, ins = raw_ref.shape
    n = taps * outs
    here = lax.broadcasted_iota(jnp.int32, (n, n), 0) == lax.broadcasted_iota(jnp.int32, (n, n), 1)
    same = jnp.where(here, 1.0, 0.0).astype(BF16)
    for b in range(taps):
        block = jnp.concatenate([raw_ref[taps - 1 - a, taps - 1 - b] for a in range(taps)], axis=0)
        dst[b * ins : (b + 1) * ins, :] = lax.dot_general(
            block, same, (((0,), (0,)), ((), ())), preferred_element_type=F32
        ).astype(BF16)


def conv_row(w_ref, src_ref, index, channels):
    window = src_ref[rows(index, 3, channels), :]
    taps = jnp.dot(w_ref[...], window, preferred_element_type=F32)
    width = taps.shape[1]
    return (
        pltpu.roll(taps[0:channels], 1, 1)
        + taps[channels : 2 * channels]
        + pltpu.roll(taps[2 * channels : 3 * channels], width - 1, 1)
    )


def silu_and_slope(act, keep=None):
    gate = 0.5 * jnp.tanh(0.5 * act) + 0.5
    if keep is not None:
        gate = gate * keep
    hidden = act * gate
    return hidden.astype(BF16), gate * (1.0 + act - hidden)


def ext_edges(channels, height, mid_ref, a_ref, b_ref, top, bottom, odd):
    edge = HALO * channels
    top[edge : 2 * edge, :] = mid_ref[0:edge, :]
    bottom[0:edge, :] = mid_ref[(height - HALO) * channels : height * channels, :]

    @pl.when(odd == 1)
    def _():
        top[0:edge, :] = a_ref[...]
        bottom[edge : 2 * edge, :] = b_ref[...]

    @pl.when(odd == 0)
    def _():
        top[0:edge, :] = b_ref[...]
        bottom[edge : 2 * edge, :] = a_ref[...]


def forward_inner_kernel(
    channels, height,
    xt_ref, raw1_ref, raw2_ref,
    hid_ref, slope_ref, res_ref, w1_ref, w2_ref, w1t_ref, w2t_ref,
):
    stack_forward(raw1_ref, w1_ref)
    stack_forward(raw2_ref, w2_ref)
    for i in range(height - 2):
        act = conv_row(w1_ref, xt_ref, i, channels)
        hid_ref[rows(i, 1, channels), :], slope_ref[rows(i, 1, channels), :] = silu_and_slope(act)
    for i in range(height - 4):
        res_ref[rows(i, 1, channels), :] = conv_row(w2_ref, hid_ref, i, channels)
    stack_backward(raw1_ref, w1t_ref)
    stack_backward(raw2_ref, w2t_ref)


def on_grid():
    me = lax.axis_index("lat")
    count = lax.axis_size("lat")
    return jnp.where(me == 0, 0.0, 1.0), jnp.where(me == count - 1, 0.0, 1.0)


def forward_edge_kernel(
    channels, height,
    xt_ref, a_ref, b_ref, hid_ref, w1_ref, w2_ref,
    slope_ref, res_ref,
    top, bottom, hid_top, hid_bottom,
):
    odd = lax.axis_index("lat") % 2
    ext_edges(channels, height, xt_ref, a_ref, b_ref, top, bottom, odd)
    has_above, has_below = on_grid()
    inner = (height - 2 - HALO) * channels
    hid_top[2 * channels : 4 * channels, :] = hid_ref[0 : 2 * channels, :]
    hid_bottom[0 : 2 * channels, :] = hid_ref[inner : inner + 2 * channels, :]
    for i, keep in ((0, has_above), (1, None)):
        act = conv_row(w1_ref, top, i, channels)
        hid_top[rows(i, 1, channels), :], slope_ref[rows(i, 1, channels), :] = silu_and_slope(act, keep)
    for i, keep in ((0, None), (1, has_below)):
        act = conv_row(w1_ref, bottom, i, channels)
        hid_bottom[rows(2 + i, 1, channels), :], slope_ref[rows(2 + i, 1, channels), :] = (
            silu_and_slope(act, keep)
        )
    for i in range(2):
        res_ref[rows(i, 1, channels), :] = conv_row(w2_ref, hid_top, i, channels)
        res_ref[rows(2 + i, 1, channels), :] = conv_row(w2_ref, hid_bottom, i, channels)


def tile_kernel(
    channels, height, columns, span,
    route_ref, xt_ref, inner_ref, edge_ref, ow_ref, own_ref, za_ref, zb_ref, *refs,
):
    near_refs, (guide_ref, low_ref, ga_ref, gb_ref) = refs[: span - 1], refs[span - 1 :]
    slots = BLK_LON
    across = columns // BLK_LON
    p, z_odd, odd = place_in_plane(span)
    guide_ref[...] = jnp.zeros_like(guide_ref)
    jobs = [
        (span, own_ref.at[0]),
        (jnp.where(z_odd == 1, 0, 2 * span), za_ref.at[p]),
        (jnp.where(z_odd == 1, 2 * span, 0), zb_ref.at[p]),
    ]
    for m in range(1, span):
        step = lax.bitwise_xor(p, m) - p
        jobs.append((span + step, near_refs[m - 1].at[0]))
        jobs.append((jnp.where(step > 0, step, 2 * span + step), near_refs[m - 1].at[1]))
    obs_weight = as_column(ow_ref[...])
    down = height // BLK_LAT
    places, blocks = [], []
    for k, ref in jobs:
        n = route_ref[0, k]
        r, q = n // across, n % across
        inside = (r > 0) & (r < down - 1)
        place, block = [], []
        for i in range(BLK_LAT):
            lanes = pl.ds(pl.multiple_of(q * BLK_LON, BLK_LON), BLK_LON)
            here = (rows(r * BLK_LAT + i, 1, channels), lanes)
            row_in = jnp.clip(r * BLK_LAT + i - HALO, 0, height - 2 * HALO - 1)
            row_edge = jnp.where(r == 0, i, HALO + i)
            res = jnp.where(
                inside,
                inner_ref[rows(row_in, 1, channels), lanes],
                edge_ref[rows(row_edge, 1, channels), lanes],
            )
            place.append(here)
            block.append((xt_ref[here].astype(F32) + res).astype(BF16))
        places.append(place)
        blocks.append(block)
    misfits = []
    for (k, ref), block in zip(jobs, blocks):
        predicted = jnp.zeros((channels, slots), F32)
        for i in range(BLK_LAT):
            predicted += lax.dot_general(
                block[i],
                ref[i * slots : (i + 1) * slots, :],
                (((1,), (1,)), ((), ())),
                preferred_element_type=F32,
            )
        obs = ref[BLK_LAT * slots : BLK_LAT * slots + channels, :].astype(F32)
        misfits.append(((obs - predicted) * obs_weight).astype(BF16))
    terms = [
        [
            jnp.dot(misfit, ref[i * slots : (i + 1) * slots, :], preferred_element_type=F32)
            .astype(BF16)
            .astype(F32)
            for i in range(BLK_LAT)
        ]
        for (k, ref), misfit in zip(jobs, misfits)
    ]
    for place, term in zip(places, terms):
        for i in range(BLK_LAT):
            guide_ref[place[i]] += term[i]
    last = height - HALO
    low_ref[...] = guide_ref[...].astype(BF16)
    ga_ref[...] = low_ref[rows(last * (1 - odd), HALO, channels), :]
    gb_ref[...] = low_ref[rows(last * odd, HALO, channels), :]


def backward_inner_kernel(
    channels, height,
    guide_ref, low_ref, slope_ref, res_ref, prior_ref, w2_ref, w1_ref,
    adj_ref, score_ref,
):
    for i in range(height - 2):
        here = rows(i, 1, channels)
        adj_ref[here, :] = (slope_ref[here, :] * conv_row(w2_ref, low_ref, i, channels)).astype(BF16)
    prior = as_column(prior_ref[...])
    for i in range(height - 4):
        here = rows(i, 1, channels)
        back = conv_row(w1_ref, adj_ref, i, channels)
        guide = guide_ref[rows(i + HALO, 1, channels), :]
        score_ref[here, :] = (prior * res_ref[here, :] + guide + back).astype(BF16)


def backward_edge_kernel(
    channels, height,
    guide_ref, low_ref, a_ref, b_ref, slope_ref, res_ref, prior_ref, adj_ref, score_ref, w2_ref, w1_ref,
    out_ref,
    top, bottom, adj_top, adj_bottom, edge_ref,
):
    odd = lax.axis_index("lat") % 2
    ext_edges(channels, height, low_ref, a_ref, b_ref, top, bottom, odd)
    inner = (height - 2 - HALO) * channels
    adj_top[2 * channels : 4 * channels, :] = adj_ref[0 : 2 * channels, :]
    adj_bottom[0 : 2 * channels, :] = adj_ref[inner : inner + 2 * channels, :]
    for i in range(2):
        adj_top[rows(i, 1, channels), :] = (
            slope_ref[rows(i, 1, channels), :] * conv_row(w2_ref, top, i, channels)
        ).astype(BF16)
        adj_bottom[rows(2 + i, 1, channels), :] = (
            slope_ref[rows(2 + i, 1, channels), :] * conv_row(w2_ref, bottom, i, channels)
        ).astype(BF16)
    prior = as_column(prior_ref[...])
    for i in range(2):
        for src, at, row in ((adj_top, i, i), (adj_bottom, HALO + i, height - HALO + i)):
            here = rows(at, 1, channels)
            back = conv_row(w1_ref, src, i, channels)
            edge_ref[here, :] = (
                prior * res_ref[here, :] + guide_ref[rows(row, 1, channels), :] + back
            ).astype(BF16)
    for start, size in channel_groups(channels):
        n = size * height
        picked = []
        for r in range(height):
            if r < HALO:
                src, at = edge_ref, r
            elif r < height - HALO:
                src, at = score_ref, r - HALO
            else:
                src, at = edge_ref, r - height + 2 * HALO
            picked.append(src[at * channels + start : at * channels + start + size, :])
        out_ref[start * height : start * height + n, :] = jnp.dot(
            permutation(height, size, True), jnp.concatenate(picked, axis=0), preferred_element_type=F32
        ).astype(BF16)


def pairs(count, step, parity):
    found = []
    for i in range(count):
        other = i + step if (i // step) % 2 == parity else i - step
        if 0 <= other < count:
            found.append((i, other))
    return found


def local(
    noisy_state, w_first, w_second, prior_weight, obs_weight, block_route, counts, tile_weights, observations
):
    channels, height, columns = noisy_state.shape
    tile_total = block_route.shape[1]
    span = tile_total // 2
    slots = tile_weights.shape[2]
    count = lax.axis_size("lat")
    pack_rows = BLK_LAT * slots + channels
    taps = w_first.shape[0]

    def field(n, dtype=BF16):
        return shape((n * channels, columns), dtype)

    def buffer(n, dtype=BF16):
        return pltpu.VMEM((n * channels, columns), dtype)

    def swap(x, step, parity):
        return lax.ppermute(x, "lat", pairs(count, step, parity))

    packed = shape((span, pack_rows, BLK_LON))
    xt, ha, hb, za, zb, own = pl.pallas_call(
        functools.partial(prepare_kernel, channels, height, span),
        out_shape=(field(height), field(HALO), field(HALO), packed, packed, packed),
        in_specs=[SM, HB, HB, HB],
        out_specs=[VM] * 6,
        scratch_shapes=[
            pltpu.VMEM((channels * height, columns), BF16),
            pltpu.VMEM(tile_weights.shape[1:], BF16),
            pltpu.VMEM(observations.shape[1:], BF16),
            pltpu.SemaphoreType.DMA((len(channel_groups(channels)) + 2,)),
        ],
        compiler_params=params(),
    )(counts, noisy_state.reshape(channels * height, columns), tile_weights, observations)
    ha, hb = swap(ha, 1, 0), swap(hb, 1, 1)
    za, zb = swap(za, span, 0), swap(zb, span, 1)

    weight = shape((taps * channels, taps * channels))
    hid, slope_in, res_in, w1, w2, w1t, w2t = pl.pallas_call(
        functools.partial(forward_inner_kernel, channels, height),
        out_shape=(field(height - 2), field(height - 2, F32), field(height - 4, F32)) + (weight,) * 4,
        in_specs=[VM] * 3,
        out_specs=[VM] * 7,
        compiler_params=params(),
    )(xt, w_first, w_second)

    relayed = pl.pallas_call(
        functools.partial(relay_kernel, span),
        out_shape=tuple(shape((2, pack_rows, BLK_LON)) for _ in range(span - 1)),
        in_specs=[VM] * 3,
        out_specs=[VM] * (span - 1),
        compiler_params=params(),
    )(za, zb, own)
    arrived = [
        lax.ppermute(relayed[m - 1], "lat", [(i, i ^ m) for i in range(count)]) for m in range(1, span)
    ]

    slope_ed, res_ed = pl.pallas_call(
        functools.partial(forward_edge_kernel, channels, height),
        out_shape=(field(2 * HALO, F32), field(2 * HALO, F32)),
        in_specs=[VM] * 6,
        out_specs=[VM] * 2,
        scratch_shapes=[buffer(2 * HALO)] * 4,
        compiler_params=params(),
    )(xt, ha, hb, hid, w1, w2)

    guide, low, ga, gb = pl.pallas_call(
        functools.partial(tile_kernel, channels, height, columns, span),
        out_shape=(field(height, F32), field(height), field(HALO), field(HALO)),
        in_specs=[SM] + [VM] * (7 + span - 1),
        out_specs=[VM] * 4,
        compiler_params=params(),
    )(block_route, xt, res_in, res_ed, obs_weight[None, :], own, za, zb, *arrived)
    ga, gb = swap(ga, 1, 0), swap(gb, 1, 1)

    prior = prior_weight[None, :]
    adj, score = pl.pallas_call(
        functools.partial(backward_inner_kernel, channels, height),
        out_shape=(field(height - 2), field(height - 4)),
        in_specs=[VM] * 7,
        out_specs=[VM] * 2,
        compiler_params=params(),
    )(guide, low, slope_in, res_in, prior, w2t, w1t)

    out = pl.pallas_call(
        functools.partial(backward_edge_kernel, channels, height),
        out_shape=shape((channels * height, columns)),
        in_specs=[VM] * 11,
        out_specs=VM,
        scratch_shapes=[buffer(2 * HALO)] * 5,
        compiler_params=params(),
    )(guide, low, ga, gb, slope_ed, res_ed, prior, adj, score, w2t, w1t)
    return out.reshape(channels, height, columns)


def solution(mesh):
    in_specs = (
        P("grp", "lat", None),
        P(),
        P(),
        P(),
        P(),
        P(("grp", "lat"), None),
        P(("grp", "lat"), None),
        P(("grp", "lat"), None, None, None),
        P(("grp", "lat"), None, None, None),
    )
    out_specs = P("grp", "lat", None)
    return jax.shard_map(local, mesh=mesh, in_specs=in_specs, out_specs=out_specs, check_vma=False)
```

time: 79.1 us -> 48.4 us (0.61)
  local copies, waits for them, and re-layouts: 32.7 us -> 3.98 us
  Pallas kernels: 25.1 us -> 13.7 us
  waiting for transfers between devices: 4.53 us -> 14.5 us
    unnamed x54 -> x18, local copies, waits for them, and re-layouts: 21.1 us -> 3.98 us
    pallas_call x2 -> x4, Pallas kernels: 18.5 us -> 9.87 us  [the longest x1 3.13 us: local(): pl.pallas_call(functools.partial(backward_edge_kernel, channels, height),...]
    ppermute x6, waiting for transfers between devices: 4.52 us -> 10.7 us  [swap(): return lax.ppermute(x, 'lat', pairs(count, step, parity))]
    transpose x6 -> x0, local copies, waits for them, and re-layouts: 5.39 us -> none  [the longest x4 5.2 us: stacked(): weights = weights[::-1, ::-1].transpose(1, 3, 0, 2)]
    ppermute x3, waiting for transfers between devices: 0.01 us -> 3.77 us  [local(): lax.ppermute(relayed[m - 1], 'lat', [(i, i ^ m) for i in range(count)])]
    reshape x4 -> x0, local copies, waits for them, and re-layouts: 2.89 us -> none  [stacked(): matrix = weights.reshape(taps * outs, row_taps * ins)]
    pallas_call x1, Pallas kernels: 3.99 us -> 1.63 us  [local(): pl.pallas_call(functools.partial(tile_kernel, channels, height, columns,...]
    pad x4 -> x0, local copies, waits for them, and re-layouts: 1.88 us -> none  [stacked(): return jnp.pad(matrix, ((0, 0), (0, -depth % 256)))]
  transfers between devices with their start and end apart: 9 -> 9, of which waited for: 2 -> 5; matrix products, arithmetic and copies ran while one was open for 15% -> 0% of each run, Pallas kernels for 13% -> 14%
where the time goes in v1:
time: 48.4 us; the launch traced here: 48.1 us
  starting transfers between devices  15.8 us (33%)
  waiting for transfers between devices  14.5 us (30%)
  Pallas kernels  13.7 us (28%)
  local copies, waits for them, and re-layouts  3.98 us (8%)
    ppermute x6, starting transfers between devices, swap(): return lax.ppermute(x, 'lat', pairs(count, step, parity))  11.1 us
    ppermute x6, waiting for transfers between devices, swap(): return lax.ppermute(x, 'lat', pairs(count, step, parity))  10.7 us
    ppermute x3, starting transfers between devices, local(): lax.ppermute(relayed[m - 1], 'lat', [(i, i ^ m) for i in range(count)])  4.7 us
    unnamed x18, local copies, waits for them, and re-layouts  3.98 us
    ppermute x3, waiting for transfers between devices, local(): lax.ppermute(relayed[m - 1], 'lat', [(i, i ^ m) for i in range(count)])  3.77 us
    pallas_call x1, Pallas kernels, local(): pl.pallas_call(functools.partial(backward_edge_kernel, channels, height),...  3.13 us
    pallas_call x1, Pallas kernels, local(): pl.pallas_call(functools.partial(forward_inner_kernel, channels, height),...  2.51 us
    pallas_call x1, Pallas kernels, local(): pl.pallas_call(functools.partial(backward_inner_kernel, channels, height)...  2.29 us
  transfers between devices with their start and end apart: 9, of which 5 were waited for; matrix products, arithmetic and copies ran while one was open for 0% of the time, Pallas kernels for 14%

profile of v1, /device:TPU:17, one launch (start us, length us, event | category | flops | bytes accessed | tf_op | source)
XLA Modules:
  0.0 48.1 jit_solution(4933519668199724013)
XLA Ops:
  0.0 0.0 copy-start
  0.0 1.3 %copy-done = bf16[80,8,1024]{2,1,0:T(8,128)(2,1)S(1)} copy-done((bf16[80,8,1024]{2,1,0:T(8,128)(2,1)S(1)}, bf16[80,8,1024]{2,1,0:T(8,128)(2,1)}, u32[]{:S(2)}) %copy-start) | copy-done | bytes 1310744
  1.3 0.0 copy-start.1
  1.3 1.1 %copy-done.1 = bf16[1,9,128,256]{3,2,1,0:T(8,128)(2,1)S(1)} copy-done((bf16[1,9,128,256]{3,2,1,0:T(8,128)(2,1)S(1)}, bf16[1,9,128,256]{3,2,1,0:T(8,128)(2,1)}, u32[]{:S(2)}) %copy-start.1) | copy-done | bytes 589848
  2.4 0.0 copy-start.4
  2.4 0.9 %copy-done.4 = bf16[1,9,80,128]{3,2,1,0:T(8,128)(2,1)S(1)} copy-done((bf16[1,9,80,128]{3,2,1,0:T(8,128)(2,1)S(1)}, bf16[1,9,80,128]{3,2,1,0:T(8,128)(2,1)}, u32[]{:S(2)}) %copy-start.4) | copy-done | bytes 184344
  3.3 0.0 copy-start.6
  3.3 0.7 %copy-done.6 = s32[1,9]{1,0:T(1,128)S(1)} copy-done((s32[1,9]{1,0:T(1,128)S(1)}, s32[1,9]{1,0:T(1,128)}, u32[]{:S(2)}) %copy-start.6) | copy-done | bytes 60
  4.0 0.0 copy-start.2
  4.0 0.0 copy-start.3
  4.0 2.1 %shard_map.91 = (bf16[640,1024]{1,0:T(8,128)(2,1)S(1)}, bf16[160,1024]{1,0:T(8,128)(2,1)S(1)}, bf16[160,1024]{1,0:T(8,128)(2,1)S(1)}, bf16[4,336,128]{2,1,0:T(8,...) custom-call(s32[1,9]{1,0:T(1,128)S(1)} %copy-done.6, bf16[640,1024]{1,0:T(8,128)(2,1)S(1)} %bitcast.4, ...), custom_call_target="tpu_custom_call" | custom-call | tf_op jit(solution)/shard_map/pallas_call | solution.py:397
  6.1 1.4 %collective-permute-start.2 = (bf16[4,336,128]{2,1,0:T(8,128)(2,1)S(1)}, bf16[4,336,128]{2,1,0:T(8,128)(2,1)S(1)}, u32[]{:S(2)}, u32[]{:S(2)}) collective-permute-start(bf16[4,336,128]{2,1,0:T(8,128)(2,1)S(1)} %get-tuple-element.38), channel_id=1, source_target_pairs={{0,4},{1,5},{2,6},{3,7},{4,0},{5,1},{6,2},{7,3},{8,12},{9,13},{10,... | collective-permute-start | bytes 1032200 | tf_op jit(solution)/shard_map/ppermute | solution.py:394
  7.4 1.9 %collective-permute-start.3 = (bf16[4,336,128]{2,1,0:T(8,128)(2,1)S(1)}, bf16[4,336,128]{2,1,0:T(8,128)(2,1)S(1)}, u32[]{:S(2)}, u32[]{:S(2)}) collective-permute-start(bf16[4,336,128]{2,1,0:T(8,128)(2,1)S(1)} %get-tuple-element.39), channel_id=1, source_target_pairs={{4,8},{5,9},{6,10},{7,11},{8,4},{9,5},{10,6},{11,7},{20,24},{21,25... | collective-permute-start | bytes 1032200 | tf_op jit(solution)/shard_map/ppermute | solution.py:394
  9.3 1.0 %collective-permute-start = (bf16[160,1024]{1,0:T(8,128)(2,1)S(1)}, bf16[160,1024]{1,0:T(8,128)(2,1)S(1)}, u32[]{:S(2)}, u32[]{:S(2)}) collective-permute-start(bf16[160,1024]{1,0:T(8,128)(2,1)S(1)} %get-tuple-element.31), channel_id=1, source_target_pairs={{0,1},{1,0},{2,3},{3,2},{4,5},{5,4},{6,7},{7,6},{8,9},{9,8},{10,11... | collective-permute-start | bytes 983048 | tf_op jit(solution)/shard_map/ppermute | solution.py:394
  10.4 3.0 %collective-permute-start.1 = (bf16[160,1024]{1,0:T(8,128)(2,1)S(1)}, bf16[160,1024]{1,0:T(8,128)(2,1)S(1)}, u32[]{:S(2)}, u32[]{:S(2)}) collective-permute-start(bf16[160,1024]{1,0:T(8,128)(2,1)S(1)} %get-tuple-element.32), channel_id=1, source_target_pairs={{1,2},{2,1},{3,4},{4,3},{5,6},{6,5},{7,8},{8,7},{9,10},{10,9},{11,... | collective-permute-start | bytes 983048 | tf_op jit(solution)/shard_map/ppermute | solution.py:394
  13.4 1.6 %collective-permute-done.2.za_ref = bf16[4,336,128]{2,1,0:T(8,128)(2,1)S(1)} collective-permute-done((bf16[4,336,128]{2,1,0:T(8,128)(2,1)S(1)}, bf16[4,336,128]{2,1,0:T(8,128)(2,1)S(1)}, u32[]{:S(2)}, u32[]{:S(2)}) %collective-permute-start.2) | collective-permute-done | bytes 344096 | tf_op jit(solution)/shard_map/ppermute | solution.py:394
  15.1 2.9 %collective-permute-done.3.zb_ref = bf16[4,336,128]{2,1,0:T(8,128)(2,1)S(1)} collective-permute-done((bf16[4,336,128]{2,1,0:T(8,128)(2,1)S(1)}, bf16[4,336,128]{2,1,0:T(8,128)(2,1)S(1)}, u32[]{:S(2)}, u32[]{:S(2)}) %collective-permute-start.3) | collective-permute-done | bytes 344096 | tf_op jit(solution)/shard_map/ppermute | solution.py:394
  18.0 1.9 %collective-permute-start.4 = (bf16[2,336,128]{2,1,0:T(8,128)(2,1)S(1)}, bf16[2,336,128]{2,1,0:T(8,128)(2,1)S(1)}, u32[]{:S(2)}, u32[]{:S(2)}) collective-permute-start(bf16[2,336,128]{2,1,0:T(8,128)(2,1)S(1)} %get-tuple-element.40), channel_id=1, source_target_pairs={{0,1},{1,0},{2,3},{3,2},{4,5},{5,4},{6,7},{7,6},{8,9},{9,8},{10,11... | collective-permute-start | bytes 516104 | tf_op jit(solution)/shard_map/ppermute | solution.py:430
  19.9 2.7 %collective-permute-start.5 = (bf16[2,336,128]{2,1,0:T(8,128)(2,1)S(1)}, bf16[2,336,128]{2,1,0:T(8,128)(2,1)S(1)}, u32[]{:S(2)}, u32[]{:S(2)}) collective-permute-start(bf16[2,336,128]{2,1,0:T(8,128)(2,1)S(1)} %get-tuple-element.41), channel_id=1, source_target_pairs={{0,2},{1,3},{2,0},{3,1},{4,6},{5,7},{6,4},{7,5},{8,10},{9,11},{10,... | collective-permute-start | bytes 516104 | tf_op jit(solution)/shard_map/ppermute | solution.py:430
  22.6 0.0 collective-permute-start.6
  22.7 0.0 copy-done.2
  22.7 0.0 copy-done.3
  22.7 2.5 %shard_map.92 = (bf16[480,1024]{1,0:T(8,128)(2,1)S(1)}, f32[480,1024]{1,0:T(8,128)S(1)}, f32[320,1024]{1,0:T(8,128)S(1)}, bf16[240,240]{1,0:T(8,128)(2,1)S(1)}, ...) custom-call(bf16[640,1024]{1,0:T(8,128)(2,1)S(1)} %get-tuple-element.29.xt_ref, ...), custom_call_target="tpu_custom_call" | custom-call | tf_op jit(solution)/shard_map/pallas_call | solution.py:414
  25.2 0.0 collective-permute-done.a_ref
  25.2 0.0 collective-permute-done.1.b_ref
  25.2 0.0 copy-start.7
  25.2 0.0 copy-start.8
  25.2 1.9 %shard_map.93 = (f32[320,1024]{1,0:T(8,128)S(1)}, f32[320,1024]{1,0:T(8,128)S(1)}) custom-call(bf16[640,1024]{1,0:T(8,128)(2,1)S(1)} %get-tuple-element.29.xt_ref, bf16[160,1024]{1,0:T(8,128)(2,1)S(1)} %collective-permute-done.a_ref, bf16[160,1024]{1,0:T(8,128)(2,1)S(1)} %collective-permute-done.1.b_ref, bf16[480,1024]{1,0:T(8,128)(2,1)S(1)} %get-tuple-element.33.hid_ref, ...), custom_call_target="tpu_custom_call" | custom-call | tf_op jit(solution)/shard_map/pallas_call | solution.py:433
  27.2 0.0 collective-permute-done.4.refs_0_
  27.2 0.1 collective-permute-done.5.refs_1_
  27.3 3.7 %collective-permute-done.6.refs_2_ = bf16[2,336,128]{2,1,0:T(8,128)(2,1)S(1)} collective-permute-done((bf16[2,336,128]{2,1,0:T(8,128)(2,1)S(1)}, bf16[2,336,128]{2,1,0:T(8,128)(2,1)S(1)}, u32[]{:S(2)}, u32[]{:S(2)}) %collective-permute-start.6) | collective-permute-done | bytes 172064 | tf_op jit(solution)/shard_map/ppermute | solution.py:430
  31.0 0.0 copy-done.7
  31.0 0.0 copy-done.8
  31.0 0.0 copy-start.5
  31.0 1.6 %shard_map.95 = (f32[640,1024]{1,0:T(8,128)S(1)}, bf16[640,1024]{1,0:T(8,128)(2,1)S(1)}, bf16[160,1024]{1,0:T(8,128)(2,1)S(1)}, bf16[160,1024]{1,0:T(8,128)(2,1)S(1)}) custom-call(s32[1,9]{1,0:T(1,128)S(1)} %copy-done.7, bf16[640,1024]{1,0:T(8,128)(2,1)S(1)} %get-tuple-element.29.xt_ref, f32[320,1024]{1,0:T(8,128)S(1)} %get-tuple-element.30.inner_ref.res_ref, ...), custom_call_target="tpu_custom_call" | custom-call | tf_op jit(solution)/shard_map/pallas_call | solution.py:442
  32.6 0.5 collective-permute-start.7
  33.1 3.3 %collective-permute-start.8 = (bf16[160,1024]{1,0:T(8,128)(2,1)S(1)}, bf16[160,1024]{1,0:T(8,128)(2,1)S(1)}, u32[]{:S(2)}, u32[]{:S(2)}) collective-permute-start(bf16[160,1024]{1,0:T(8,128)(2,1)S(1)} %get-tuple-element.46), channel_id=1, source_target_pairs={{1,2},{2,1},{3,4},{4,3},{5,6},{6,5},{7,8},{8,7},{9,10},{10,9},{11,... | collective-permute-start | bytes 983048 | tf_op jit(solution)/shard_map/ppermute | solution.py:394
  36.4 0.0 copy-done.5
  36.5 2.3 %shard_map.96 = (bf16[480,1024]{1,0:T(8,128)(2,1)S(1)}, bf16[320,1024]{1,0:T(8,128)(2,1)S(1)}) custom-call(f32[640,1024]{1,0:T(8,128)S(1)} %get-tuple-element.43.guide_ref, bf16[640,1024]{1,0:T(8,128)(2,1)S(1)} %get-tuple-element.44.low_ref, f32[480,1024]{1,0:T(8,128)S(1)} %get-tuple-element.48.slope_ref, ...), custom_call_target="tpu_custom_call" | custom-call | tf_op jit(solution)/shard_map/pallas_call | solution.py:452
  38.7 0.0 collective-permute-done.7.a_ref
  38.8 6.2 %collective-permute-done.8.b_ref = bf16[160,1024]{1,0:T(8,128)(2,1)S(1)} collective-permute-done((bf16[160,1024]{1,0:T(8,128)(2,1)S(1)}, bf16[160,1024]{1,0:T(8,128)(2,1)S(1)}, u32[]{:S(2)}, u32[]{:S(2)}) %collective-permute-start.8) | collective-permute-done | bytes 327712 | tf_op jit(solution)/shard_map/ppermute | solution.py:394
  45.0 3.1 %shard_map.97 = bf16[640,1024]{1,0:T(8,128)(2,1)} custom-call(f32[640,1024]{1,0:T(8,128)S(1)} %get-tuple-element.43.guide_ref, bf16[640,1024]{1,0:T(8,128)(2,1)S(1)} %get-tuple-element.44.low_ref, bf16[160,1024]{1,0:T(8,128)(2,1)S(1)} %collective-permute-done.7.a_ref, bf16[160,1024]{1,0:T(8,128)(2,1)S(1)} %collective-permute-done.8.b_ref, ...), custom_call_target="tpu_custom_call" | custom-call | tf_op jit(solution)/shard_map/pallas_call | solution.py:460
  (1 shorter events, 0.0 us)
Async XLA Ops:
  0.0 1.3 %copy-start = (bf16[80,8,1024]{2,1,0:T(8,128)(2,1)S(1)}, bf16[80,8,1024]{2,1,0:T(8,128)(2,1)}, u32[]{:S(2)}) copy-start(bf16[80,8,1024]{2,1,0:T(8,128)(2,1)} %param.9) | copy-start | bytes 3932164
  1.3 1.1 %copy-start.1 = (bf16[1,9,128,256]{3,2,1,0:T(8,128)(2,1)S(1)}, bf16[1,9,128,256]{3,2,1,0:T(8,128)(2,1)}, u32[]{:S(2)}) copy-start(bf16[1,9,128,256]{3,2,1,0:T(8,128)(2,1)} %w_hbm.1) | copy-start | bytes 1769476
  2.4 0.9 %copy-start.4 = (bf16[1,9,80,128]{3,2,1,0:T(8,128)(2,1)S(1)}, bf16[1,9,80,128]{3,2,1,0:T(8,128)(2,1)}, u32[]{:S(2)}) copy-start(bf16[1,9,80,128]{3,2,1,0:T(8,128)(2,1)} %obs_hbm.1) | copy-start | bytes 552964
  3.3 0.7 %copy-start.6 = (s32[1,9]{1,0:T(1,128)S(1)}, s32[1,9]{1,0:T(1,128)}, u32[]{:S(2)}) copy-start(s32[1,9]{1,0:T(1,128)} %count_ref.1) | copy-start | bytes 112
  4.0 18.7 %copy-start.2 = (bf16[3,3,80,80]{3,2,1,0:T(8,128)(2,1)S(1)}, bf16[3,3,80,80]{3,2,1,0:T(8,128)(2,1)}, u32[]{:S(2)}) copy-start(bf16[3,3,80,80]{3,2,1,0:T(8,128)(2,1)} %raw1_ref.1) | copy-start | bytes 345604
  4.0 18.7 %copy-start.3 = (bf16[3,3,80,80]{3,2,1,0:T(8,128)(2,1)S(1)}, bf16[3,3,80,80]{3,2,1,0:T(8,128)(2,1)}, u32[]{:S(2)}) copy-start(bf16[3,3,80,80]{3,2,1,0:T(8,128)(2,1)} %raw2_ref.1) | copy-start | bytes 345604
  6.1 9.0 %collective-permute-start.2 = (bf16[4,336,128]{2,1,0:T(8,128)(2,1)S(1)}, bf16[4,336,128]{2,1,0:T(8,128)(2,1)S(1)}, u32[]{:S(2)}, u32[]{:S(2)}) collective-permute-start(bf16[4,336,128]{2,1,0:T(8,128)(2,1)S(1)} %get-tuple-element.38), channel_id=1, source_target_pairs={{0,4},{1,5},{2,6},{3,7},{4,0},{5,1},{6,2},{7,3},{8,12},{9,13},{10,... | collective-permute-start | bytes 1032200 | tf_op jit(solution)/shard_map/ppermute | solution.py:394
  7.4 10.5 %collective-permute-start.3 = (bf16[4,336,128]{2,1,0:T(8,128)(2,1)S(1)}, bf16[4,336,128]{2,1,0:T(8,128)(2,1)S(1)}, u32[]{:S(2)}, u32[]{:S(2)}) collective-permute-start(bf16[4,336,128]{2,1,0:T(8,128)(2,1)S(1)} %get-tuple-element.39), channel_id=1, source_target_pairs={{4,8},{5,9},{6,10},{7,11},{8,4},{9,5},{10,6},{11,7},{20,24},{21,25... | collective-permute-start | bytes 1032200 | tf_op jit(solution)/shard_map/ppermute | solution.py:394
  9.3 15.8 %collective-permute-start = (bf16[160,1024]{1,0:T(8,128)(2,1)S(1)}, bf16[160,1024]{1,0:T(8,128)(2,1)S(1)}, u32[]{:S(2)}, u32[]{:S(2)}) collective-permute-start(bf16[160,1024]{1,0:T(8,128)(2,1)S(1)} %get-tuple-element.31), channel_id=1, source_target_pairs={{0,1},{1,0},{2,3},{3,2},{4,5},{5,4},{6,7},{7,6},{8,9},{9,8},{10,11... | collective-permute-start | bytes 983048 | tf_op jit(solution)/shard_map/ppermute | solution.py:394
  10.4 14.8 %collective-permute-start.1 = (bf16[160,1024]{1,0:T(8,128)(2,1)S(1)}, bf16[160,1024]{1,0:T(8,128)(2,1)S(1)}, u32[]{:S(2)}, u32[]{:S(2)}) collective-permute-start(bf16[160,1024]{1,0:T(8,128)(2,1)S(1)} %get-tuple-element.32), channel_id=1, source_target_pairs={{1,2},{2,1},{3,4},{4,3},{5,6},{6,5},{7,8},{8,7},{9,10},{10,9},{11,... | collective-permute-start | bytes 983048 | tf_op jit(solution)/shard_map/ppermute | solution.py:394
  18.0 9.2 %collective-permute-start.4 = (bf16[2,336,128]{2,1,0:T(8,128)(2,1)S(1)}, bf16[2,336,128]{2,1,0:T(8,128)(2,1)S(1)}, u32[]{:S(2)}, u32[]{:S(2)}) collective-permute-start(bf16[2,336,128]{2,1,0:T(8,128)(2,1)S(1)} %get-tuple-element.40), channel_id=1, source_target_pairs={{0,1},{1,0},{2,3},{3,2},{4,5},{5,4},{6,7},{7,6},{8,9},{9,8},{10,11... | collective-permute-start | bytes 516104 | tf_op jit(solution)/shard_map/ppermute | solution.py:430
  19.9 7.4 %collective-permute-start.5 = (bf16[2,336,128]{2,1,0:T(8,128)(2,1)S(1)}, bf16[2,336,128]{2,1,0:T(8,128)(2,1)S(1)}, u32[]{:S(2)}, u32[]{:S(2)}) collective-permute-start(bf16[2,336,128]{2,1,0:T(8,128)(2,1)S(1)} %get-tuple-element.41), channel_id=1, source_target_pairs={{0,2},{1,3},{2,0},{3,1},{4,6},{5,7},{6,4},{7,5},{8,10},{9,11},{10,... | collective-permute-start | bytes 516104 | tf_op jit(solution)/shard_map/ppermute | solution.py:430
  22.6 8.3 %collective-permute-start.6 = (bf16[2,336,128]{2,1,0:T(8,128)(2,1)S(1)}, bf16[2,336,128]{2,1,0:T(8,128)(2,1)S(1)}, u32[]{:S(2)}, u32[]{:S(2)}) collective-permute-start(bf16[2,336,128]{2,1,0:T(8,128)(2,1)S(1)} %get-tuple-element.42), channel_id=1, source_target_pairs={{0,3},{1,2},{2,1},{3,0},{4,7},{5,6},{6,5},{7,4},{8,11},{9,10},{10,... | collective-permute-start | bytes 516104 | tf_op jit(solution)/shard_map/ppermute | solution.py:430
  25.2 5.8 %copy-start.7 = (s32[1,9]{1,0:T(1,128)S(1)}, s32[1,9]{1,0:T(1,128)}, u32[]{:S(2)}) copy-start(s32[1,9]{1,0:T(1,128)} %route_ref.1) | copy-start | bytes 112
  25.2 5.8 %copy-start.8 = (f32[80]{0:T(128)S(1)}, f32[80]{0:T(128)}, u32[]{:S(2)}) copy-start(f32[80]{0:T(128)} %param.13) | copy-start | bytes 964
  31.0 5.5 %copy-start.5 = (f32[80]{0:T(128)S(1)}, f32[80]{0:T(128)}, u32[]{:S(2)}) copy-start(f32[80]{0:T(128)} %param.12) | copy-start | bytes 964
  32.6 6.1 %collective-permute-start.7 = (bf16[160,1024]{1,0:T(8,128)(2,1)S(1)}, bf16[160,1024]{1,0:T(8,128)(2,1)S(1)}, u32[]{:S(2)}, u32[]{:S(2)}) collective-permute-start(bf16[160,1024]{1,0:T(8,128)(2,1)S(1)} %get-tuple-element.45), channel_id=1, source_target_pairs={{0,1},{1,0},{2,3},{3,2},{4,5},{5,4},{6,7},{7,6},{8,9},{9,8},{10,11... | collective-permute-start | bytes 983048 | tf_op jit(solution)/shard_map/ppermute | solution.py:394
  33.1 11.9 %collective-permute-start.8 = (bf16[160,1024]{1,0:T(8,128)(2,1)S(1)}, bf16[160,1024]{1,0:T(8,128)(2,1)S(1)}, u32[]{:S(2)}, u32[]{:S(2)}) collective-permute-start(bf16[160,1024]{1,0:T(8,128)(2,1)S(1)} %get-tuple-element.46), channel_id=1, source_target_pairs={{1,2},{2,1},{3,4},{4,3},{5,6},{6,5},{7,8},{8,7},{9,10},{10,9},{11,... | collective-permute-start | bytes 983048 | tf_op jit(solution)/shard_map/ppermute | solution.py:394

commit v2 on v1

--- a/solution.py
+++ b/solution.py
@@ -16,6 +16,7 @@
 VM = pl.BlockSpec(memory_space=pltpu.VMEM)
 SM = pl.BlockSpec(memory_space=pltpu.SMEM)
 HB = pl.BlockSpec(memory_space=pltpu.HBM)
+AN = pl.BlockSpec(memory_space=pl.ANY)
 
 
 def params(mib=16):
@@ -68,28 +69,19 @@
     dst[BLK_LAT * slots : BLK_LAT * slots + channels, :] = obs_ref[k]
 
 
-def prepare_kernel(
-    channels, height, span,
-    count_ref, x_hbm, w_hbm, obs_hbm,
-    xt_ref, ha_ref, hb_ref, za_ref, zb_ref, own_ref,
-    x_ref, w_ref, obs_ref, sems,
-):
+def prepare_kernel(channels, height, x_hbm, xt_ref, ha_ref, hb_ref, x_ref, sems):
     copies = []
     for index, (start, size) in enumerate(channel_groups(channels)):
         part = pl.ds(start * height, size * height)
         copies.append(pltpu.make_async_copy(x_hbm.at[part], x_ref.at[part], sems.at[index]))
-    copies.append(pltpu.make_async_copy(w_hbm.at[0], w_ref, sems.at[len(copies)]))
-    copies.append(pltpu.make_async_copy(obs_hbm.at[0], obs_ref, sems.at[len(copies)]))
-    for copy in copies:
-        copy.start()
-    p, z_odd, odd = place_in_plane(span)
+        copies[-1].start()
+    odd = lax.axis_index("lat") % 2
     for index, (start, size) in enumerate(channel_groups(channels)):
+        moving = permutation(height, size, False)
         copies[index].wait()
         n = size * height
         moved = jnp.dot(
-            permutation(height, size, False),
-            x_ref[start * height : start * height + n, :],
-            preferred_element_type=F32,
+            moving, x_ref[start * height : start * height + n, :], preferred_element_type=F32
         ).astype(BF16)
         for r in range(height):
             xt_ref[r * channels + start : r * channels + start + size, :] = (
@@ -98,8 +90,23 @@
     last = height - HALO
     ha_ref[...] = xt_ref[rows(last * (1 - odd), HALO, channels), :]
     hb_ref[...] = xt_ref[rows(last * odd, HALO, channels), :]
-    copies[-2].wait()
-    copies[-1].wait()
+
+
+def pack_kernel(
+    channels, span,
+    count_ref, w_hbm, obs_hbm, after_ref,
+    za_ref, zb_ref, own_ref,
+    w_ref, obs_ref, sems,
+):
+    copies = [
+        pltpu.make_async_copy(w_hbm.at[0], w_ref, sems.at[0]),
+        pltpu.make_async_copy(obs_hbm.at[0], obs_ref, sems.at[1]),
+    ]
+    for copy in copies:
+        copy.start()
+    for copy in copies:
+        copy.wait()
+    p, z_odd, _ = place_in_plane(span)
     slots = w_ref.shape[1]
     pack = functools.partial(
         pack_tile, w_ref=w_ref, obs_ref=obs_ref, count_ref=count_ref, slots=slots, channels=channels
@@ -115,7 +122,7 @@
             pack(span + p - lax.bitwise_xor(p, j), own_ref.at[j])
 
 
-def relay_kernel(span, za_ref, zb_ref, own_ref, *outs):
+def relay_kernel(span, after_ref, za_ref, zb_ref, own_ref, *outs):
     p, z_odd, _ = place_in_plane(span)
     for m in range(1, span):
         to = lax.bitwise_xor(p, m)
@@ -394,20 +401,33 @@
         return lax.ppermute(x, "lat", pairs(count, step, parity))
 
     packed = shape((span, pack_rows, BLK_LON))
-    xt, ha, hb, za, zb, own = pl.pallas_call(
-        functools.partial(prepare_kernel, channels, height, span),
-        out_shape=(field(height), field(HALO), field(HALO), packed, packed, packed),
-        in_specs=[SM, HB, HB, HB],
-        out_specs=[VM] * 6,
+    def in_hbm(x):
+        return pltpu.with_memory_space_constraint(x, pltpu.HBM)
+
+    xt, ha, hb = pl.pallas_call(
+        functools.partial(prepare_kernel, channels, height),
+        out_shape=(field(height), field(HALO), field(HALO)),
+        in_specs=[HB],
+        out_specs=[VM] * 3,
         scratch_shapes=[
             pltpu.VMEM((channels * height, columns), BF16),
+            pltpu.SemaphoreType.DMA((len(channel_groups(channels)),)),
+        ],
+        compiler_params=params(),
+    )(in_hbm(noisy_state.reshape(channels * height, columns)))
+    ha, hb = swap(ha, 1, 0), swap(hb, 1, 1)
+    za, zb, own = pl.pallas_call(
+        functools.partial(pack_kernel, channels, span),
+        out_shape=(packed, packed, packed),
+        in_specs=[SM, HB, HB, AN],
+        out_specs=[VM] * 3,
+        scratch_shapes=[
             pltpu.VMEM(tile_weights.shape[1:], BF16),
             pltpu.VMEM(observations.shape[1:], BF16),
-            pltpu.SemaphoreType.DMA((len(channel_groups(channels)) + 2,)),
+            pltpu.SemaphoreType.DMA((2,)),
         ],
         compiler_params=params(),
-    )(counts, noisy_state.reshape(channels * height, columns), tile_weights, observations)
-    ha, hb = swap(ha, 1, 0), swap(hb, 1, 1)
+    )(counts, in_hbm(tile_weights), in_hbm(observations), xt)
     za, zb = swap(za, span, 0), swap(zb, span, 1)
 
     weight = shape((taps * channels, taps * channels))
@@ -422,10 +442,10 @@
     relayed = pl.pallas_call(
         functools.partial(relay_kernel, span),
         out_shape=tuple(shape((2, pack_rows, BLK_LON)) for _ in range(span - 1)),
-        in_specs=[VM] * 3,
+        in_specs=[AN] + [VM] * 3,
         out_specs=[VM] * (span - 1),
         compiler_params=params(),
-    )(za, zb, own)
+    )(w1, za, zb, own)
     arrived = [
         lax.ppermute(relayed[m - 1], "lat", [(i, i ^ m) for i in range(count)]) for m in range(1, span)
     ]

time: 48.4 us -> 46.1 us (0.952)
  local copies, waits for them, and re-layouts: 3.98 us -> 0.03 us
  Pallas kernels: 13.7 us -> 15.2 us
    unnamed x18 -> x12, local copies, waits for them, and re-layouts: 3.98 us -> 0.03 us
    ppermute x3, waiting for transfers between devices: 3.77 us -> 6.38 us  [local(): lax.ppermute(relayed[m - 1], 'lat', [(i, i ^ m) for i in range(count)])]
    ppermute x6, waiting for transfers between devices: 10.7 us -> 8.22 us  [swap(): return lax.ppermute(x, 'lat', pairs(count, step, parity))]
    pallas_call x1 -> x2, Pallas kernels: 2.1 us -> 3.78 us  [the longest x1 1.92 us: local(): pl.pallas_call(functools.partial(prepare_kernel, channels, height), out_s...]
  transfers between devices with their start and end apart: 9 -> 9, of which waited for: 5 -> 4; matrix products, arithmetic and copies ran while one was open for 0% -> 0% of each run, Pallas kernels for 14% -> 15%
where the time goes in v2:
time: 46.1 us; the launch traced here: 45.9 us
  starting transfers between devices  15.9 us (34%)
  Pallas kernels  15.2 us (33%)
  waiting for transfers between devices  14.6 us (32%)
    ppermute x6, starting transfers between devices, swap(): return lax.ppermute(x, 'lat', pairs(count, step, parity))  11.2 us
    ppermute x6, waiting for transfers between devices, swap(): return lax.ppermute(x, 'lat', pairs(count, step, parity))  8.22 us
    ppermute x3, waiting for transfers between devices, local(): lax.ppermute(relayed[m - 1], 'lat', [(i, i ^ m) for i in range(count)])  6.38 us
    ppermute x3, starting transfers between devices, local(): lax.ppermute(relayed[m - 1], 'lat', [(i, i ^ m) for i in range(count)])  4.71 us
    pallas_call x1, Pallas kernels, local(): pl.pallas_call(functools.partial(backward_edge_kernel, channels, height),...  3.13 us
    pallas_call x1, Pallas kernels, local(): pl.pallas_call(functools.partial(forward_inner_kernel, channels, height),...  2.47 us
    pallas_call x1, Pallas kernels, local(): pl.pallas_call(functools.partial(backward_inner_kernel, channels, height)...  2.29 us
    pallas_call x1, Pallas kernels, local(): pl.pallas_call(functools.partial(prepare_kernel, channels, height), out_s...  1.92 us
  transfers between devices with their start and end apart: 9, of which 4 were waited for; matrix products, arithmetic and copies ran while one was open for 0% of the time, Pallas kernels for 15%

profile of v2, /device:TPU:17, one launch (start us, length us, event | category | flops | bytes accessed | tf_op | source)
XLA Modules:
  0.0 45.9 jit_solution(8826060412405148564)
XLA Ops:
  0.0 0.0 copy-start.3
  0.0 1.9 %shard_map.91 = (bf16[640,1024]{1,0:T(8,128)(2,1)S(1)}, bf16[160,1024]{1,0:T(8,128)(2,1)S(1)}, bf16[160,1024]{1,0:T(8,128)(2,1)S(1)}) custom-call(bf16[640,1024]{1,0:T(8,128)(2,1)} %bitcast.7), custom_call_target="tpu_custom_call" | custom-call | tf_op jit(solution)/shard_map/pallas_call | solution.py:407
  1.9 0.0 copy-start
  1.9 0.0 copy-start.1
  2.0 0.0 copy-done.3
  2.0 1.9 %shard_map.94 = (bf16[4,336,128]{2,1,0:T(8,128)(2,1)S(1)}, bf16[4,336,128]{2,1,0:T(8,128)(2,1)S(1)}, bf16[4,336,128]{2,1,0:T(8,128)(2,1)S(1)}) custom-call(s32[1,9]{1,0:T(1,128)S(1)} %copy-done.3, bf16[1,9,128,256]{3,2,1,0:T(8,128)(2,1)} %w_hbm.1, bf16[1,9,80,128]{3,2,1,0:T(8,128)(2,1)} %obs_hbm.1, bf16[640,1024]{1,0:T(8,128)(2,1)S(1)} %get-tuple-element.29.xt_ref.after_ref), custom_call_target="tpu_custom_call" | custom-call | tf_op jit(solution)/shard_map/pallas_call | solution.py:419
  3.8 1.4 %collective-permute-start.2 = (bf16[4,336,128]{2,1,0:T(8,128)(2,1)S(1)}, bf16[4,336,128]{2,1,0:T(8,128)(2,1)S(1)}, u32[]{:S(2)}, u32[]{:S(2)}) collective-permute-start(bf16[4,336,128]{2,1,0:T(8,128)(2,1)S(1)} %get-tuple-element.38), channel_id=1, source_target_pairs={{0,4},{1,5},{2,6},{3,7},{4,0},{5,1},{6,2},{7,3},{8,12},{9,13},{10,... | collective-permute-start | bytes 1032200 | tf_op jit(solution)/shard_map/ppermute | solution.py:401
  5.2 1.9 %collective-permute-start.3 = (bf16[4,336,128]{2,1,0:T(8,128)(2,1)S(1)}, bf16[4,336,128]{2,1,0:T(8,128)(2,1)S(1)}, u32[]{:S(2)}, u32[]{:S(2)}) collective-permute-start(bf16[4,336,128]{2,1,0:T(8,128)(2,1)S(1)} %get-tuple-element.39), channel_id=1, source_target_pairs={{4,8},{5,9},{6,10},{7,11},{8,4},{9,5},{10,6},{11,7},{20,24},{21,25... | collective-permute-start | bytes 1032200 | tf_op jit(solution)/shard_map/ppermute | solution.py:401
  7.1 1.0 %collective-permute-start = (bf16[160,1024]{1,0:T(8,128)(2,1)S(1)}, bf16[160,1024]{1,0:T(8,128)(2,1)S(1)}, u32[]{:S(2)}, u32[]{:S(2)}) collective-permute-start(bf16[160,1024]{1,0:T(8,128)(2,1)S(1)} %get-tuple-element.31), channel_id=1, source_target_pairs={{0,1},{1,0},{2,3},{3,2},{4,5},{5,4},{6,7},{7,6},{8,9},{9,8},{10,11... | collective-permute-start | bytes 983048 | tf_op jit(solution)/shard_map/ppermute | solution.py:401
  8.1 3.1 %collective-permute-start.1 = (bf16[160,1024]{1,0:T(8,128)(2,1)S(1)}, bf16[160,1024]{1,0:T(8,128)(2,1)S(1)}, u32[]{:S(2)}, u32[]{:S(2)}) collective-permute-start(bf16[160,1024]{1,0:T(8,128)(2,1)S(1)} %get-tuple-element.32), channel_id=1, source_target_pairs={{1,2},{2,1},{3,4},{4,3},{5,6},{6,5},{7,8},{8,7},{9,10},{10,9},{11,... | collective-permute-start | bytes 983048 | tf_op jit(solution)/shard_map/ppermute | solution.py:401
  11.2 0.0 copy-done
  11.2 0.0 copy-done.1
  11.2 2.5 %shard_map.92 = (bf16[480,1024]{1,0:T(8,128)(2,1)S(1)}, f32[480,1024]{1,0:T(8,128)S(1)}, f32[320,1024]{1,0:T(8,128)S(1)}, bf16[240,240]{1,0:T(8,128)(2,1)S(1)}, ...) custom-call(bf16[640,1024]{1,0:T(8,128)(2,1)S(1)} %get-tuple-element.29.xt_ref.after_ref, ...), custom_call_target="tpu_custom_call" | custom-call | tf_op jit(solution)/shard_map/pallas_call | solution.py:434
  13.7 0.0 collective-permute-done.2.za_ref
  13.7 2.0 %collective-permute-done.3.zb_ref = bf16[4,336,128]{2,1,0:T(8,128)(2,1)S(1)} collective-permute-done((bf16[4,336,128]{2,1,0:T(8,128)(2,1)S(1)}, bf16[4,336,128]{2,1,0:T(8,128)(2,1)S(1)}, u32[]{:S(2)}, u32[]{:S(2)}) %collective-permute-start.3) | collective-permute-done | bytes 344096 | tf_op jit(solution)/shard_map/ppermute | solution.py:401
  15.7 1.9 %collective-permute-start.4 = (bf16[2,336,128]{2,1,0:T(8,128)(2,1)S(1)}, bf16[2,336,128]{2,1,0:T(8,128)(2,1)S(1)}, u32[]{:S(2)}, u32[]{:S(2)}) collective-permute-start(bf16[2,336,128]{2,1,0:T(8,128)(2,1)S(1)} %get-tuple-element.40), channel_id=1, source_target_pairs={{0,1},{1,0},{2,3},{3,2},{4,5},{5,4},{6,7},{7,6},{8,9},{9,8},{10,11... | collective-permute-start | bytes 516104 | tf_op jit(solution)/shard_map/ppermute | solution.py:450
  17.7 2.7 %collective-permute-start.5 = (bf16[2,336,128]{2,1,0:T(8,128)(2,1)S(1)}, bf16[2,336,128]{2,1,0:T(8,128)(2,1)S(1)}, u32[]{:S(2)}, u32[]{:S(2)}) collective-permute-start(bf16[2,336,128]{2,1,0:T(8,128)(2,1)S(1)} %get-tuple-element.41), channel_id=1, source_target_pairs={{0,2},{1,3},{2,0},{3,1},{4,6},{5,7},{6,4},{7,5},{8,10},{9,11},{10,... | collective-permute-start | bytes 516104 | tf_op jit(solution)/shard_map/ppermute | solution.py:450
  20.4 0.0 collective-permute-start.6
  20.4 0.0 collective-permute-done.a_ref
  20.4 0.0 collective-permute-done.1.b_ref
  20.4 0.0 copy-start.4
  20.5 0.0 copy-start.5
  20.5 1.9 %shard_map.93 = (f32[320,1024]{1,0:T(8,128)S(1)}, f32[320,1024]{1,0:T(8,128)S(1)}) custom-call(bf16[640,1024]{1,0:T(8,128)(2,1)S(1)} %get-tuple-element.29.xt_ref.after_ref, bf16[160,1024]{1,0:T(8,128)(2,1)S(1)} %collective-permute-done.a_ref, bf16[160,1024]{1,0:T(8,128)(2,1)S(1)} %collective-permute-done.1.b_ref, ...), custom_call_target="tpu_custom_call" | custom-call | tf_op jit(solution)/shard_map/pallas_call | solution.py:453
  22.4 0.0 collective-permute-done.4.refs_0_
  22.4 2.7 %collective-permute-done.5.refs_1_ = bf16[2,336,128]{2,1,0:T(8,128)(2,1)S(1)} collective-permute-done((bf16[2,336,128]{2,1,0:T(8,128)(2,1)S(1)}, bf16[2,336,128]{2,1,0:T(8,128)(2,1)S(1)}, u32[]{:S(2)}, u32[]{:S(2)}) %collective-permute-start.5) | collective-permute-done | bytes 172064 | tf_op jit(solution)/shard_map/ppermute | solution.py:450
  25.1 3.7 %collective-permute-done.6.refs_2_ = bf16[2,336,128]{2,1,0:T(8,128)(2,1)S(1)} collective-permute-done((bf16[2,336,128]{2,1,0:T(8,128)(2,1)S(1)}, bf16[2,336,128]{2,1,0:T(8,128)(2,1)S(1)}, u32[]{:S(2)}, u32[]{:S(2)}) %collective-permute-start.6) | collective-permute-done | bytes 172064 | tf_op jit(solution)/shard_map/ppermute | solution.py:450
  28.7 0.0 copy-done.4
  28.7 0.0 copy-done.5
  28.7 0.0 copy-start.2
  28.7 1.6 %shard_map.96 = (f32[640,1024]{1,0:T(8,128)S(1)}, bf16[640,1024]{1,0:T(8,128)(2,1)S(1)}, bf16[160,1024]{1,0:T(8,128)(2,1)S(1)}, bf16[160,1024]{1,0:T(8,128)(2,1)S(1)}) custom-call(s32[1,9]{1,0:T(1,128)S(1)} %copy-done.4, bf16[640,1024]{1,0:T(8,128)(2,1)S(1)} %get-tuple-element.29.xt_ref.after_ref, f32[320,1024]{1,0:T(8,128)S(1)} %get-tuple-element.30.inner_ref.res_ref, ...), custom_call_target="tpu_custom_call" | custom-call | tf_op jit(solution)/shard_map/pallas_call | solution.py:462
  30.4 0.5 %collective-permute-start.7 = (bf16[160,1024]{1,0:T(8,128)(2,1)S(1)}, bf16[160,1024]{1,0:T(8,128)(2,1)S(1)}, u32[]{:S(2)}, u32[]{:S(2)}) collective-permute-start(bf16[160,1024]{1,0:T(8,128)(2,1)S(1)} %get-tuple-element.45), channel_id=1, source_target_pairs={{0,1},{1,0},{2,3},{3,2},{4,5},{5,4},{6,7},{7,6},{8,9},{9,8},{10,11... | collective-permute-start | bytes 983048 | tf_op jit(solution)/shard_map/ppermute | solution.py:401
  30.9 3.3 %collective-permute-start.8 = (bf16[160,1024]{1,0:T(8,128)(2,1)S(1)}, bf16[160,1024]{1,0:T(8,128)(2,1)S(1)}, u32[]{:S(2)}, u32[]{:S(2)}) collective-permute-start(bf16[160,1024]{1,0:T(8,128)(2,1)S(1)} %get-tuple-element.46), channel_id=1, source_target_pairs={{1,2},{2,1},{3,4},{4,3},{5,6},{6,5},{7,8},{8,7},{9,10},{10,9},{11,... | collective-permute-start | bytes 983048 | tf_op jit(solution)/shard_map/ppermute | solution.py:401
  34.2 0.0 copy-done.2
  34.2 2.3 %shard_map.97 = (bf16[480,1024]{1,0:T(8,128)(2,1)S(1)}, bf16[320,1024]{1,0:T(8,128)(2,1)S(1)}) custom-call(f32[640,1024]{1,0:T(8,128)S(1)} %get-tuple-element.43.guide_ref, bf16[640,1024]{1,0:T(8,128)(2,1)S(1)} %get-tuple-element.44.low_ref, f32[480,1024]{1,0:T(8,128)S(1)} %get-tuple-element.48.slope_ref, ...), custom_call_target="tpu_custom_call" | custom-call | tf_op jit(solution)/shard_map/pallas_call | solution.py:472
  36.5 0.0 collective-permute-done.7.a_ref
  36.5 6.2 %collective-permute-done.8.b_ref = bf16[160,1024]{1,0:T(8,128)(2,1)S(1)} collective-permute-done((bf16[160,1024]{1,0:T(8,128)(2,1)S(1)}, bf16[160,1024]{1,0:T(8,128)(2,1)S(1)}, u32[]{:S(2)}, u32[]{:S(2)}) %collective-permute-start.8) | collective-permute-done | bytes 327712 | tf_op jit(solution)/shard_map/ppermute | solution.py:401
  42.8 3.1 %shard_map.98 = bf16[640,1024]{1,0:T(8,128)(2,1)} custom-call(f32[640,1024]{1,0:T(8,128)S(1)} %get-tuple-element.43.guide_ref, bf16[640,1024]{1,0:T(8,128)(2,1)S(1)} %get-tuple-element.44.low_ref, bf16[160,1024]{1,0:T(8,128)(2,1)S(1)} %collective-permute-done.7.a_ref, bf16[160,1024]{1,0:T(8,128)(2,1)S(1)} %collective-permute-done.8.b_ref, ...), custom_call_target="tpu_custom_call" | custom-call | tf_op jit(solution)/shard_map/pallas_call | solution.py:480
  (1 shorter events, 0.0 us)
Async XLA Ops:
  0.0 2.0 %copy-start.3 = (s32[1,9]{1,0:T(1,128)S(1)}, s32[1,9]{1,0:T(1,128)}, u32[]{:S(2)}) copy-start(s32[1,9]{1,0:T(1,128)} %count_ref.1) | copy-start | bytes 112
  1.9 9.3 %copy-start = (bf16[3,3,80,80]{3,2,1,0:T(8,128)(2,1)S(1)}, bf16[3,3,80,80]{3,2,1,0:T(8,128)(2,1)}, u32[]{:S(2)}) copy-start(bf16[3,3,80,80]{3,2,1,0:T(8,128)(2,1)} %raw1_ref.1) | copy-start | bytes 345604
  1.9 9.3 %copy-start.1 = (bf16[3,3,80,80]{3,2,1,0:T(8,128)(2,1)S(1)}, bf16[3,3,80,80]{3,2,1,0:T(8,128)(2,1)}, u32[]{:S(2)}) copy-start(bf16[3,3,80,80]{3,2,1,0:T(8,128)(2,1)} %raw2_ref.1) | copy-start | bytes 345604
  3.8 9.9 %collective-permute-start.2 = (bf16[4,336,128]{2,1,0:T(8,128)(2,1)S(1)}, bf16[4,336,128]{2,1,0:T(8,128)(2,1)S(1)}, u32[]{:S(2)}, u32[]{:S(2)}) collective-permute-start(bf16[4,336,128]{2,1,0:T(8,128)(2,1)S(1)} %get-tuple-element.38), channel_id=1, source_target_pairs={{0,4},{1,5},{2,6},{3,7},{4,0},{5,1},{6,2},{7,3},{8,12},{9,13},{10,... | collective-permute-start | bytes 1032200 | tf_op jit(solution)/shard_map/ppermute | solution.py:401
  5.2 10.5 %collective-permute-start.3 = (bf16[4,336,128]{2,1,0:T(8,128)(2,1)S(1)}, bf16[4,336,128]{2,1,0:T(8,128)(2,1)S(1)}, u32[]{:S(2)}, u32[]{:S(2)}) collective-permute-start(bf16[4,336,128]{2,1,0:T(8,128)(2,1)S(1)} %get-tuple-element.39), channel_id=1, source_target_pairs={{4,8},{5,9},{6,10},{7,11},{8,4},{9,5},{10,6},{11,7},{20,24},{21,25... | collective-permute-start | bytes 1032200 | tf_op jit(solution)/shard_map/ppermute | solution.py:401
  7.1 13.3 %collective-permute-start = (bf16[160,1024]{1,0:T(8,128)(2,1)S(1)}, bf16[160,1024]{1,0:T(8,128)(2,1)S(1)}, u32[]{:S(2)}, u32[]{:S(2)}) collective-permute-start(bf16[160,1024]{1,0:T(8,128)(2,1)S(1)} %get-tuple-element.31), channel_id=1, source_target_pairs={{0,1},{1,0},{2,3},{3,2},{4,5},{5,4},{6,7},{7,6},{8,9},{9,8},{10,11... | collective-permute-start | bytes 983048 | tf_op jit(solution)/shard_map/ppermute | solution.py:401
  8.1 12.3 %collective-permute-start.1 = (bf16[160,1024]{1,0:T(8,128)(2,1)S(1)}, bf16[160,1024]{1,0:T(8,128)(2,1)S(1)}, u32[]{:S(2)}, u32[]{:S(2)}) collective-permute-start(bf16[160,1024]{1,0:T(8,128)(2,1)S(1)} %get-tuple-element.32), channel_id=1, source_target_pairs={{1,2},{2,1},{3,4},{4,3},{5,6},{6,5},{7,8},{8,7},{9,10},{10,9},{11,... | collective-permute-start | bytes 983048 | tf_op jit(solution)/shard_map/ppermute | solution.py:401
  15.7 6.6 %collective-permute-start.4 = (bf16[2,336,128]{2,1,0:T(8,128)(2,1)S(1)}, bf16[2,336,128]{2,1,0:T(8,128)(2,1)S(1)}, u32[]{:S(2)}, u32[]{:S(2)}) collective-permute-start(bf16[2,336,128]{2,1,0:T(8,128)(2,1)S(1)} %get-tuple-element.40), channel_id=1, source_target_pairs={{0,1},{1,0},{2,3},{3,2},{4,5},{5,4},{6,7},{7,6},{8,9},{9,8},{10,11... | collective-permute-start | bytes 516104 | tf_op jit(solution)/shard_map/ppermute | solution.py:450
  17.7 7.4 %collective-permute-start.5 = (bf16[2,336,128]{2,1,0:T(8,128)(2,1)S(1)}, bf16[2,336,128]{2,1,0:T(8,128)(2,1)S(1)}, u32[]{:S(2)}, u32[]{:S(2)}) collective-permute-start(bf16[2,336,128]{2,1,0:T(8,128)(2,1)S(1)} %get-tuple-element.41), channel_id=1, source_target_pairs={{0,2},{1,3},{2,0},{3,1},{4,6},{5,7},{6,4},{7,5},{8,10},{9,11},{10,... | collective-permute-start | bytes 516104 | tf_op jit(solution)/shard_map/ppermute | solution.py:450
  20.4 8.3 %collective-permute-start.6 = (bf16[2,336,128]{2,1,0:T(8,128)(2,1)S(1)}, bf16[2,336,128]{2,1,0:T(8,128)(2,1)S(1)}, u32[]{:S(2)}, u32[]{:S(2)}) collective-permute-start(bf16[2,336,128]{2,1,0:T(8,128)(2,1)S(1)} %get-tuple-element.42), channel_id=1, source_target_pairs={{0,3},{1,2},{2,1},{3,0},{4,7},{5,6},{6,5},{7,4},{8,11},{9,10},{10,... | collective-permute-start | bytes 516104 | tf_op jit(solution)/shard_map/ppermute | solution.py:450
  20.4 8.3 %copy-start.4 = (s32[1,9]{1,0:T(1,128)S(1)}, s32[1,9]{1,0:T(1,128)}, u32[]{:S(2)}) copy-start(s32[1,9]{1,0:T(1,128)} %route_ref.1) | copy-start | bytes 112
  20.5 8.3 %copy-start.5 = (f32[80]{0:T(128)S(1)}, f32[80]{0:T(128)}, u32[]{:S(2)}) copy-start(f32[80]{0:T(128)} %param.13) | copy-start | bytes 964
  28.7 5.5 %copy-start.2 = (f32[80]{0:T(128)S(1)}, f32[80]{0:T(128)}, u32[]{:S(2)}) copy-start(f32[80]{0:T(128)} %param.12) | copy-start | bytes 964
  30.4 6.1 %collective-permute-start.7 = (bf16[160,1024]{1,0:T(8,128)(2,1)S(1)}, bf16[160,1024]{1,0:T(8,128)(2,1)S(1)}, u32[]{:S(2)}, u32[]{:S(2)}) collective-permute-start(bf16[160,1024]{1,0:T(8,128)(2,1)S(1)} %get-tuple-element.45), channel_id=1, source_target_pairs={{0,1},{1,0},{2,3},{3,2},{4,5},{5,4},{6,7},{7,6},{8,9},{9,8},{10,11... | collective-permute-start | bytes 983048 | tf_op jit(solution)/shard_map/ppermute | solution.py:401
  30.9 11.9 %collective-permute-start.8 = (bf16[160,1024]{1,0:T(8,128)(2,1)S(1)}, bf16[160,1024]{1,0:T(8,128)(2,1)S(1)}, u32[]{:S(2)}, u32[]{:S(2)}) collective-permute-start(bf16[160,1024]{1,0:T(8,128)(2,1)S(1)} %get-tuple-element.46), channel_id=1, source_target_pairs={{1,2},{2,1},{3,4},{4,3},{5,6},{6,5},{7,8},{8,7},{9,10},{10,9},{11,... | collective-permute-start | bytes 983048 | tf_op jit(solution)/shard_map/ppermute | solution.py:401

commit v3 on v1

--- a/solution.py
+++ b/solution.py
@@ -16,6 +16,7 @@
 VM = pl.BlockSpec(memory_space=pltpu.VMEM)
 SM = pl.BlockSpec(memory_space=pltpu.SMEM)
 HB = pl.BlockSpec(memory_space=pltpu.HBM)
+AN = pl.BlockSpec(memory_space=pl.ANY)
 
 
 def params(mib=16):
@@ -68,6 +69,21 @@
     dst[BLK_LAT * slots : BLK_LAT * slots + channels, :] = obs_ref[k]
 
 
+def edge_pair(src_ref, ha_ref, hb_ref, height, channels):
+    me, odd = lax.axis_index("lat"), lax.axis_index("lat") % 2
+    last = height - HALO
+    ha_ref[...] = src_ref[rows(last * (1 - odd), HALO, channels), :]
+    alone = (me == 0) | (me == lax.axis_size("lat") - 1)
+
+    @pl.when(alone)
+    def _():
+        hb_ref[...] = jnp.zeros_like(hb_ref)
+
+    @pl.when(jnp.logical_not(alone))
+    def _():
+        hb_ref[...] = src_ref[rows(last * odd, HALO, channels), :]
+
+
 def prepare_kernel(
     channels, height, span,
     count_ref, x_hbm, w_hbm, obs_hbm,
@@ -75,31 +91,28 @@
     x_ref, w_ref, obs_ref, sems,
 ):
     copies = []
-    for index, (start, size) in enumerate(channel_groups(channels)):
+    for start, size in channel_groups(channels):
         part = pl.ds(start * height, size * height)
-        copies.append(pltpu.make_async_copy(x_hbm.at[part], x_ref.at[part], sems.at[index]))
+        copies.append(pltpu.make_async_copy(x_hbm.at[part], x_ref.at[part], sems.at[len(copies)]))
     copies.append(pltpu.make_async_copy(w_hbm.at[0], w_ref, sems.at[len(copies)]))
     copies.append(pltpu.make_async_copy(obs_hbm.at[0], obs_ref, sems.at[len(copies)]))
     for copy in copies:
         copy.start()
-    p, z_odd, odd = place_in_plane(span)
     for index, (start, size) in enumerate(channel_groups(channels)):
+        moving = permutation(height, size, False)
         copies[index].wait()
         n = size * height
         moved = jnp.dot(
-            permutation(height, size, False),
-            x_ref[start * height : start * height + n, :],
-            preferred_element_type=F32,
+            moving, x_ref[start * height : start * height + n, :], preferred_element_type=F32
         ).astype(BF16)
         for r in range(height):
             xt_ref[r * channels + start : r * channels + start + size, :] = (
                 moved[r * size : (r + 1) * size, :]
             )
-    last = height - HALO
-    ha_ref[...] = xt_ref[rows(last * (1 - odd), HALO, channels), :]
-    hb_ref[...] = xt_ref[rows(last * odd, HALO, channels), :]
+    edge_pair(xt_ref, ha_ref, hb_ref, height, channels)
     copies[-2].wait()
     copies[-1].wait()
+    p, z_odd, _ = place_in_plane(span)
     slots = w_ref.shape[1]
     pack = functools.partial(
         pack_tile, w_ref=w_ref, obs_ref=obs_ref, count_ref=count_ref, slots=slots, channels=channels
@@ -115,7 +128,7 @@
             pack(span + p - lax.bitwise_xor(p, j), own_ref.at[j])
 
 
-def relay_kernel(span, za_ref, zb_ref, own_ref, *outs):
+def relay_kernel(span, after_ref, za_ref, zb_ref, own_ref, *outs):
     p, z_odd, _ = place_in_plane(span)
     for m in range(1, span):
         to = lax.bitwise_xor(p, m)
@@ -243,7 +256,7 @@
     near_refs, (guide_ref, low_ref, ga_ref, gb_ref) = refs[: span - 1], refs[span - 1 :]
     slots = BLK_LON
     across = columns // BLK_LON
-    p, z_odd, odd = place_in_plane(span)
+    p, z_odd, _ = place_in_plane(span)
     guide_ref[...] = jnp.zeros_like(guide_ref)
     jobs = [
         (span, own_ref.at[0]),
@@ -300,10 +313,8 @@
     for place, term in zip(places, terms):
         for i in range(BLK_LAT):
             guide_ref[place[i]] += term[i]
-    last = height - HALO
     low_ref[...] = guide_ref[...].astype(BF16)
-    ga_ref[...] = low_ref[rows(last * (1 - odd), HALO, channels), :]
-    gb_ref[...] = low_ref[rows(last * odd, HALO, channels), :]
+    edge_pair(low_ref, ga_ref, gb_ref, height, channels)
 
 
 def backward_inner_kernel(
@@ -364,12 +375,15 @@
         ).astype(BF16)
 
 
-def pairs(count, step, parity):
+def pairs(groups, count, partner):
     found = []
-    for i in range(count):
-        other = i + step if (i // step) % 2 == parity else i - step
-        if 0 <= other < count:
-            found.append((i, other))
+    for g in range(groups):
+        for i in range(count):
+            other = partner(i)
+            if 0 <= other < count:
+                found.append((g * count + i, g * count + other))
+            elif groups % 2 == 0:
+                found.append((g * count + i, (g ^ 1) * count + i))
     return found
 
 
@@ -390,10 +404,16 @@
     def buffer(n, dtype=BF16):
         return pltpu.VMEM((n * channels, columns), dtype)
 
+    def exchange(x, partner):
+        return lax.ppermute(x, ("grp", "lat"), pairs(lax.axis_size("grp"), count, partner))
+
     def swap(x, step, parity):
-        return lax.ppermute(x, "lat", pairs(count, step, parity))
+        return exchange(x, lambda i: i + step if (i // step) % 2 == parity else i - step)
 
     packed = shape((span, pack_rows, BLK_LON))
+    def in_hbm(x):
+        return pltpu.with_memory_space_constraint(x, pltpu.HBM)
+
     xt, ha, hb, za, zb, own = pl.pallas_call(
         functools.partial(prepare_kernel, channels, height, span),
         out_shape=(field(height), field(HALO), field(HALO), packed, packed, packed),
@@ -406,7 +426,12 @@
             pltpu.SemaphoreType.DMA((len(channel_groups(channels)) + 2,)),
         ],
         compiler_params=params(),
-    )(counts, noisy_state.reshape(channels * height, columns), tile_weights, observations)
+    )(
+        counts,
+        in_hbm(noisy_state.reshape(channels * height, columns)),
+        in_hbm(tile_weights),
+        in_hbm(observations),
+    )
     ha, hb = swap(ha, 1, 0), swap(hb, 1, 1)
     za, zb = swap(za, span, 0), swap(zb, span, 1)
 
@@ -422,13 +447,11 @@
     relayed = pl.pallas_call(
         functools.partial(relay_kernel, span),
         out_shape=tuple(shape((2, pack_rows, BLK_LON)) for _ in range(span - 1)),
-        in_specs=[VM] * 3,
+        in_specs=[AN] + [VM] * 3,
         out_specs=[VM] * (span - 1),
         compiler_params=params(),
-    )(za, zb, own)
-    arrived = [
-        lax.ppermute(relayed[m - 1], "lat", [(i, i ^ m) for i in range(count)]) for m in range(1, span)
-    ]
+    )(w1, za, zb, own)
+    arrived = [exchange(relayed[m - 1], lambda i, m=m: i ^ m) for m in range(1, span)]
 
     slope_ed, res_ed = pl.pallas_call(
         functools.partial(forward_edge_kernel, channels, height),

time: 48.4 us -> 41.9 us (0.87)
  starting transfers between devices: 15.8 us -> 10.1 us
  local copies, waits for them, and re-layouts: 3.98 us -> 0.72 us
  waiting for transfers between devices: 14.5 us -> 16.7 us
    ppermute x9, starting transfers between devices: 15.8 us -> 10.1 us  [exchange(): lax.ppermute(x, ('grp', 'lat'), pairs(lax.axis_size('grp'), count, partner))]
    unnamed x18 -> x12, local copies, waits for them, and re-layouts: 3.98 us -> 0.72 us
    ppermute x9, waiting for transfers between devices: 14.5 us -> 16.7 us  [exchange(): lax.ppermute(x, ('grp', 'lat'), pairs(lax.axis_size('grp'), count, partner))]
    pallas_call x1, Pallas kernels: 2.1 us -> 2.7 us  [local(): pl.pallas_call(functools.partial(prepare_kernel, channels, height, span),...]
  transfers between devices with their start and end apart: 9 -> 9, of which waited for: 5 -> 5; matrix products, arithmetic and copies ran while one was open for 0% -> 0% of each run, Pallas kernels for 14% -> 16%
where the time goes in v3:
time: 41.9 us; the launch traced here: 41.7 us
  waiting for transfers between devices  16.7 us (40%)
  Pallas kernels  14.1 us (34%)
  starting transfers between devices  10.1 us (24%)
  local copies, waits for them, and re-layouts  0.72 us (2%)
    ppermute x9, waiting for transfers between devices, exchange(): lax.ppermute(x, ('grp', 'lat'), pairs(lax.axis_size('grp'), count, partner))  16.7 us
    ppermute x9, starting transfers between devices, exchange(): lax.ppermute(x, ('grp', 'lat'), pairs(lax.axis_size('grp'), count, partner))  10.1 us
    pallas_call x1, Pallas kernels, local(): pl.pallas_call(functools.partial(backward_edge_kernel, channels, height),...  3.13 us
    pallas_call x1, Pallas kernels, local(): pl.pallas_call(functools.partial(prepare_kernel, channels, height, span),...  2.7 us
    pallas_call x1, Pallas kernels, local(): pl.pallas_call(functools.partial(forward_inner_kernel, channels, height),...  2.46 us
    pallas_call x1, Pallas kernels, local(): pl.pallas_call(functools.partial(backward_inner_kernel, channels, height)...  2.28 us
    pallas_call x1, Pallas kernels, local(): pl.pallas_call(functools.partial(forward_edge_kernel, channels, height),...  1.88 us
    pallas_call x1, Pallas kernels, local(): pl.pallas_call(functools.partial(tile_kernel, channels, height, columns,...  1.64 us
  transfers between devices with their start and end apart: 9, of which 5 were waited for; matrix products, arithmetic and copies ran while one was open for 0% of the time, Pallas kernels for 16%

profile of v3, /device:TPU:17, one launch (start us, length us, event | category | flops | bytes accessed | tf_op | source)
XLA Modules:
  0.0 41.7 jit_solution(6674106704836405503)
XLA Ops:
  0.0 0.0 copy-start.1
  0.0 0.0 copy-start
  0.0 0.0 copy-start.3
  0.0 0.7 %copy-done.3 = s32[1,9]{1,0:T(1,128)S(1)} copy-done((s32[1,9]{1,0:T(1,128)S(1)}, s32[1,9]{1,0:T(1,128)}, u32[]{:S(2)}) %copy-start.3) | copy-done | bytes 60
  0.7 2.7 %shard_map.91 = (bf16[640,1024]{1,0:T(8,128)(2,1)S(1)}, bf16[160,1024]{1,0:T(8,128)(2,1)S(1)}, bf16[160,1024]{1,0:T(8,128)(2,1)S(1)}, bf16[4,336,128]{2,1,0:T(8,...) custom-call(s32[1,9]{1,0:T(1,128)S(1)} %copy-done.3, bf16[640,1024]{1,0:T(8,128)(2,1)} %bitcast.7, ...), custom_call_target="tpu_custom_call" | custom-call | tf_op jit(solution)/shard_map/pallas_call | solution.py:417
  3.4 1.4 %collective-permute-start.2 = (bf16[4,336,128]{2,1,0:T(8,128)(2,1)S(1)}, bf16[4,336,128]{2,1,0:T(8,128)(2,1)S(1)}, u32[]{:S(2)}, u32[]{:S(2)}) collective-permute-start(bf16[4,336,128]{2,1,0:T(8,128)(2,1)S(1)} %get-tuple-element.38), channel_id=1, source_target_pairs={{0,4},{1,5},{2,6},{3,7},{4,0},{5,1},{6,2},{7,3},{8,12},{9,13},{10,... | collective-permute-start | bytes 1032200 | tf_op jit(solution)/shard_map/ppermute | solution.py:408
  4.8 0.0 collective-permute-start.3
  4.8 1.0 %collective-permute-start = (bf16[160,1024]{1,0:T(8,128)(2,1)S(1)}, bf16[160,1024]{1,0:T(8,128)(2,1)S(1)}, u32[]{:S(2)}, u32[]{:S(2)}) collective-permute-start(bf16[160,1024]{1,0:T(8,128)(2,1)S(1)} %get-tuple-element.31), channel_id=1, source_target_pairs={{0,1},{1,0},{2,3},{3,2},{4,5},{5,4},{6,7},{7,6},{8,9},{9,8},{10,11... | collective-permute-start | bytes 983048 | tf_op jit(solution)/shard_map/ppermute | solution.py:408
  5.7 1.1 %collective-permute-start.1 = (bf16[160,1024]{1,0:T(8,128)(2,1)S(1)}, bf16[160,1024]{1,0:T(8,128)(2,1)S(1)}, u32[]{:S(2)}, u32[]{:S(2)}) collective-permute-start(bf16[160,1024]{1,0:T(8,128)(2,1)S(1)} %get-tuple-element.32), channel_id=1, source_target_pairs={{0,16},{1,2},{2,1},{3,4},{4,3},{5,6},{6,5},{7,8},{8,7},{9,10},{10,... | collective-permute-start | bytes 983048 | tf_op jit(solution)/shard_map/ppermute | solution.py:408
  6.9 0.0 copy-done.1
  6.9 0.0 copy-done
  6.9 2.5 %shard_map.92 = (bf16[480,1024]{1,0:T(8,128)(2,1)S(1)}, f32[480,1024]{1,0:T(8,128)S(1)}, f32[320,1024]{1,0:T(8,128)S(1)}, bf16[240,240]{1,0:T(8,128)(2,1)S(1)}, ...) custom-call(bf16[640,1024]{1,0:T(8,128)(2,1)S(1)} %get-tuple-element.29.xt_ref, ...), custom_call_target="tpu_custom_call" | custom-call | tf_op jit(solution)/shard_map/pallas_call | solution.py:439
  9.3 3.1 %collective-permute-done.2.za_ref = bf16[4,336,128]{2,1,0:T(8,128)(2,1)S(1)} collective-permute-done((bf16[4,336,128]{2,1,0:T(8,128)(2,1)S(1)}, bf16[4,336,128]{2,1,0:T(8,128)(2,1)S(1)}, u32[]{:S(2)}, u32[]{:S(2)}) %collective-permute-start.2) | collective-permute-done | bytes 344096 | tf_op jit(solution)/shard_map/ppermute | solution.py:408
  12.4 1.0 %collective-permute-done.3.zb_ref = bf16[4,336,128]{2,1,0:T(8,128)(2,1)S(1)} collective-permute-done((bf16[4,336,128]{2,1,0:T(8,128)(2,1)S(1)}, bf16[4,336,128]{2,1,0:T(8,128)(2,1)S(1)}, u32[]{:S(2)}, u32[]{:S(2)}) %collective-permute-start.3) | collective-permute-done | bytes 344096 | tf_op jit(solution)/shard_map/ppermute | solution.py:408
  13.4 1.9 %collective-permute-start.4 = (bf16[2,336,128]{2,1,0:T(8,128)(2,1)S(1)}, bf16[2,336,128]{2,1,0:T(8,128)(2,1)S(1)}, u32[]{:S(2)}, u32[]{:S(2)}) collective-permute-start(bf16[2,336,128]{2,1,0:T(8,128)(2,1)S(1)} %get-tuple-element.40), channel_id=1, source_target_pairs={{0,1},{1,0},{2,3},{3,2},{4,5},{5,4},{6,7},{7,6},{8,9},{9,8},{10,11... | collective-permute-start | bytes 516104 | tf_op jit(solution)/shard_map/ppermute | solution.py:408
  15.4 2.7 %collective-permute-start.5 = (bf16[2,336,128]{2,1,0:T(8,128)(2,1)S(1)}, bf16[2,336,128]{2,1,0:T(8,128)(2,1)S(1)}, u32[]{:S(2)}, u32[]{:S(2)}) collective-permute-start(bf16[2,336,128]{2,1,0:T(8,128)(2,1)S(1)} %get-tuple-element.41), channel_id=1, source_target_pairs={{0,2},{1,3},{2,0},{3,1},{4,6},{5,7},{6,4},{7,5},{8,10},{9,11},{10,... | collective-permute-start | bytes 516104 | tf_op jit(solution)/shard_map/ppermute | solution.py:408
  18.1 0.0 collective-permute-start.6
  18.1 0.0 collective-permute-done.a_ref
  18.1 0.0 collective-permute-done.1.b_ref
  18.2 0.0 copy-start.4
  18.2 0.0 copy-start.5
  18.2 1.9 %shard_map.93 = (f32[320,1024]{1,0:T(8,128)S(1)}, f32[320,1024]{1,0:T(8,128)S(1)}) custom-call(bf16[640,1024]{1,0:T(8,128)(2,1)S(1)} %get-tuple-element.29.xt_ref, bf16[160,1024]{1,0:T(8,128)(2,1)S(1)} %collective-permute-done.a_ref, bf16[160,1024]{1,0:T(8,128)(2,1)S(1)} %collective-permute-done.1.b_ref, bf16[480,1024]{1,0:T(8,128)(2,1)S(1)} %get-tuple-element.33.hid_ref, ...), custom_call_target="tpu_custom_call" | custom-call | tf_op jit(solution)/shard_map/pallas_call | solution.py:456
  20.1 0.0 collective-permute-done.4.refs_0_
  20.1 2.7 %collective-permute-done.5.refs_1_ = bf16[2,336,128]{2,1,0:T(8,128)(2,1)S(1)} collective-permute-done((bf16[2,336,128]{2,1,0:T(8,128)(2,1)S(1)}, bf16[2,336,128]{2,1,0:T(8,128)(2,1)S(1)}, u32[]{:S(2)}, u32[]{:S(2)}) %collective-permute-start.5) | collective-permute-done | bytes 172064 | tf_op jit(solution)/shard_map/ppermute | solution.py:408
  22.8 3.7 %collective-permute-done.6.refs_2_ = bf16[2,336,128]{2,1,0:T(8,128)(2,1)S(1)} collective-permute-done((bf16[2,336,128]{2,1,0:T(8,128)(2,1)S(1)}, bf16[2,336,128]{2,1,0:T(8,128)(2,1)S(1)}, u32[]{:S(2)}, u32[]{:S(2)}) %collective-permute-start.6) | collective-permute-done | bytes 172064 | tf_op jit(solution)/shard_map/ppermute | solution.py:408
  26.4 0.0 copy-done.4
  26.4 0.0 copy-done.5
  26.4 0.0 copy-start.2
  26.5 1.6 %shard_map.95 = (f32[640,1024]{1,0:T(8,128)S(1)}, bf16[640,1024]{1,0:T(8,128)(2,1)S(1)}, bf16[160,1024]{1,0:T(8,128)(2,1)S(1)}, bf16[160,1024]{1,0:T(8,128)(2,1)S(1)}) custom-call(s32[1,9]{1,0:T(1,128)S(1)} %copy-done.4, bf16[640,1024]{1,0:T(8,128)(2,1)S(1)} %get-tuple-element.29.xt_ref, f32[320,1024]{1,0:T(8,128)S(1)} %get-tuple-element.30.inner_ref.res_ref, ...), custom_call_target="tpu_custom_call" | custom-call | tf_op jit(solution)/shard_map/pallas_call | solution.py:465
  28.1 0.5 %collective-permute-start.7 = (bf16[160,1024]{1,0:T(8,128)(2,1)S(1)}, bf16[160,1024]{1,0:T(8,128)(2,1)S(1)}, u32[]{:S(2)}, u32[]{:S(2)}) collective-permute-start(bf16[160,1024]{1,0:T(8,128)(2,1)S(1)} %get-tuple-element.45), channel_id=1, source_target_pairs={{0,1},{1,0},{2,3},{3,2},{4,5},{5,4},{6,7},{7,6},{8,9},{9,8},{10,11... | collective-permute-start | bytes 983048 | tf_op jit(solution)/shard_map/ppermute | solution.py:408
  28.6 1.4 %collective-permute-start.8 = (bf16[160,1024]{1,0:T(8,128)(2,1)S(1)}, bf16[160,1024]{1,0:T(8,128)(2,1)S(1)}, u32[]{:S(2)}, u32[]{:S(2)}) collective-permute-start(bf16[160,1024]{1,0:T(8,128)(2,1)S(1)} %get-tuple-element.46), channel_id=1, source_target_pairs={{0,16},{1,2},{2,1},{3,4},{4,3},{5,6},{6,5},{7,8},{8,7},{9,10},{10,... | collective-permute-start | bytes 983048 | tf_op jit(solution)/shard_map/ppermute | solution.py:408
  30.0 0.0 copy-done.2
  30.0 2.3 %shard_map.96 = (bf16[480,1024]{1,0:T(8,128)(2,1)S(1)}, bf16[320,1024]{1,0:T(8,128)(2,1)S(1)}) custom-call(f32[640,1024]{1,0:T(8,128)S(1)} %get-tuple-element.43.guide_ref, bf16[640,1024]{1,0:T(8,128)(2,1)S(1)} %get-tuple-element.44.low_ref, f32[480,1024]{1,0:T(8,128)S(1)} %get-tuple-element.48.slope_ref, ...), custom_call_target="tpu_custom_call" | custom-call | tf_op jit(solution)/shard_map/pallas_call | solution.py:475
  32.3 0.0 collective-permute-done.7.a_ref
  32.3 6.3 %collective-permute-done.8.b_ref = bf16[160,1024]{1,0:T(8,128)(2,1)S(1)} collective-permute-done((bf16[160,1024]{1,0:T(8,128)(2,1)S(1)}, bf16[160,1024]{1,0:T(8,128)(2,1)S(1)}, u32[]{:S(2)}, u32[]{:S(2)}) %collective-permute-start.8) | collective-permute-done | bytes 327712 | tf_op jit(solution)/shard_map/ppermute | solution.py:408
  38.6 3.1 %shard_map.97 = bf16[640,1024]{1,0:T(8,128)(2,1)} custom-call(f32[640,1024]{1,0:T(8,128)S(1)} %get-tuple-element.43.guide_ref, bf16[640,1024]{1,0:T(8,128)(2,1)S(1)} %get-tuple-element.44.low_ref, bf16[160,1024]{1,0:T(8,128)(2,1)S(1)} %collective-permute-done.7.a_ref, bf16[160,1024]{1,0:T(8,128)(2,1)S(1)} %collective-permute-done.8.b_ref, ...), custom_call_target="tpu_custom_call" | custom-call | tf_op jit(solution)/shard_map/pallas_call | solution.py:483
  (1 shorter events, 0.0 us)
Async XLA Ops:
  0.0 6.9 %copy-start.1 = (bf16[3,3,80,80]{3,2,1,0:T(8,128)(2,1)S(1)}, bf16[3,3,80,80]{3,2,1,0:T(8,128)(2,1)}, u32[]{:S(2)}) copy-start(bf16[3,3,80,80]{3,2,1,0:T(8,128)(2,1)} %raw2_ref.1) | copy-start | bytes 345604
  0.0 6.9 %copy-start = (bf16[3,3,80,80]{3,2,1,0:T(8,128)(2,1)S(1)}, bf16[3,3,80,80]{3,2,1,0:T(8,128)(2,1)}, u32[]{:S(2)}) copy-start(bf16[3,3,80,80]{3,2,1,0:T(8,128)(2,1)} %raw1_ref.1) | copy-start | bytes 345604
  0.0 0.7 %copy-start.3 = (s32[1,9]{1,0:T(1,128)S(1)}, s32[1,9]{1,0:T(1,128)}, u32[]{:S(2)}) copy-start(s32[1,9]{1,0:T(1,128)} %count_ref.1) | copy-start | bytes 112
  3.4 9.0 %collective-permute-start.2 = (bf16[4,336,128]{2,1,0:T(8,128)(2,1)S(1)}, bf16[4,336,128]{2,1,0:T(8,128)(2,1)S(1)}, u32[]{:S(2)}, u32[]{:S(2)}) collective-permute-start(bf16[4,336,128]{2,1,0:T(8,128)(2,1)S(1)} %get-tuple-element.38), channel_id=1, source_target_pairs={{0,4},{1,5},{2,6},{3,7},{4,0},{5,1},{6,2},{7,3},{8,12},{9,13},{10,... | collective-permute-start | bytes 1032200 | tf_op jit(solution)/shard_map/ppermute | solution.py:408
  4.8 8.6 %collective-permute-start.3 = (bf16[4,336,128]{2,1,0:T(8,128)(2,1)S(1)}, bf16[4,336,128]{2,1,0:T(8,128)(2,1)S(1)}, u32[]{:S(2)}, u32[]{:S(2)}) collective-permute-start(bf16[4,336,128]{2,1,0:T(8,128)(2,1)S(1)} %get-tuple-element.39), channel_id=1, source_target_pairs={{0,16},{1,17},{2,18},{3,19},{4,8},{5,9},{6,10},{7,11},{8,4},{9,5},... | collective-permute-start | bytes 1032200 | tf_op jit(solution)/shard_map/ppermute | solution.py:408
  4.8 13.4 %collective-permute-start = (bf16[160,1024]{1,0:T(8,128)(2,1)S(1)}, bf16[160,1024]{1,0:T(8,128)(2,1)S(1)}, u32[]{:S(2)}, u32[]{:S(2)}) collective-permute-start(bf16[160,1024]{1,0:T(8,128)(2,1)S(1)} %get-tuple-element.31), channel_id=1, source_target_pairs={{0,1},{1,0},{2,3},{3,2},{4,5},{5,4},{6,7},{7,6},{8,9},{9,8},{10,11... | collective-permute-start | bytes 983048 | tf_op jit(solution)/shard_map/ppermute | solution.py:408
  5.7 12.4 %collective-permute-start.1 = (bf16[160,1024]{1,0:T(8,128)(2,1)S(1)}, bf16[160,1024]{1,0:T(8,128)(2,1)S(1)}, u32[]{:S(2)}, u32[]{:S(2)}) collective-permute-start(bf16[160,1024]{1,0:T(8,128)(2,1)S(1)} %get-tuple-element.32), channel_id=1, source_target_pairs={{0,16},{1,2},{2,1},{3,4},{4,3},{5,6},{6,5},{7,8},{8,7},{9,10},{10,... | collective-permute-start | bytes 983048 | tf_op jit(solution)/shard_map/ppermute | solution.py:408
  13.4 6.6 %collective-permute-start.4 = (bf16[2,336,128]{2,1,0:T(8,128)(2,1)S(1)}, bf16[2,336,128]{2,1,0:T(8,128)(2,1)S(1)}, u32[]{:S(2)}, u32[]{:S(2)}) collective-permute-start(bf16[2,336,128]{2,1,0:T(8,128)(2,1)S(1)} %get-tuple-element.40), channel_id=1, source_target_pairs={{0,1},{1,0},{2,3},{3,2},{4,5},{5,4},{6,7},{7,6},{8,9},{9,8},{10,11... | collective-permute-start | bytes 516104 | tf_op jit(solution)/shard_map/ppermute | solution.py:408
  15.4 7.4 %collective-permute-start.5 = (bf16[2,336,128]{2,1,0:T(8,128)(2,1)S(1)}, bf16[2,336,128]{2,1,0:T(8,128)(2,1)S(1)}, u32[]{:S(2)}, u32[]{:S(2)}) collective-permute-start(bf16[2,336,128]{2,1,0:T(8,128)(2,1)S(1)} %get-tuple-element.41), channel_id=1, source_target_pairs={{0,2},{1,3},{2,0},{3,1},{4,6},{5,7},{6,4},{7,5},{8,10},{9,11},{10,... | collective-permute-start | bytes 516104 | tf_op jit(solution)/shard_map/ppermute | solution.py:408
  18.1 8.3 %collective-permute-start.6 = (bf16[2,336,128]{2,1,0:T(8,128)(2,1)S(1)}, bf16[2,336,128]{2,1,0:T(8,128)(2,1)S(1)}, u32[]{:S(2)}, u32[]{:S(2)}) collective-permute-start(bf16[2,336,128]{2,1,0:T(8,128)(2,1)S(1)} %get-tuple-element.42), channel_id=1, source_target_pairs={{0,3},{1,2},{2,1},{3,0},{4,7},{5,6},{6,5},{7,4},{8,11},{9,10},{10,... | collective-permute-start | bytes 516104 | tf_op jit(solution)/shard_map/ppermute | solution.py:408
  18.2 8.3 %copy-start.4 = (s32[1,9]{1,0:T(1,128)S(1)}, s32[1,9]{1,0:T(1,128)}, u32[]{:S(2)}) copy-start(s32[1,9]{1,0:T(1,128)} %route_ref.1) | copy-start | bytes 112
  18.2 8.3 %copy-start.5 = (f32[80]{0:T(128)S(1)}, f32[80]{0:T(128)}, u32[]{:S(2)}) copy-start(f32[80]{0:T(128)} %param.13) | copy-start | bytes 964
  26.4 3.6 %copy-start.2 = (f32[80]{0:T(128)S(1)}, f32[80]{0:T(128)}, u32[]{:S(2)}) copy-start(f32[80]{0:T(128)} %param.12) | copy-start | bytes 964
  28.1 4.2 %collective-permute-start.7 = (bf16[160,1024]{1,0:T(8,128)(2,1)S(1)}, bf16[160,1024]{1,0:T(8,128)(2,1)S(1)}, u32[]{:S(2)}, u32[]{:S(2)}) collective-permute-start(bf16[160,1024]{1,0:T(8,128)(2,1)S(1)} %get-tuple-element.45), channel_id=1, source_target_pairs={{0,1},{1,0},{2,3},{3,2},{4,5},{5,4},{6,7},{7,6},{8,9},{9,8},{10,11... | collective-permute-start | bytes 983048 | tf_op jit(solution)/shard_map/ppermute | solution.py:408
  28.6 10.0 %collective-permute-start.8 = (bf16[160,1024]{1,0:T(8,128)(2,1)S(1)}, bf16[160,1024]{1,0:T(8,128)(2,1)S(1)}, u32[]{:S(2)}, u32[]{:S(2)}) collective-permute-start(bf16[160,1024]{1,0:T(8,128)(2,1)S(1)} %get-tuple-element.46), channel_id=1, source_target_pairs={{0,16},{1,2},{2,1},{3,4},{4,3},{5,6},{6,5},{7,8},{8,7},{9,10},{10,... | collective-permute-start | bytes 983048 | tf_op jit(solution)/shard_map/ppermute | solution.py:408

commit v4 on v3

v4 whole, which is shorter than its diff:
```python
import functools

import jax
import jax.numpy as jnp
from jax import lax
from jax.experimental import pallas as pl
from jax.experimental.pallas import tpu as pltpu
from jax.sharding import PartitionSpec as P

BLK_LAT = 2
BLK_LON = 128
HALO = 2
F32 = jnp.float32
BF16 = jnp.bfloat16

VM = pl.BlockSpec(memory_space=pltpu.VMEM)
SM = pl.BlockSpec(memory_space=pltpu.SMEM)
HB = pl.BlockSpec(memory_space=pltpu.HBM)
AN = pl.BlockSpec(memory_space=pl.ANY)


def params(mib=16):
    return pltpu.CompilerParams(vmem_limit_bytes=mib << 20)


def shape(dims, dtype=BF16):
    return jax.ShapeDtypeStruct(dims, dtype)


def rows(index, count, channels):
    start = index * channels
    if not isinstance(start, int):
        start = pl.multiple_of(start, 16)
    return pl.ds(start, count * channels)


def permutation(height, group, back):
    n = height * group
    out = lax.broadcasted_iota(jnp.int32, (n, n), 0)
    src = lax.broadcasted_iota(jnp.int32, (n, n), 1)
    if back:
        want = (out % height) * group + out // height
    else:
        want = (out % group) * height + out // group
    return jnp.where(src == want, 1.0, 0.0).astype(BF16)


def channel_groups(channels):
    return [(start, min(32, channels - start)) for start in range(0, channels, 32)]


def as_column(row):
    n = row.shape[1]
    here = lax.broadcasted_iota(jnp.int32, (n, n), 0) == lax.broadcasted_iota(jnp.int32, (n, n), 1)
    return jnp.sum(jnp.where(here, jnp.broadcast_to(row, (n, n)), 0.0), axis=1, keepdims=True)


def place_in_plane(span):
    me = lax.axis_index("lat")
    return me % span, (me // span) % 2, me % 2


def pack_tile(k, dst, w_ref, obs_ref, count_ref, slots, channels):
    live = lax.broadcasted_iota(jnp.int32, (slots, BLK_LON), 0) < count_ref[0, k]
    zero = jnp.zeros((slots, BLK_LON), BF16)
    for i in range(BLK_LAT):
        half = w_ref[k, :, i * BLK_LON : (i + 1) * BLK_LON]
        dst[i * slots : (i + 1) * slots, :] = jnp.where(live, half, zero)
    dst[BLK_LAT * slots : BLK_LAT * slots + channels, :] = obs_ref[k]


def edge_pair(src_ref, ha_ref, hb_ref, height, channels):
    me, odd = lax.axis_index("lat"), lax.axis_index("lat") % 2
    last = height - HALO
    ha_ref[...] = src_ref[rows(last * (1 - odd), HALO, channels), :]
    alone = (me == 0) | (me == lax.axis_size("lat") - 1)

    @pl.when(alone)
    def _():
        hb_ref[...] = jnp.zeros_like(hb_ref)

    @pl.when(jnp.logical_not(alone))
    def _():
        hb_ref[...] = src_ref[rows(last * odd, HALO, channels), :]


def pack_kernel(
    channels, span,
    count_hbm, w_hbm, obs_hbm, x_hbm,
    za_ref, zb_ref, own_ref, x_ref,
    count_ref, w_ref, obs_ref, sems,
):
    copies = [
        pltpu.make_async_copy(count_hbm, count_ref, sems.at[0]),
        pltpu.make_async_copy(w_hbm.at[0], w_ref, sems.at[1]),
        pltpu.make_async_copy(obs_hbm.at[0], obs_ref, sems.at[2]),
        pltpu.make_async_copy(x_hbm, x_ref, sems.at[3]),
    ]
    for copy in copies:
        copy.start()
    for copy in copies[:3]:
        copy.wait()
    p, z_odd, _ = place_in_plane(span)
    slots = w_ref.shape[1]
    pack = functools.partial(
        pack_tile, w_ref=w_ref, obs_ref=obs_ref, count_ref=count_ref, slots=slots, channels=channels
    )
    for j in range(span):
        up = jnp.maximum(p - j, 0)
        down = jnp.minimum(2 * span + p - j, 2 * span)
        pack(jnp.where(z_odd == 1, down, up), za_ref.at[j])
        pack(jnp.where(z_odd == 1, up, down), zb_ref.at[j])
        if j == 0:
            pack(span, own_ref.at[0])
        else:
            pack(span + p - lax.bitwise_xor(p, j), own_ref.at[j])
    copies[3].wait()


def prepare_kernel(channels, height, x_ref, after_ref, xt_ref, ha_ref, hb_ref):
    for start, size in channel_groups(channels):
        n = size * height
        moved = jnp.dot(
            permutation(height, size, False),
            x_ref[start * height : start * height + n, :],
            preferred_element_type=F32,
        ).astype(BF16)
        for r in range(height):
            xt_ref[r * channels + start : r * channels + start + size, :] = (
                moved[r * size : (r + 1) * size, :]
            )
    edge_pair(xt_ref, ha_ref, hb_ref, height, channels)


def relay_kernel(span, after_ref, za_ref, zb_ref, own_ref, *outs):
    p, z_odd, _ = place_in_plane(span)
    for m in range(1, span):
        to = lax.bitwise_xor(p, m)
        below = jnp.where(to < p, 1, 0)
        outs[m - 1][0] = own_ref[m]

        @pl.when(below == z_odd)
        def _():
            outs[m - 1][1] = za_ref[to]

        @pl.when(below != z_odd)
        def _():
            outs[m - 1][1] = zb_ref[to]


def stack_forward(raw_ref, dst):
    taps, _, outs, ins = raw_ref.shape
    total = jnp.zeros(dst.shape, F32)
    for a in range(taps):
        block = raw_ref[a].reshape(taps * outs, ins)
        to = lax.broadcasted_iota(jnp.int32, (ins, taps * ins), 1)
        pick = jnp.where(to == lax.broadcasted_iota(jnp.int32, to.shape, 0) + a * ins, 1.0, 0.0)
        total += jnp.dot(block, pick.astype(BF16), preferred_element_type=F32)
    dst[...] = total.astype(BF16)


def stack_backward(raw_ref, dst, shifts):
    taps, _, outs, ins = raw_ref.shape
    n, width = taps * outs, dst.shape[1]
    src = lax.broadcasted_iota(jnp.int32, (n, width), 0)
    to = lax.broadcasted_iota(jnp.int32, (n, width), 1)
    for half, shift in enumerate(shifts):
        pick = jnp.where(src == to + shift * outs, 1.0, 0.0).astype(BF16)
        for b in range(taps):
            block = jnp.concatenate([raw_ref[taps - 1 - a, taps - 1 - b] for a in range(taps)], axis=0)
            start = (half * taps + b) * ins
            dst[start : start + ins, :] = lax.dot_general(
                block, pick, (((0,), (0,)), ((), ())), preferred_element_type=F32
            ).astype(BF16)


def join_taps(taps, channels):
    width = taps.shape[1]
    return (
        pltpu.roll(taps[0:channels], 1, 1)
        + taps[channels : 2 * channels]
        + pltpu.roll(taps[2 * channels : 3 * channels], width - 1, 1)
    )


def conv_row(w_ref, src_ref, index, channels):
    window = src_ref[rows(index, 3, channels), :]
    return join_taps(jnp.dot(w_ref[...], window, preferred_element_type=F32), channels)


def conv_pair(w_ref, window, channels):
    taps = jnp.dot(w_ref[...], window, preferred_element_type=F32)
    return join_taps(taps[: 3 * channels], channels), join_taps(taps[3 * channels :], channels)


def silu_and_slope(act, keep=None):
    gate = 0.5 * jnp.tanh(0.5 * act) + 0.5
    if keep is not None:
        gate = gate * keep
    hidden = act * gate
    return hidden.astype(BF16), gate * (1.0 + act - hidden)


def ext_edges(channels, height, mid_ref, a_ref, b_ref, top, bottom, odd):
    edge = HALO * channels
    top[edge : 2 * edge, :] = mid_ref[0:edge, :]
    bottom[0:edge, :] = mid_ref[(height - HALO) * channels : height * channels, :]

    @pl.when(odd == 1)
    def _():
        top[0:edge, :] = a_ref[...]
        bottom[edge : 2 * edge, :] = b_ref[...]

    @pl.when(odd == 0)
    def _():
        top[0:edge, :] = b_ref[...]
        bottom[edge : 2 * edge, :] = a_ref[...]


def forward_inner_kernel(
    channels, height,
    xt_ref, raw1_ref, raw2_ref,
    hid_ref, slope_ref, res_ref, w1_ref, w2_ref,
):
    stack_forward(raw1_ref, w1_ref)
    stack_forward(raw2_ref, w2_ref)
    for i in range(height - 2):
        act = conv_row(w1_ref, xt_ref, i, channels)
        hid_ref[rows(i, 1, channels), :], slope_ref[rows(i, 1, channels), :] = silu_and_slope(act)
    for i in range(height - 4):
        res_ref[rows(i, 1, channels), :] = conv_row(w2_ref, hid_ref, i, channels)


def on_grid():
    me = lax.axis_index("lat")
    count = lax.axis_size("lat")
    return jnp.where(me == 0, 0.0, 1.0), jnp.where(me == count - 1, 0.0, 1.0)


def forward_edge_kernel(
    channels, height,
    xt_ref, a_ref, b_ref, hid_ref, w1_ref, w2_ref, raw1_ref, raw2_ref,
    slope_ref, res_ref, w1t_ref, w2t_ref, above1_ref, above2_ref, below1_ref, below2_ref,
    top, bottom, hid_top, hid_bottom,
):
    odd = lax.axis_index("lat") % 2
    ext_edges(channels, height, xt_ref, a_ref, b_ref, top, bottom, odd)
    has_above, has_below = on_grid()
    inner = (height - 2 - HALO) * channels
    hid_top[2 * channels : 4 * channels, :] = hid_ref[0 : 2 * channels, :]
    hid_bottom[0 : 2 * channels, :] = hid_ref[inner : inner + 2 * channels, :]
    for i, keep in ((0, has_above), (1, None)):
        act = conv_row(w1_ref, top, i, channels)
        hid_top[rows(i, 1, channels), :], slope_ref[rows(i, 1, channels), :] = silu_and_slope(act, keep)
    for i, keep in ((0, None), (1, has_below)):
        act = conv_row(w1_ref, bottom, i, channels)
        hid_bottom[rows(2 + i, 1, channels), :], slope_ref[rows(2 + i, 1, channels), :] = (
            silu_and_slope(act, keep)
        )
    for i in range(2):
        res_ref[rows(i, 1, channels), :] = conv_row(w2_ref, hid_top, i, channels)
        res_ref[rows(2 + i, 1, channels), :] = conv_row(w2_ref, hid_bottom, i, channels)
    for raw_ref, full, above, below in (
        (raw1_ref, w1t_ref, above1_ref, below1_ref),
        (raw2_ref, w2t_ref, above2_ref, below2_ref),
    ):
        stack_backward(raw_ref, full, (0,))
        stack_backward(raw_ref, above, (0, -1))
        stack_backward(raw_ref, below, (2, 1))


def early_jobs(span, own_ref, za_ref, zb_ref, near_refs):
    p, z_odd, _ = place_in_plane(span)
    jobs = [
        (span, own_ref.at[0]),
        (jnp.where(z_odd == 1, 0, 2 * span), za_ref.at[p]),
        (jnp.where(z_odd == 1, 2 * span, 0), zb_ref.at[p]),
    ]
    return jobs + plane_jobs(span, range(1, 1 + len(near_refs)), near_refs)


def plane_jobs(span, partners, near_refs):
    p, _, _ = place_in_plane(span)
    jobs = []
    for m, ref in zip(partners, near_refs):
        step = lax.bitwise_xor(p, m) - p
        jobs.append((span + step, ref.at[0]))
        jobs.append((jnp.where(step > 0, step, 2 * span + step), ref.at[1]))
    return jobs


def tile_terms(jobs, route_ref, xt_ref, inner_ref, edge_ref, obs_weight, channels, height, columns):
    slots = BLK_LON
    across, down = columns // BLK_LON, height // BLK_LAT
    places, blocks = [], []
    for k, _ in jobs:
        n = route_ref[0, k]
        r, q = n // across, n % across
        inside = (r > 0) & (r < down - 1)
        lanes = pl.ds(pl.multiple_of(q * BLK_LON, BLK_LON), BLK_LON)
        block = []
        for i in range(BLK_LAT):
            row_in = jnp.clip(r * BLK_LAT + i - HALO, 0, height - 2 * HALO - 1)
            row_edge = jnp.where(r == 0, i, HALO + i)
            res = jnp.where(
                inside,
                inner_ref[rows(row_in, 1, channels), lanes],
                edge_ref[rows(row_edge, 1, channels), lanes],
            )
            here = (rows(r * BLK_LAT + i, 1, channels), lanes)
            block.append((xt_ref[here].astype(F32) + res).astype(BF16))
        places.append((r, lanes))
        blocks.append(block)
    misfits = []
    for (_, ref), block in zip(jobs, blocks):
        predicted = jnp.zeros((channels, slots), F32)
        for i in range(BLK_LAT):
            predicted += lax.dot_general(
                block[i],
                ref[i * slots : (i + 1) * slots, :],
                (((1,), (1,)), ((), ())),
                preferred_element_type=F32,
            )
        obs = ref[BLK_LAT * slots : BLK_LAT * slots + channels, :].astype(F32)
        misfits.append(((obs - predicted) * obs_weight).astype(BF16))
    terms = [
        [
            jnp.dot(misfit, ref[i * slots : (i + 1) * slots, :], preferred_element_type=F32).astype(BF16)
            for i in range(BLK_LAT)
        ]
        for (_, ref), misfit in zip(jobs, misfits)
    ]
    return places, terms


def early_tile_kernel(
    channels, height, columns, span,
    route_hbm, xt_ref, inner_ref, edge_ref, ow_ref, own_ref, za_ref, zb_ref, near_ref,
    guide_ref,
    route_ref, sem,
):
    copy = pltpu.make_async_copy(route_hbm, route_ref, sem)
    copy.start()
    guide_ref[...] = jnp.zeros_like(guide_ref)
    copy.wait()
    jobs = early_jobs(span, own_ref, za_ref, zb_ref, [near_ref])
    places, terms = tile_terms(
        jobs, route_ref, xt_ref, inner_ref, edge_ref, as_column(ow_ref[...]), channels, height, columns
    )
    for (r, lanes), term in zip(places, terms):
        for i in range(BLK_LAT):
            guide_ref[rows(r * BLK_LAT + i, 1, channels), lanes] += term[i].astype(F32)


def late_tile_kernel(
    channels, height, columns, span,
    route_ref, xt_ref, inner_ref, edge_ref, ow_ref, guide_ref, *refs,
):
    near_refs, (late_ref, ga_ref, gb_ref, sums, low) = refs[: span - 2], refs[span - 2 :]
    edge = HALO * channels
    last = (height - HALO) * channels
    sums[0:edge, :] = guide_ref[0:edge, :]
    sums[edge : 2 * edge, :] = guide_ref[last : last + edge, :]
    jobs = plane_jobs(span, range(2, span), near_refs)
    places, terms = tile_terms(
        jobs, route_ref, xt_ref, inner_ref, edge_ref, as_column(ow_ref[...]), channels, height, columns
    )
    down = height // BLK_LAT
    for index, ((r, lanes), term) in enumerate(zip(places, terms)):
        part = jnp.where(r == 0, 0, jnp.where(r == down - 1, 1, 2))
        for i in range(BLK_LAT):
            late_ref[index, i] = term[i]
            sums[rows(part * HALO + i, 1, channels), lanes] += term[i].astype(F32)
    low[...] = sums[0 : 2 * edge, :].astype(BF16)
    edge_pair(low, ga_ref, gb_ref, 2 * HALO, channels)


def backward_inner_kernel(
    channels, height, columns, span,
    route_ref, early_ref, late_ref, slope_ref, inner_ref, edge_ref, prior_ref, w2_ref, w1_ref,
    part_adj_ref, part_score_ref, score_ref,
    guide, low, adj,
):
    guide[...] = early_ref[...]
    across = columns // BLK_LON
    jobs = plane_jobs(span, range(2, span), [late_ref] * (span - 2))
    for index, (k, _) in enumerate(jobs):
        n = route_ref[0, k]
        lanes = pl.ds(pl.multiple_of((n % across) * BLK_LON, BLK_LON), BLK_LON)
        for i in range(BLK_LAT):
            here = (rows((n // across) * BLK_LAT + i, 1, channels), lanes)
            guide[here] += late_ref[index, i].astype(F32)
    edge = HALO * channels
    none = jnp.zeros((edge, columns), BF16)
    low[0:edge, :] = none
    low[edge : edge + height * channels, :] = guide[...].astype(BF16)
    low[edge + height * channels :, :] = none
    adj[0:edge, :] = none
    adj[height * channels :, :] = none
    for i in range(height + 2):
        part = conv_row(w2_ref, low, i, channels)
        if HALO <= i < height:
            adj[rows(i, 1, channels), :] = (slope_ref[rows(i - HALO, 1, channels), :] * part).astype(BF16)
        else:
            part_adj_ref[rows(i if i < HALO else i - height + HALO, 1, channels), :] = part
    prior = as_column(prior_ref[...])
    for i in range(height):
        part = conv_row(w1_ref, adj, i, channels) + guide[rows(i, 1, channels), :]
        if HALO <= i < height - HALO:
            here = rows(i - HALO, 1, channels)
            score_ref[here, :] = (prior * inner_ref[here, :] + part).astype(BF16)
        else:
            here = rows(i if i < HALO else i - height + 2 * HALO, 1, channels)
            part_score_ref[here, :] = prior * edge_ref[here, :] + part


def backward_edge_kernel(
    channels, height,
    a_ref, b_ref, slope_ref, part_adj_ref, part_score_ref, score_ref,
    above2_ref, below2_ref, above1_ref, below1_ref,
    out_hbm,
    out_ref, edge_ref, sems,
):
    odd = lax.axis_index("lat") % 2
    first, second = a_ref[...], b_ref[...]
    for at, window, w2_ref, w1_ref in (
        (0, jnp.where(odd == 1, first, second), above2_ref, above1_ref),
        (HALO, jnp.where(odd == 1, second, first), below2_ref, below1_ref),
    ):
        here = [rows(at + i, 1, channels) for i in range(HALO)]
        adj = [
            (slope_ref[place, :] * (part_adj_ref[place, :] + back)).astype(BF16)
            for place, back in zip(here, conv_pair(w2_ref, window, channels))
        ]
        for place, back in zip(here, conv_pair(w1_ref, jnp.concatenate(adj, axis=0), channels)):
            edge_ref[place, :] = (part_score_ref[place, :] + back).astype(BF16)
    copies = []
    for start, size in channel_groups(channels):
        n = size * height
        picked = []
        for r in range(height):
            if r < HALO:
                src, at = edge_ref, r
            elif r < height - HALO:
                src, at = score_ref, r - HALO
            else:
                src, at = edge_ref, r - height + 2 * HALO
            picked.append(src[at * channels + start : at * channels + start + size, :])
        part = pl.ds(start * height, n)
        out_ref[part, :] = jnp.dot(
            permutation(height, size, True), jnp.concatenate(picked, axis=0), preferred_element_type=F32
        ).astype(BF16)
        copies.append(pltpu.make_async_copy(out_ref.at[part], out_hbm.at[part], sems.at[len(copies)]))
        copies[-1].start()
    for copy in copies:
        copy.wait()


def pairs(groups, count, partner):
    found = []
    for g in range(groups):
        for i in range(count):
            other = partner(i)
            if 0 <= other < count:
                found.append((g * count + i, g * count + other))
            elif groups % 2 == 0:
                found.append((g * count + i, (g ^ 1) * count + i))
    return found


def local(
    noisy_state, w_first, w_second, prior_weight, obs_weight, block_route, counts, tile_weights, observations
):
    channels, height, columns = noisy_state.shape
    tile_total = block_route.shape[1]
    span = tile_total // 2
    slots = tile_weights.shape[2]
    count = lax.axis_size("lat")
    pack_rows = BLK_LAT * slots + channels
    taps = w_first.shape[0]

    def field(n, dtype=BF16):
        return shape((n * channels, columns), dtype)

    def buffer(n, dtype=BF16):
        return pltpu.VMEM((n * channels, columns), dtype)

    def exchange(x, partner):
        return lax.ppermute(x, ("grp", "lat"), pairs(lax.axis_size("grp"), count, partner))

    def swap(x, step, parity):
        return exchange(x, lambda i: i + step if (i // step) % 2 == parity else i - step)

    packed = shape((span, pack_rows, BLK_LON))
    def in_hbm(x):
        return pltpu.with_memory_space_constraint(x, pltpu.HBM)

    za_send, zb_send, own, x = pl.pallas_call(
        functools.partial(pack_kernel, channels, span),
        out_shape=(packed, packed, packed, field(height)),
        in_specs=[HB] * 4,
        out_specs=[VM] * 4,
        scratch_shapes=[
            pltpu.SMEM(counts.shape, jnp.int32),
            pltpu.VMEM(tile_weights.shape[1:], BF16),
            pltpu.VMEM(observations.shape[1:], BF16),
            pltpu.SemaphoreType.DMA((4,)),
        ],
        compiler_params=params(),
    )(
        in_hbm(counts),
        in_hbm(tile_weights),
        in_hbm(observations),
        in_hbm(noisy_state.reshape(channels * height, columns)),
    )
    za, zb = swap(za_send, span, 0), swap(zb_send, span, 1)
    xt, ha, hb = pl.pallas_call(
        functools.partial(prepare_kernel, channels, height),
        out_shape=(field(height), field(HALO), field(HALO)),
        in_specs=[VM, AN],
        out_specs=[VM] * 3,
        compiler_params=params(),
    )(x, za_send)
    ha, hb = swap(ha, 1, 0), swap(hb, 1, 1)

    weight = shape((taps * channels, taps * channels))
    pair_weight = shape((HALO * taps * channels, HALO * channels))
    hid, slope_in, res_in, w1, w2 = pl.pallas_call(
        functools.partial(forward_inner_kernel, channels, height),
        out_shape=(field(height - 2), field(height - 2, F32), field(height - 4, F32), weight, weight),
        in_specs=[VM] * 3,
        out_specs=[VM] * 5,
        compiler_params=params(),
    )(xt, w_first, w_second)

    relayed = pl.pallas_call(
        functools.partial(relay_kernel, span),
        out_shape=tuple(shape((2, pack_rows, BLK_LON)) for _ in range(span - 1)),
        in_specs=[AN] + [VM] * 3,
        out_specs=[VM] * (span - 1),
        compiler_params=params(),
    )(w1, za, zb, own)
    arrived = [exchange(relayed[m - 1], lambda i, m=m: i ^ m) for m in range(1, span)]

    slope_ed, res_ed, w1t, w2t, above1, above2, below1, below2 = pl.pallas_call(
        functools.partial(forward_edge_kernel, channels, height),
        out_shape=(field(2 * HALO, F32), field(2 * HALO, F32), weight, weight) + (pair_weight,) * 4,
        in_specs=[VM] * 8,
        out_specs=[VM] * 8,
        scratch_shapes=[buffer(2 * HALO)] * 4,
        compiler_params=params(),
    )(xt, ha, hb, hid, w1, w2, w_first, w_second)

    observed = obs_weight[None, :]
    early = pl.pallas_call(
        functools.partial(early_tile_kernel, channels, height, columns, span),
        out_shape=field(height, F32),
        in_specs=[HB] + [VM] * 8,
        out_specs=VM,
        scratch_shapes=[pltpu.SMEM(block_route.shape, jnp.int32), pltpu.SemaphoreType.DMA],
        compiler_params=params(),
    )(in_hbm(block_route), xt, res_in, res_ed, observed, own, za, zb, arrived[0])

    late, ga, gb = pl.pallas_call(
        functools.partial(late_tile_kernel, channels, height, columns, span),
        out_shape=(
            shape((2 * (span - 2), BLK_LAT, channels, BLK_LON)),
            field(HALO),
            field(HALO),
        ),
        in_specs=[SM] + [VM] * (5 + span - 2),
        out_specs=[VM] * 3,
        scratch_shapes=[buffer(3 * HALO, F32), buffer(2 * HALO)],
        compiler_params=params(),
    )(block_route, xt, res_in, res_ed, observed, early, *arrived[1:])
    ga, gb = swap(ga, 1, 0), swap(gb, 1, 1)

    part_adj, part_score, score = pl.pallas_call(
        functools.partial(backward_inner_kernel, channels, height, columns, span),
        out_shape=(field(2 * HALO, F32), field(2 * HALO, F32), field(height - 2 * HALO)),
        in_specs=[SM] + [VM] * 8,
        out_specs=[VM] * 3,
        scratch_shapes=[buffer(height, F32), buffer(height + 2 * HALO), buffer(height + 2)],
        compiler_params=params(),
    )(block_route, early, late, slope_in, res_in, res_ed, prior_weight[None, :], w2t, w1t)

    out = pl.pallas_call(
        functools.partial(backward_edge_kernel, channels, height),
        out_shape=shape((channels * height, columns)),
        in_specs=[VM] * 10,
        out_specs=HB,
        scratch_shapes=[
            buffer(height),
            buffer(2 * HALO),
            pltpu.SemaphoreType.DMA((len(channel_groups(channels)),)),
        ],
        compiler_params=params(),
    )(ga, gb, slope_ed, part_adj, part_score, score, above2, below2, above1, below1)
    return out.reshape(channels, height, columns)


def solution(mesh):
    in_specs = (
        P("grp", "lat", None),
        P(),
        P(),
        P(),
        P(),
        P(("grp", "lat"), None),
        P(("grp", "lat"), None),
        P(("grp", "lat"), None, None, None),
        P(("grp", "lat"), None, None, None),
    )
    out_specs = P("grp", "lat", None)
    return jax.shard_map(local, mesh=mesh, in_specs=in_specs, out_specs=out_specs, check_vma=False)
```

time: 41.9 us -> 39.9 us (0.952)
  the two profiles are of different devices: /device:TPU:17 before, /device:TPU:11 now
where the time goes in v4:
time: 39.9 us; the launch traced here: 39.8 us
  Pallas kernels  17.7 us (44%)
  waiting for transfers between devices  11.6 us (29%)
  starting transfers between devices  10.2 us (26%)
    ppermute x9, waiting for transfers between devices, exchange(): lax.ppermute(x, ('grp', 'lat'), pairs(lax.axis_size('grp'), count, partner))  11.6 us
    ppermute x9, starting transfers between devices, exchange(): lax.ppermute(x, ('grp', 'lat'), pairs(lax.axis_size('grp'), count, partner))  10.2 us
    pallas_call x1, Pallas kernels, local(): pl.pallas_call(functools.partial(backward_inner_kernel, channels, height,...  4.63 us
    pallas_call x1, Pallas kernels, local(): pl.pallas_call(functools.partial(backward_edge_kernel, channels, height),...  3.15 us
    pallas_call x1, Pallas kernels, local(): pl.pallas_call(functools.partial(forward_edge_kernel, channels, height),...  2.48 us
    pallas_call x1, Pallas kernels, local(): pl.pallas_call(functools.partial(forward_inner_kernel, channels, height),...  2.47 us
    pallas_call x1, Pallas kernels, local(): pl.pallas_call(functools.partial(pack_kernel, channels, span), out_shape=...  1.59 us
    pallas_call x1, Pallas kernels, local(): pl.pallas_call(functools.partial(early_tile_kernel, channels, height, col...  1.37 us
  transfers between devices with their start and end apart: 9, of which 5 were waited for; matrix products, arithmetic and copies ran while one was open for 0% of the time, Pallas kernels for 29%

profile of v4, /device:TPU:11, one launch (start us, length us, event | category | flops | bytes accessed | tf_op | source)
XLA Modules:
  0.0 39.8 jit_solution(11995211766503971446)
XLA Ops:
  0.0 1.6 %shard_map.91 = (bf16[4,336,128]{2,1,0:T(8,128)(2,1)S(1)}, bf16[4,336,128]{2,1,0:T(8,128)(2,1)S(1)}, bf16[4,336,128]{2,1,0:T(8,128)(2,1)S(1)}, bf16[640,1024]{1,0:T(8,128)(2,1)S(1)}) custom-call(s32[1,9]{1,0:T(1,128)} %count_hbm.1, bf16[1,9,128,256]{3,2,1,0:T(8,128)(2,1)} %w_hbm.1, bf16[1,9,80,128]{3,2,1,0:T(8,128)(2,1)} %obs_hbm.1, bf16[640,1024]{1,0:T(8,128)(2,1)} %bitcast.7), custom_call_target="tpu_custom_call" | custom-call | tf_op jit(solution)/shard_map/pallas_call | solution.py:498
  1.6 0.0 copy-start
  1.6 0.0 copy-start.1
  1.6 1.4 %collective-permute-start.3 = (bf16[4,336,128]{2,1,0:T(8,128)(2,1)S(1)}, bf16[4,336,128]{2,1,0:T(8,128)(2,1)S(1)}, u32[]{:S(2)}, u32[]{:S(2)}) collective-permute-start(bf16[4,336,128]{2,1,0:T(8,128)(2,1)S(1)} %get-tuple-element.45), channel_id=1, source_target_pairs={{0,16},{1,17},{2,18},{3,19},{4,8},{5,9},{6,10},{7,11},{8,4},{9,5},... | collective-permute-start | bytes 1032200 | tf_op jit(solution)/shard_map/ppermute | solution.py:489
  3.0 0.0 collective-permute-start.2
  3.0 0.6 %shard_map.92 = (bf16[640,1024]{1,0:T(8,128)(2,1)S(1)}, bf16[160,1024]{1,0:T(8,128)(2,1)S(1)}, bf16[160,1024]{1,0:T(8,128)(2,1)S(1)}) custom-call(bf16[640,1024]{1,0:T(8,128)(2,1)S(1)} %get-tuple-element.34.x_ref, bf16[4,336,128]{2,1,0:T(8,128)(2,1)S(1)} %get-tuple-element.35.after_ref), custom_call_target="tpu_custom_call" | custom-call | tf_op jit(solution)/shard_map/pallas_call | solution.py:517
  3.6 1.0 %collective-permute-start = (bf16[160,1024]{1,0:T(8,128)(2,1)S(1)}, bf16[160,1024]{1,0:T(8,128)(2,1)S(1)}, u32[]{:S(2)}, u32[]{:S(2)}) collective-permute-start(bf16[160,1024]{1,0:T(8,128)(2,1)S(1)} %get-tuple-element.38), channel_id=1, source_target_pairs={{0,1},{1,0},{2,3},{3,2},{4,5},{5,4},{6,7},{7,6},{8,9},{9,8},{10,11... | collective-permute-start | bytes 983048 | tf_op jit(solution)/shard_map/ppermute | solution.py:489
  4.6 1.2 %collective-permute-start.1 = (bf16[160,1024]{1,0:T(8,128)(2,1)S(1)}, bf16[160,1024]{1,0:T(8,128)(2,1)S(1)}, u32[]{:S(2)}, u32[]{:S(2)}) collective-permute-start(bf16[160,1024]{1,0:T(8,128)(2,1)S(1)} %get-tuple-element.39), channel_id=1, source_target_pairs={{0,16},{1,2},{2,1},{3,4},{4,3},{5,6},{6,5},{7,8},{8,7},{9,10},{10,... | collective-permute-start | bytes 983048 | tf_op jit(solution)/shard_map/ppermute | solution.py:489
  5.8 0.0 copy-done
  5.8 0.0 copy-done.1
  5.8 2.5 %shard_map.93 = (bf16[480,1024]{1,0:T(8,128)(2,1)S(1)}, f32[480,1024]{1,0:T(8,128)S(1)}, f32[320,1024]{1,0:T(8,128)S(1)}, bf16[240,240]{1,0:T(8,128)(2,1)S(1)}, bf16[240,240]{1,0:T(8,128)(2,1)S(1)}) custom-call(bf16[640,1024]{1,0:T(8,128)(2,1)S(1)} %get-tuple-element.36.xt_ref, bf16[3,3,80,80]{3,2,1,0:T(8,128)(2,1)S(1)} %copy-done, ...), custom_call_target="tpu_custom_call" | custom-call | tf_op jit(solution)/shard_map/pallas_call | solution.py:528
  8.3 2.3 %collective-permute-done.3.zb_ref = bf16[4,336,128]{2,1,0:T(8,128)(2,1)S(1)} collective-permute-done((bf16[4,336,128]{2,1,0:T(8,128)(2,1)S(1)}, bf16[4,336,128]{2,1,0:T(8,128)(2,1)S(1)}, u32[]{:S(2)}, u32[]{:S(2)}) %collective-permute-start.3) | collective-permute-done | bytes 344096 | tf_op jit(solution)/shard_map/ppermute | solution.py:489
  10.6 1.0 %collective-permute-done.2.za_ref = bf16[4,336,128]{2,1,0:T(8,128)(2,1)S(1)} collective-permute-done((bf16[4,336,128]{2,1,0:T(8,128)(2,1)S(1)}, bf16[4,336,128]{2,1,0:T(8,128)(2,1)S(1)}, u32[]{:S(2)}, u32[]{:S(2)}) %collective-permute-start.2) | collective-permute-done | bytes 344096 | tf_op jit(solution)/shard_map/ppermute | solution.py:489
  11.7 1.9 %collective-permute-start.4 = (bf16[2,336,128]{2,1,0:T(8,128)(2,1)S(1)}, bf16[2,336,128]{2,1,0:T(8,128)(2,1)S(1)}, u32[]{:S(2)}, u32[]{:S(2)}) collective-permute-start(bf16[2,336,128]{2,1,0:T(8,128)(2,1)S(1)} %get-tuple-element.46), channel_id=1, source_target_pairs={{0,1},{1,0},{2,3},{3,2},{4,5},{5,4},{6,7},{7,6},{8,9},{9,8},{10,11... | collective-permute-start | bytes 516104 | tf_op jit(solution)/shard_map/ppermute | solution.py:489
  13.6 2.7 %collective-permute-start.5 = (bf16[2,336,128]{2,1,0:T(8,128)(2,1)S(1)}, bf16[2,336,128]{2,1,0:T(8,128)(2,1)S(1)}, u32[]{:S(2)}, u32[]{:S(2)}) collective-permute-start(bf16[2,336,128]{2,1,0:T(8,128)(2,1)S(1)} %get-tuple-element.47), channel_id=1, source_target_pairs={{0,2},{1,3},{2,0},{3,1},{4,6},{5,7},{6,4},{7,5},{8,10},{9,11},{10,... | collective-permute-start | bytes 516104 | tf_op jit(solution)/shard_map/ppermute | solution.py:489
  16.3 0.0 collective-permute-start.6
  16.3 0.0 collective-permute-done.a_ref
  16.3 0.0 collective-permute-done.1.b_ref
  16.4 0.0 copy-start.3
  16.4 2.5 %shard_map.94 = (f32[320,1024]{1,0:T(8,128)S(1)}, f32[320,1024]{1,0:T(8,128)S(1)}, bf16[240,240]{1,0:T(8,128)(2,1)S(1)}, bf16[240,240]{1,0:T(8,128)(2,1)S(1)}, b...) custom-call(bf16[640,1024]{1,0:T(8,128)(2,1)S(1)} %get-tuple-element, ...), custom_call_target="tpu_custom_call" | custom-call | tf_op jit(solution)/shard_map/pallas_call | solution.py:545
  18.8 0.0 collective-permute-done.4.near_ref
  18.9 0.0 copy-done.3
  18.9 0.0 copy-start.2
  18.9 1.4 %shard_map.96.guide_ref.early_ref = f32[640,1024]{1,0:T(8,128)S(1)} custom-call(s32[1,9]{1,0:T(1,128)} %route_ref.3, bf16[640,1024]{1,0:T(8,128)(2,1)S(1)} %get-tuple-element.36.xt_ref, f32[320,1024]{1,0:T(8,128)S(1)} %get-tuple-element.37.inner_ref, f32[320,1024]{1,0:T(8,128)S(1)} %get-tuple-element.43.edge_ref, f32[1,80]{1,0:T(1,128)S(1)} %bitcast.4, ...), custom_call_target="tpu_custom_call" | custom-call | tf_op jit(solution)/shard_map/pallas_call | solution.py:555
  20.3 0.0 copy-start.4
  20.3 0.7 %collective-permute-done.5.refs_0_ = bf16[2,336,128]{2,1,0:T(8,128)(2,1)S(1)} collective-permute-done((bf16[2,336,128]{2,1,0:T(8,128)(2,1)S(1)}, bf16[2,336,128]{2,1,0:T(8,128)(2,1)S(1)}, u32[]{:S(2)}, u32[]{:S(2)}) %collective-permute-start.5) | collective-permute-done | bytes 172064 | tf_op jit(solution)/shard_map/ppermute | solution.py:489
  21.0 3.7 %collective-permute-done.6.refs_1_ = bf16[2,336,128]{2,1,0:T(8,128)(2,1)S(1)} collective-permute-done((bf16[2,336,128]{2,1,0:T(8,128)(2,1)S(1)}, bf16[2,336,128]{2,1,0:T(8,128)(2,1)S(1)}, u32[]{:S(2)}, u32[]{:S(2)}) %collective-permute-start.6) | collective-permute-done | bytes 172064 | tf_op jit(solution)/shard_map/ppermute | solution.py:489
  24.7 0.0 copy-done.2
  24.7 1.3 %shard_map.97 = (bf16[4,2,80,128]{3,2,1,0:T(8,128)(2,1)S(1)}, bf16[160,1024]{1,0:T(8,128)(2,1)S(1)}, bf16[160,1024]{1,0:T(8,128)(2,1)S(1)}) custom-call(s32[1,9]{1,0:T(1,128)S(1)} %copy-done.2, bf16[640,1024]{1,0:T(8,128)(2,1)S(1)} %get-tuple-element.36.xt_ref, f32[320,1024]{1,0:T(8,128)S(1)} %get-tuple-element.37.inner_ref, ...), custom_call_target="tpu_custom_call" | custom-call | tf_op jit(solution)/shard_map/pallas_call | solution.py:564
  26.0 0.5 %collective-permute-start.7 = (bf16[160,1024]{1,0:T(8,128)(2,1)S(1)}, bf16[160,1024]{1,0:T(8,128)(2,1)S(1)}, u32[]{:S(2)}, u32[]{:S(2)}) collective-permute-start(bf16[160,1024]{1,0:T(8,128)(2,1)S(1)} %get-tuple-element.49), channel_id=1, source_target_pairs={{0,1},{1,0},{2,3},{3,2},{4,5},{5,4},{6,7},{7,6},{8,9},{9,8},{10,11... | collective-permute-start | bytes 983048 | tf_op jit(solution)/shard_map/ppermute | solution.py:489
  26.5 1.4 %collective-permute-start.8 = (bf16[160,1024]{1,0:T(8,128)(2,1)S(1)}, bf16[160,1024]{1,0:T(8,128)(2,1)S(1)}, u32[]{:S(2)}, u32[]{:S(2)}) collective-permute-start(bf16[160,1024]{1,0:T(8,128)(2,1)S(1)} %get-tuple-element.50), channel_id=1, source_target_pairs={{0,16},{1,2},{2,1},{3,4},{4,3},{5,6},{6,5},{7,8},{8,7},{9,10},{10,... | collective-permute-start | bytes 983048 | tf_op jit(solution)/shard_map/ppermute | solution.py:489
  27.9 0.0 copy-done.4
  27.9 4.6 %shard_map.98 = (f32[320,1024]{1,0:T(8,128)S(1)}, f32[320,1024]{1,0:T(8,128)S(1)}, bf16[320,1024]{1,0:T(8,128)(2,1)S(1)}) custom-call(s32[1,9]{1,0:T(1,128)S(1)} %copy-done.2, f32[640,1024]{1,0:T(8,128)S(1)} %shard_map.96.guide_ref.early_ref, bf16[4,2,80,128]{3,2,1,0:T(8,128)(2,1)S(1)} %get-tuple-element.52.late_ref, ...), custom_call_target="tpu_custom_call" | custom-call | tf_op jit(solution)/shard_map/pallas_call | solution.py:578
  32.5 0.0 collective-permute-done.7.a_ref
  32.5 3.9 %collective-permute-done.8.b_ref = bf16[160,1024]{1,0:T(8,128)(2,1)S(1)} collective-permute-done((bf16[160,1024]{1,0:T(8,128)(2,1)S(1)}, bf16[160,1024]{1,0:T(8,128)(2,1)S(1)}, u32[]{:S(2)}, u32[]{:S(2)}) %collective-permute-start.8) | collective-permute-done | bytes 327712 | tf_op jit(solution)/shard_map/ppermute | solution.py:489
  36.5 3.2 %shard_map.99 = bf16[640,1024]{1,0:T(8,128)(2,1)} custom-call(bf16[160,1024]{1,0:T(8,128)(2,1)S(1)} %collective-permute-done.7.a_ref, bf16[160,1024]{1,0:T(8,128)(2,1)S(1)} %collective-permute-done.8.b_ref, f32[320,1024]{1,0:T(8,128)S(1)} %get-tuple-element.51.slope_ref, f32[320,1024]{1,0:T(8,128)S(1)} %get-tuple-element.56.part_adj_ref, ...), custom_call_target="tpu_custom_call" | custom-call | tf_op jit(solution)/shard_map/pallas_call | solution.py:587
  (1 shorter events, 0.0 us)
Async XLA Ops:
  1.6 4.2 %copy-start = (bf16[3,3,80,80]{3,2,1,0:T(8,128)(2,1)S(1)}, bf16[3,3,80,80]{3,2,1,0:T(8,128)(2,1)}, u32[]{:S(2)}) copy-start(bf16[3,3,80,80]{3,2,1,0:T(8,128)(2,1)} %raw1_ref.3) | copy-start | bytes 345604
  1.6 4.2 %copy-start.1 = (bf16[3,3,80,80]{3,2,1,0:T(8,128)(2,1)S(1)}, bf16[3,3,80,80]{3,2,1,0:T(8,128)(2,1)}, u32[]{:S(2)}) copy-start(bf16[3,3,80,80]{3,2,1,0:T(8,128)(2,1)} %raw2_ref.3) | copy-start | bytes 345604
  1.6 9.0 %collective-permute-start.3 = (bf16[4,336,128]{2,1,0:T(8,128)(2,1)S(1)}, bf16[4,336,128]{2,1,0:T(8,128)(2,1)S(1)}, u32[]{:S(2)}, u32[]{:S(2)}) collective-permute-start(bf16[4,336,128]{2,1,0:T(8,128)(2,1)S(1)} %get-tuple-element.45), channel_id=1, source_target_pairs={{0,16},{1,17},{2,18},{3,19},{4,8},{5,9},{6,10},{7,11},{8,4},{9,5},... | collective-permute-start | bytes 1032200 | tf_op jit(solution)/shard_map/ppermute | solution.py:489
  3.0 8.6 %collective-permute-start.2 = (bf16[4,336,128]{2,1,0:T(8,128)(2,1)S(1)}, bf16[4,336,128]{2,1,0:T(8,128)(2,1)S(1)}, u32[]{:S(2)}, u32[]{:S(2)}) collective-permute-start(bf16[4,336,128]{2,1,0:T(8,128)(2,1)S(1)} %get-tuple-element.35.after_ref), channel_id=1, source_target_pairs={{0,4},{1,5},{2,6},{3,7},{4,0},{5,1},{6,2},{7,3},{8,12},{9,13},{10,... | collective-permute-start | bytes 1032200 | tf_op jit(solution)/shard_map/ppermute | solution.py:489
  3.6 12.8 %collective-permute-start = (bf16[160,1024]{1,0:T(8,128)(2,1)S(1)}, bf16[160,1024]{1,0:T(8,128)(2,1)S(1)}, u32[]{:S(2)}, u32[]{:S(2)}) collective-permute-start(bf16[160,1024]{1,0:T(8,128)(2,1)S(1)} %get-tuple-element.38), channel_id=1, source_target_pairs={{0,1},{1,0},{2,3},{3,2},{4,5},{5,4},{6,7},{7,6},{8,9},{9,8},{10,11... | collective-permute-start | bytes 983048 | tf_op jit(solution)/shard_map/ppermute | solution.py:489
  4.6 11.7 %collective-permute-start.1 = (bf16[160,1024]{1,0:T(8,128)(2,1)S(1)}, bf16[160,1024]{1,0:T(8,128)(2,1)S(1)}, u32[]{:S(2)}, u32[]{:S(2)}) collective-permute-start(bf16[160,1024]{1,0:T(8,128)(2,1)S(1)} %get-tuple-element.39), channel_id=1, source_target_pairs={{0,16},{1,2},{2,1},{3,4},{4,3},{5,6},{6,5},{7,8},{8,7},{9,10},{10,... | collective-permute-start | bytes 983048 | tf_op jit(solution)/shard_map/ppermute | solution.py:489
  11.7 7.2 %collective-permute-start.4 = (bf16[2,336,128]{2,1,0:T(8,128)(2,1)S(1)}, bf16[2,336,128]{2,1,0:T(8,128)(2,1)S(1)}, u32[]{:S(2)}, u32[]{:S(2)}) collective-permute-start(bf16[2,336,128]{2,1,0:T(8,128)(2,1)S(1)} %get-tuple-element.46), channel_id=1, source_target_pairs={{0,1},{1,0},{2,3},{3,2},{4,5},{5,4},{6,7},{7,6},{8,9},{9,8},{10,11... | collective-permute-start | bytes 516104 | tf_op jit(solution)/shard_map/ppermute | solution.py:489
  13.6 7.4 %collective-permute-start.5 = (bf16[2,336,128]{2,1,0:T(8,128)(2,1)S(1)}, bf16[2,336,128]{2,1,0:T(8,128)(2,1)S(1)}, u32[]{:S(2)}, u32[]{:S(2)}) collective-permute-start(bf16[2,336,128]{2,1,0:T(8,128)(2,1)S(1)} %get-tuple-element.47), channel_id=1, source_target_pairs={{0,2},{1,3},{2,0},{3,1},{4,6},{5,7},{6,4},{7,5},{8,10},{9,11},{10,... | collective-permute-start | bytes 516104 | tf_op jit(solution)/shard_map/ppermute | solution.py:489
  16.3 8.4 %collective-permute-start.6 = (bf16[2,336,128]{2,1,0:T(8,128)(2,1)S(1)}, bf16[2,336,128]{2,1,0:T(8,128)(2,1)S(1)}, u32[]{:S(2)}, u32[]{:S(2)}) collective-permute-start(bf16[2,336,128]{2,1,0:T(8,128)(2,1)S(1)} %get-tuple-element.48), channel_id=1, source_target_pairs={{0,3},{1,2},{2,1},{3,0},{4,7},{5,6},{6,5},{7,4},{8,11},{9,10},{10,... | collective-permute-start | bytes 516104 | tf_op jit(solution)/shard_map/ppermute | solution.py:489
  16.4 2.5 %copy-start.3 = (f32[80]{0:T(128)S(1)}, f32[80]{0:T(128)}, u32[]{:S(2)}) copy-start(f32[80]{0:T(128)} %param.13) | copy-start | bytes 964
  18.9 5.8 %copy-start.2 = (s32[1,9]{1,0:T(1,128)S(1)}, s32[1,9]{1,0:T(1,128)}, u32[]{:S(2)}) copy-start(s32[1,9]{1,0:T(1,128)} %route_ref.3) | copy-start | bytes 112
  20.3 7.6 %copy-start.4 = (f32[80]{0:T(128)S(1)}, f32[80]{0:T(128)}, u32[]{:S(2)}) copy-start(f32[80]{0:T(128)} %param.12) | copy-start | bytes 964
  26.0 6.5 %collective-permute-start.7 = (bf16[160,1024]{1,0:T(8,128)(2,1)S(1)}, bf16[160,1024]{1,0:T(8,128)(2,1)S(1)}, u32[]{:S(2)}, u32[]{:S(2)}) collective-permute-start(bf16[160,1024]{1,0:T(8,128)(2,1)S(1)} %get-tuple-element.49), channel_id=1, source_target_pairs={{0,1},{1,0},{2,3},{3,2},{4,5},{5,4},{6,7},{7,6},{8,9},{9,8},{10,11... | collective-permute-start | bytes 983048 | tf_op jit(solution)/shard_map/ppermute | solution.py:489
  26.5 10.0 %collective-permute-start.8 = (bf16[160,1024]{1,0:T(8,128)(2,1)S(1)}, bf16[160,1024]{1,0:T(8,128)(2,1)S(1)}, u32[]{:S(2)}, u32[]{:S(2)}) collective-permute-start(bf16[160,1024]{1,0:T(8,128)(2,1)S(1)} %get-tuple-element.50), channel_id=1, source_target_pairs={{0,16},{1,2},{2,1},{3,4},{4,3},{5,6},{6,5},{7,8},{8,7},{9,10},{10,... | collective-permute-start | bytes 983048 | tf_op jit(solution)/shard_map/ppermute | solution.py:489

commit v5 on v4

--- a/solution.py
+++ b/solution.py
@@ -69,25 +69,28 @@
     dst[BLK_LAT * slots : BLK_LAT * slots + channels, :] = obs_ref[k]
 
 
-def edge_pair(src_ref, ha_ref, hb_ref, height, channels):
+def first_rows(src_ref, dst, height, channels):
+    odd = lax.axis_index("lat") % 2
+    dst[...] = src_ref[rows((height - HALO) * (1 - odd), HALO, channels), :]
+
+
+def second_rows(src_ref, dst, height, channels):
     me, odd = lax.axis_index("lat"), lax.axis_index("lat") % 2
-    last = height - HALO
-    ha_ref[...] = src_ref[rows(last * (1 - odd), HALO, channels), :]
     alone = (me == 0) | (me == lax.axis_size("lat") - 1)
 
     @pl.when(alone)
     def _():
-        hb_ref[...] = jnp.zeros_like(hb_ref)
+        dst[...] = jnp.zeros_like(dst)
 
     @pl.when(jnp.logical_not(alone))
     def _():
-        hb_ref[...] = src_ref[rows(last * odd, HALO, channels), :]
+        dst[...] = src_ref[rows((height - HALO) * odd, HALO, channels), :]
 
 
 def pack_kernel(
     channels, span,
     count_hbm, w_hbm, obs_hbm, x_hbm,
-    za_ref, zb_ref, own_ref, x_ref,
+    za_ref, zb_ref, own_ref, near_ref, y2_ref, y3_ref, x_ref,
     count_ref, w_ref, obs_ref, sems,
 ):
     copies = [
@@ -110,14 +113,13 @@
         down = jnp.minimum(2 * span + p - j, 2 * span)
         pack(jnp.where(z_odd == 1, down, up), za_ref.at[j])
         pack(jnp.where(z_odd == 1, up, down), zb_ref.at[j])
-        if j == 0:
-            pack(span, own_ref.at[0])
-        else:
-            pack(span + p - lax.bitwise_xor(p, j), own_ref.at[j])
+    pack(span, own_ref)
+    for j, dst in enumerate((near_ref, y2_ref, y3_ref), 1):
+        pack(span + p - lax.bitwise_xor(p, j), dst)
     copies[3].wait()
 
 
-def prepare_kernel(channels, height, x_ref, after_ref, xt_ref, ha_ref, hb_ref):
+def prepare_kernel(channels, height, x_ref, after_ref, xt_ref, hb_ref):
     for start, size in channel_groups(channels):
         n = size * height
         moved = jnp.dot(
@@ -129,23 +131,24 @@
             xt_ref[r * channels + start : r * channels + start + size, :] = (
                 moved[r * size : (r + 1) * size, :]
             )
-    edge_pair(xt_ref, ha_ref, hb_ref, height, channels)
-
-
-def relay_kernel(span, after_ref, za_ref, zb_ref, own_ref, *outs):
+    second_rows(xt_ref, hb_ref, height, channels)
+
+
+def relay_kernel(span, za_ref, zb_ref, near_ref, *refs):
+    near_out, *far_outs = refs[-span + 1 :]
     p, z_odd, _ = place_in_plane(span)
-    for m in range(1, span):
+    near_out[0] = near_ref[...]
+    for m, out in enumerate([near_out.at[1]] + far_outs, 1):
         to = lax.bitwise_xor(p, m)
         below = jnp.where(to < p, 1, 0)
-        outs[m - 1][0] = own_ref[m]
 
         @pl.when(below == z_odd)
         def _():
-            outs[m - 1][1] = za_ref[to]
+            out[...] = za_ref[to]
 
         @pl.when(below != z_odd)
         def _():
-            outs[m - 1][1] = zb_ref[to]
+            out[...] = zb_ref[to]
 
 
 def stack_forward(raw_ref, dst):
@@ -159,18 +162,18 @@
     dst[...] = total.astype(BF16)
 
 
-def stack_backward(raw_ref, dst, shifts):
+def stack_backward(raw_ref, by_row_ref, by_column_ref):
     taps, _, outs, ins = raw_ref.shape
-    n, width = taps * outs, dst.shape[1]
-    src = lax.broadcasted_iota(jnp.int32, (n, width), 0)
-    to = lax.broadcasted_iota(jnp.int32, (n, width), 1)
-    for half, shift in enumerate(shifts):
-        pick = jnp.where(src == to + shift * outs, 1.0, 0.0).astype(BF16)
-        for b in range(taps):
-            block = jnp.concatenate([raw_ref[taps - 1 - a, taps - 1 - b] for a in range(taps)], axis=0)
-            start = (half * taps + b) * ins
-            dst[start : start + ins, :] = lax.dot_general(
-                block, pick, (((0,), (0,)), ((), ())), preferred_element_type=F32
+    n = taps * outs
+    here = lax.broadcasted_iota(jnp.int32, (n, n), 0) == lax.broadcasted_iota(jnp.int32, (n, n), 1)
+    same = jnp.where(here, 1.0, 0.0).astype(BF16)
+    end = taps - 1
+    for i in range(taps):
+        by_row = jnp.concatenate([raw_ref[end - j, end - i] for j in range(taps)], axis=0)
+        by_column = jnp.concatenate([raw_ref[i, end - j] for j in range(taps)], axis=0)
+        for block, dst in ((by_row, by_row_ref), (by_column, by_column_ref)):
+            dst[i * ins : (i + 1) * ins, :] = lax.dot_general(
+                block, same, (((0,), (0,)), ((), ())), preferred_element_type=F32
             ).astype(BF16)
 
 
@@ -188,9 +191,19 @@
     return join_taps(jnp.dot(w_ref[...], window, preferred_element_type=F32), channels)
 
 
-def conv_pair(w_ref, window, channels):
-    taps = jnp.dot(w_ref[...], window, preferred_element_type=F32)
-    return join_taps(taps[: 3 * channels], channels), join_taps(taps[3 * channels :], channels)
+def shifted(row):
+    return jnp.concatenate([pltpu.roll(row, 1, 1), row, pltpu.roll(row, row.shape[1] - 1, 1)], axis=0)
+
+
+def halo_share(w_ref, first, second, above, channels):
+    near, far = (second, first) if above else (first, second)
+    start = channels if above else 0
+    near = jnp.dot(w_ref[start : start + 2 * channels, :], shifted(near), preferred_element_type=F32)
+    start = 2 * channels if above else 0
+    far = jnp.dot(w_ref[start : start + channels, :], shifted(far), preferred_element_type=F32)
+    if above:
+        return near[:channels] + far, near[channels:]
+    return near[:channels], near[channels:] + far
 
 
 def silu_and_slope(act, keep=None):
@@ -219,9 +232,10 @@
 
 def forward_inner_kernel(
     channels, height,
-    xt_ref, raw1_ref, raw2_ref,
-    hid_ref, slope_ref, res_ref, w1_ref, w2_ref,
-):
+    xt_ref, raw1_ref, raw2_ref, after2_ref, after3_ref,
+    hid_ref, slope_ref, res_ref, w1_ref, w2_ref, ha_ref,
+):
+    first_rows(xt_ref, ha_ref, height, channels)
     stack_forward(raw1_ref, w1_ref)
     stack_forward(raw2_ref, w2_ref)
     for i in range(height - 2):
@@ -240,7 +254,7 @@
 def forward_edge_kernel(
     channels, height,
     xt_ref, a_ref, b_ref, hid_ref, w1_ref, w2_ref, raw1_ref, raw2_ref,
-    slope_ref, res_ref, w1t_ref, w2t_ref, above1_ref, above2_ref, below1_ref, below2_ref,
+    slope_ref, res_ref, w1t_ref, w2t_ref, col1_ref, col2_ref,
     top, bottom, hid_top, hid_bottom,
 ):
     odd = lax.axis_index("lat") % 2
@@ -260,33 +274,35 @@
     for i in range(2):
         res_ref[rows(i, 1, channels), :] = conv_row(w2_ref, hid_top, i, channels)
         res_ref[rows(2 + i, 1, channels), :] = conv_row(w2_ref, hid_bottom, i, channels)
-    for raw_ref, full, above, below in (
-        (raw1_ref, w1t_ref, above1_ref, below1_ref),
-        (raw2_ref, w2t_ref, above2_ref, below2_ref),
-    ):
-        stack_backward(raw_ref, full, (0,))
-        stack_backward(raw_ref, above, (0, -1))
-        stack_backward(raw_ref, below, (2, 1))
-
-
-def early_jobs(span, own_ref, za_ref, zb_ref, near_refs):
+    stack_backward(raw1_ref, w1t_ref, col1_ref)
+    stack_backward(raw2_ref, w2t_ref, col2_ref)
+
+
+def direct_job(span, m, ref):
+    p, _, _ = place_in_plane(span)
+    return span + lax.bitwise_xor(p, m) - p, ref
+
+
+def relayed_job(span, m, ref):
+    p, _, _ = place_in_plane(span)
+    step = lax.bitwise_xor(p, m) - p
+    return jnp.where(step > 0, step, 2 * span + step), ref
+
+
+def early_jobs(span, own_ref, za_ref, zb_ref, near_ref, far_refs):
     p, z_odd, _ = place_in_plane(span)
     jobs = [
-        (span, own_ref.at[0]),
+        (span, own_ref),
         (jnp.where(z_odd == 1, 0, 2 * span), za_ref.at[p]),
         (jnp.where(z_odd == 1, 2 * span, 0), zb_ref.at[p]),
+        direct_job(span, 1, near_ref.at[0]),
+        relayed_job(span, 1, near_ref.at[1]),
     ]
-    return jobs + plane_jobs(span, range(1, 1 + len(near_refs)), near_refs)
-
-
-def plane_jobs(span, partners, near_refs):
-    p, _, _ = place_in_plane(span)
-    jobs = []
-    for m, ref in zip(partners, near_refs):
-        step = lax.bitwise_xor(p, m) - p
-        jobs.append((span + step, ref.at[0]))
-        jobs.append((jnp.where(step > 0, step, 2 * span + step), ref.at[1]))
-    return jobs
+    return jobs + [direct_job(span, m, ref) for m, ref in enumerate(far_refs, 2)]
+
+
+def late_jobs(span, far_refs):
+    return [relayed_job(span, m, ref) for m, ref in enumerate(far_refs, 2)]
 
 
 def tile_terms(jobs, route_ref, xt_ref, inner_ref, edge_ref, obs_weight, channels, height, columns):
@@ -335,15 +351,14 @@
 
 def early_tile_kernel(
     channels, height, columns, span,
-    route_hbm, xt_ref, inner_ref, edge_ref, ow_ref, own_ref, za_ref, zb_ref, near_ref,
-    guide_ref,
-    route_ref, sem,
-):
+    route_hbm, xt_ref, inner_ref, edge_ref, ow_ref, own_ref, za_ref, zb_ref, near_ref, *refs,
+):
+    far_refs, (guide_ref, route_ref, sem) = refs[: span - 2], refs[span - 2 :]
     copy = pltpu.make_async_copy(route_hbm, route_ref, sem)
     copy.start()
     guide_ref[...] = jnp.zeros_like(guide_ref)
     copy.wait()
-    jobs = early_jobs(span, own_ref, za_ref, zb_ref, [near_ref])
+    jobs = early_jobs(span, own_ref, za_ref, zb_ref, near_ref, far_refs)
     places, terms = tile_terms(
         jobs, route_ref, xt_ref, inner_ref, edge_ref, as_column(ow_ref[...]), channels, height, columns
     )
@@ -356,12 +371,12 @@
     channels, height, columns, span,
     route_ref, xt_ref, inner_ref, edge_ref, ow_ref, guide_ref, *refs,
 ):
-    near_refs, (late_ref, ga_ref, gb_ref, sums, low) = refs[: span - 2], refs[span - 2 :]
+    far_refs, (late_ref, ga_ref, gb_ref, sums, low) = refs[: span - 2], refs[span - 2 :]
     edge = HALO * channels
     last = (height - HALO) * channels
     sums[0:edge, :] = guide_ref[0:edge, :]
     sums[edge : 2 * edge, :] = guide_ref[last : last + edge, :]
-    jobs = plane_jobs(span, range(2, span), near_refs)
+    jobs = late_jobs(span, far_refs)
     places, terms = tile_terms(
         jobs, route_ref, xt_ref, inner_ref, edge_ref, as_column(ow_ref[...]), channels, height, columns
     )
@@ -372,7 +387,8 @@
             late_ref[index, i] = term[i]
             sums[rows(part * HALO + i, 1, channels), lanes] += term[i].astype(F32)
     low[...] = sums[0 : 2 * edge, :].astype(BF16)
-    edge_pair(low, ga_ref, gb_ref, 2 * HALO, channels)
+    second_rows(low, gb_ref, 2 * HALO, channels)
+    first_rows(low, ga_ref, 2 * HALO, channels)
 
 
 def backward_inner_kernel(
@@ -383,7 +399,7 @@
 ):
     guide[...] = early_ref[...]
     across = columns // BLK_LON
-    jobs = plane_jobs(span, range(2, span), [late_ref] * (span - 2))
+    jobs = late_jobs(span, [late_ref] * (span - 2))
     for index, (k, _) in enumerate(jobs):
         n = route_ref[0, k]
         lanes = pl.ds(pl.multiple_of((n % across) * BLK_LON, BLK_LON), BLK_LON)
@@ -417,22 +433,20 @@
 def backward_edge_kernel(
     channels, height,
     a_ref, b_ref, slope_ref, part_adj_ref, part_score_ref, score_ref,
-    above2_ref, below2_ref, above1_ref, below1_ref,
+    w2_ref, w1_ref,
     out_hbm,
     out_ref, edge_ref, sems,
 ):
     odd = lax.axis_index("lat") % 2
-    first, second = a_ref[...], b_ref[...]
-    for at, window, w2_ref, w1_ref in (
-        (0, jnp.where(odd == 1, first, second), above2_ref, above1_ref),
-        (HALO, jnp.where(odd == 1, second, first), below2_ref, below1_ref),
-    ):
+    a, b = a_ref[...], b_ref[...]
+    for at, window, above in ((0, jnp.where(odd == 1, a, b), True), (HALO, jnp.where(odd == 1, b, a), False)):
         here = [rows(at + i, 1, channels) for i in range(HALO)]
+        share = halo_share(w2_ref, window[:channels], window[channels:], above, channels)
         adj = [
             (slope_ref[place, :] * (part_adj_ref[place, :] + back)).astype(BF16)
-            for place, back in zip(here, conv_pair(w2_ref, window, channels))
+            for place, back in zip(here, share)
         ]
-        for place, back in zip(here, conv_pair(w1_ref, jnp.concatenate(adj, axis=0), channels)):
+        for place, back in zip(here, halo_share(w1_ref, adj[0], adj[1], above, channels)):
             edge_ref[place, :] = (part_score_ref[place, :] + back).astype(BF16)
     copies = []
     for start, size in channel_groups(channels):
@@ -495,11 +509,12 @@
     def in_hbm(x):
         return pltpu.with_memory_space_constraint(x, pltpu.HBM)
 
-    za_send, zb_send, own, x = pl.pallas_call(
+    tile = shape((pack_rows, BLK_LON))
+    za_send, zb_send, own, near, *far, x = pl.pallas_call(
         functools.partial(pack_kernel, channels, span),
-        out_shape=(packed, packed, packed, field(height)),
+        out_shape=(packed, packed) + (tile,) * span + (field(height),),
         in_specs=[HB] * 4,
-        out_specs=[VM] * 4,
+        out_specs=[VM] * (3 + span),
         scratch_shapes=[
             pltpu.SMEM(counts.shape, jnp.int32),
             pltpu.VMEM(tile_weights.shape[1:], BF16),
@@ -514,39 +529,47 @@
         in_hbm(noisy_state.reshape(channels * height, columns)),
     )
     za, zb = swap(za_send, span, 0), swap(zb_send, span, 1)
-    xt, ha, hb = pl.pallas_call(
+    far = [exchange(buf, lambda i, m=m: i ^ m) for m, buf in enumerate(far, 2)]
+    xt, hb = pl.pallas_call(
         functools.partial(prepare_kernel, channels, height),
-        out_shape=(field(height), field(HALO), field(HALO)),
+        out_shape=(field(height), field(HALO)),
         in_specs=[VM, AN],
-        out_specs=[VM] * 3,
+        out_specs=[VM] * 2,
         compiler_params=params(),
     )(x, za_send)
-    ha, hb = swap(ha, 1, 0), swap(hb, 1, 1)
+    hb = swap(hb, 1, 1)
 
     weight = shape((taps * channels, taps * channels))
-    pair_weight = shape((HALO * taps * channels, HALO * channels))
-    hid, slope_in, res_in, w1, w2 = pl.pallas_call(
+    hid, slope_in, res_in, w1, w2, ha = pl.pallas_call(
         functools.partial(forward_inner_kernel, channels, height),
-        out_shape=(field(height - 2), field(height - 2, F32), field(height - 4, F32), weight, weight),
-        in_specs=[VM] * 3,
-        out_specs=[VM] * 5,
-        compiler_params=params(),
-    )(xt, w_first, w_second)
+        out_shape=(
+            field(height - 2),
+            field(height - 2, F32),
+            field(height - 4, F32),
+            weight,
+            weight,
+            field(HALO),
+        ),
+        in_specs=[VM] * 3 + [AN] * len(far),
+        out_specs=[VM] * 6,
+        compiler_params=params(),
+    )(xt, w_first, w_second, *far)
+    ha = swap(ha, 1, 0)
 
     relayed = pl.pallas_call(
         functools.partial(relay_kernel, span),
-        out_shape=tuple(shape((2, pack_rows, BLK_LON)) for _ in range(span - 1)),
-        in_specs=[AN] + [VM] * 3,
+        out_shape=(shape((2, pack_rows, BLK_LON)),) + (tile,) * (span - 2),
+        in_specs=[VM] * 3 + [AN],
         out_specs=[VM] * (span - 1),
         compiler_params=params(),
-    )(w1, za, zb, own)
-    arrived = [exchange(relayed[m - 1], lambda i, m=m: i ^ m) for m in range(1, span)]
-
-    slope_ed, res_ed, w1t, w2t, above1, above2, below1, below2 = pl.pallas_call(
+    )(za, zb, near, w1)
+    near, *last = [exchange(buf, lambda i, m=m: i ^ m) for m, buf in enumerate(relayed, 1)]
+
+    slope_ed, res_ed, w1t, w2t, col1, col2 = pl.pallas_call(
         functools.partial(forward_edge_kernel, channels, height),
-        out_shape=(field(2 * HALO, F32), field(2 * HALO, F32), weight, weight) + (pair_weight,) * 4,
+        out_shape=(field(2 * HALO, F32), field(2 * HALO, F32)) + (weight,) * 4,
         in_specs=[VM] * 8,
-        out_specs=[VM] * 8,
+        out_specs=[VM] * 6,
         scratch_shapes=[buffer(2 * HALO)] * 4,
         compiler_params=params(),
     )(xt, ha, hb, hid, w1, w2, w_first, w_second)
@@ -555,16 +578,16 @@
     early = pl.pallas_call(
         functools.partial(early_tile_kernel, channels, height, columns, span),
         out_shape=field(height, F32),
-        in_specs=[HB] + [VM] * 8,
+        in_specs=[HB] + [VM] * (8 + span - 2),
         out_specs=VM,
         scratch_shapes=[pltpu.SMEM(block_route.shape, jnp.int32), pltpu.SemaphoreType.DMA],
         compiler_params=params(),
-    )(in_hbm(block_route), xt, res_in, res_ed, observed, own, za, zb, arrived[0])
+    )(in_hbm(block_route), xt, res_in, res_ed, observed, own, za, zb, near, *far)
 
     late, ga, gb = pl.pallas_call(
         functools.partial(late_tile_kernel, channels, height, columns, span),
         out_shape=(
-            shape((2 * (span - 2), BLK_LAT, channels, BLK_LON)),
+            shape((span - 2, BLK_LAT, channels, BLK_LON)),
             field(HALO),
             field(HALO),
         ),
@@ -572,7 +595,7 @@
         out_specs=[VM] * 3,
         scratch_shapes=[buffer(3 * HALO, F32), buffer(2 * HALO)],
         compiler_params=params(),
-    )(block_route, xt, res_in, res_ed, observed, early, *arrived[1:])
+    )(block_route, xt, res_in, res_ed, observed, early, *last)
     ga, gb = swap(ga, 1, 0), swap(gb, 1, 1)
 
     part_adj, part_score, score = pl.pallas_call(
@@ -587,7 +610,7 @@
     out = pl.pallas_call(
         functools.partial(backward_edge_kernel, channels, height),
         out_shape=shape((channels * height, columns)),
-        in_specs=[VM] * 10,
+        in_specs=[VM] * 8,
         out_specs=HB,
         scratch_shapes=[
             buffer(height),
@@ -595,7 +618,7 @@
             pltpu.SemaphoreType.DMA((len(channel_groups(channels)),)),
         ],
         compiler_params=params(),
-    )(ga, gb, slope_ed, part_adj, part_score, score, above2, below2, above1, below1)
+    )(ga, gb, slope_ed, part_adj, part_score, score, col2, col1)
     return out.reshape(channels, height, columns)
 
 

time: 39.9 us -> 36.4 us (0.912)
  the two profiles are of different devices: /device:TPU:11 before, /device:TPU:17 now
where the time goes in v5:
time: 36.4 us; the launch traced here: 36.3 us
  Pallas kernels  16.6 us (46%)
  starting transfers between devices  9.99 us (27%)
  waiting for transfers between devices  9.31 us (26%)
    ppermute x11, starting transfers between devices, exchange(): lax.ppermute(x, ('grp', 'lat'), pairs(lax.axis_size('grp'), count, partner))  9.99 us
    ppermute x11, waiting for transfers between devices, exchange(): lax.ppermute(x, ('grp', 'lat'), pairs(lax.axis_size('grp'), count, partner))  9.31 us
    pallas_call x1, Pallas kernels, local(): pl.pallas_call(functools.partial(backward_inner_kernel, channels, height,...  4.63 us
    pallas_call x1, Pallas kernels, local(): pl.pallas_call(functools.partial(backward_edge_kernel, channels, height),...  2.51 us
    pallas_call x1, Pallas kernels, local(): pl.pallas_call(functools.partial(forward_inner_kernel, channels, height),...  2.44 us
    pallas_call x1, Pallas kernels, local(): pl.pallas_call(functools.partial(forward_edge_kernel, channels, height),...  2.13 us
    pallas_call x1, Pallas kernels, local(): pl.pallas_call(functools.partial(pack_kernel, channels, span), out_shape=...  1.59 us
    pallas_call x1, Pallas kernels, local(): pl.pallas_call(functools.partial(early_tile_kernel, channels, height, col...  1.48 us
  transfers between devices with their start and end apart: 11, of which 3 were waited for; matrix products, arithmetic and copies ran while one was open for 0% of the time, Pallas kernels for 31%

profile of v5, /device:TPU:17, one launch (start us, length us, event | category | flops | bytes accessed | tf_op | source)
XLA Modules:
  0.0 36.3 jit_solution(8592741974890623460)
XLA Ops:
  0.0 1.6 %shard_map.91 = (bf16[4,336,128]{2,1,0:T(8,128)(2,1)S(1)}, bf16[4,336,128]{2,1,0:T(8,128)(2,1)S(1)}, bf16[336,128]{1,0:T(8,128)(2,1)S(1)}, bf16[336,128]{1,0:T(8...) custom-call(s32[1,9]{1,0:T(1,128)} %count_hbm.1, ...), custom_call_target="tpu_custom_call" | custom-call | tf_op jit(solution)/shard_map/pallas_call | solution.py:513
  1.6 0.0 copy-start
  1.6 0.0 copy-start.1
  1.6 0.2 collective-permute-start.5
  1.9 2.3 %collective-permute-start.4 = (bf16[4,336,128]{2,1,0:T(8,128)(2,1)S(1)}, bf16[4,336,128]{2,1,0:T(8,128)(2,1)S(1)}, u32[]{:S(2)}, u32[]{:S(2)}) collective-permute-start(bf16[4,336,128]{2,1,0:T(8,128)(2,1)S(1)} %get-tuple-element.36.after_ref), channel_id=1, source_target_pairs={{0,4},{1,5},{2,6},{3,7},{4,0},{5,1},{6,2},{7,3},{8,12},{9,13},{10,... | collective-permute-start | bytes 1032200 | tf_op jit(solution)/shard_map/ppermute | solution.py:503
  4.2 1.2 %collective-permute-start = (bf16[336,128]{1,0:T(8,128)(2,1)S(1)}, bf16[336,128]{1,0:T(8,128)(2,1)S(1)}, u32[]{:S(2)}, u32[]{:S(2)}) collective-permute-start(bf16[336,128]{1,0:T(8,128)(2,1)S(1)} %get-tuple-element.38), channel_id=1, source_target_pairs={{0,2},{1,3},{2,0},{3,1},{4,6},{5,7},{6,4},{7,5},{8,10},{9,11},{10,... | collective-permute-start | bytes 258056 | tf_op jit(solution)/shard_map/ppermute | solution.py:503
  5.4 1.6 %collective-permute-start.1 = (bf16[336,128]{1,0:T(8,128)(2,1)S(1)}, bf16[336,128]{1,0:T(8,128)(2,1)S(1)}, u32[]{:S(2)}, u32[]{:S(2)}) collective-permute-start(bf16[336,128]{1,0:T(8,128)(2,1)S(1)} %get-tuple-element.39), channel_id=1, source_target_pairs={{0,3},{1,2},{2,1},{3,0},{4,7},{5,6},{6,5},{7,4},{8,11},{9,10},{10,... | collective-permute-start | bytes 258056 | tf_op jit(solution)/shard_map/ppermute | solution.py:503
  7.1 0.5 %shard_map.92 = (bf16[640,1024]{1,0:T(8,128)(2,1)S(1)}, bf16[160,1024]{1,0:T(8,128)(2,1)S(1)}) custom-call(bf16[640,1024]{1,0:T(8,128)(2,1)S(1)} %get-tuple-element.35.x_ref, bf16[4,336,128]{2,1,0:T(8,128)(2,1)S(1)} %get-tuple-element.36.after_ref), custom_call_target="tpu_custom_call" | custom-call | tf_op jit(solution)/shard_map/pallas_call | solution.py:533
  7.6 0.2 collective-permute-start.3
  7.8 0.0 collective-permute-done.after2_ref.refs_0_
  7.8 3.5 %collective-permute-done.1.after3_ref.refs_1_ = bf16[336,128]{1,0:T(8,128)(2,1)S(1)} collective-permute-done((bf16[336,128]{1,0:T(8,128)(2,1)S(1)}, bf16[336,128]{1,0:T(8,128)(2,1)S(1)}, u32[]{:S(2)}, u32[]{:S(2)}) %collective-permute-start.1) | collective-permute-done | bytes 86048 | tf_op jit(solution)/shard_map/ppermute | solution.py:503
  11.4 0.0 copy-done
  11.4 0.0 copy-done.1
  11.4 2.4 %shard_map.93 = (bf16[480,1024]{1,0:T(8,128)(2,1)S(1)}, f32[480,1024]{1,0:T(8,128)S(1)}, f32[320,1024]{1,0:T(8,128)S(1)}, bf16[240,240]{1,0:T(8,128)(2,1)S(1)}, ...) custom-call(bf16[640,1024]{1,0:T(8,128)(2,1)S(1)} %get-tuple-element.37.xt_ref, ...), custom_call_target="tpu_custom_call" | custom-call | tf_op jit(solution)/shard_map/pallas_call | solution.py:543
  13.8 0.5 %collective-permute-start.2 = (bf16[160,1024]{1,0:T(8,128)(2,1)S(1)}, bf16[160,1024]{1,0:T(8,128)(2,1)S(1)}, u32[]{:S(2)}, u32[]{:S(2)}) collective-permute-start(bf16[160,1024]{1,0:T(8,128)(2,1)S(1)} %get-tuple-element.41), channel_id=1, source_target_pairs={{0,1},{1,0},{2,3},{3,2},{4,5},{5,4},{6,7},{7,6},{8,9},{9,8},{10,11... | collective-permute-start | bytes 983048 | tf_op jit(solution)/shard_map/ppermute | solution.py:503
  14.3 0.0 collective-permute-done.5.zb_ref
  14.3 0.0 collective-permute-done.4.za_ref
  14.3 0.1 shard_map.95
  14.4 0.2 collective-permute-start.6
  14.5 2.2 %collective-permute-start.7 = (bf16[336,128]{1,0:T(8,128)(2,1)S(1)}, bf16[336,128]{1,0:T(8,128)(2,1)S(1)}, u32[]{:S(2)}, u32[]{:S(2)}) collective-permute-start(bf16[336,128]{1,0:T(8,128)(2,1)S(1)} %get-tuple-element.51), channel_id=1, source_target_pairs={{0,2},{1,3},{2,0},{3,1},{4,6},{5,7},{6,4},{7,5},{8,10},{9,11},{10,... | collective-permute-start | bytes 258056 | tf_op jit(solution)/shard_map/ppermute | solution.py:503
  16.7 0.0 collective-permute-start.8
  16.7 1.7 %collective-permute-done.3.b_ref = bf16[160,1024]{1,0:T(8,128)(2,1)S(1)} collective-permute-done((bf16[160,1024]{1,0:T(8,128)(2,1)S(1)}, bf16[160,1024]{1,0:T(8,128)(2,1)S(1)}, u32[]{:S(2)}, u32[]{:S(2)}) %collective-permute-start.3) | collective-permute-done | bytes 327712 | tf_op jit(solution)/shard_map/ppermute | solution.py:503
  18.5 0.0 collective-permute-done.2.a_ref
  18.5 0.0 copy-start.3
  18.5 2.1 %shard_map.94 = (f32[320,1024]{1,0:T(8,128)S(1)}, f32[320,1024]{1,0:T(8,128)S(1)}, bf16[240,240]{1,0:T(8,128)(2,1)S(1)}, bf16[240,240]{1,0:T(8,128)(2,1)S(1)}, b...) custom-call(bf16[640,1024]{1,0:T(8,128)(2,1)S(1)} %get-tuple-element.37.xt_ref, ...), custom_call_target="tpu_custom_call" | custom-call | tf_op jit(solution)/shard_map/pallas_call | solution.py:568
  20.6 0.0 collective-permute-done.6.near_ref
  20.6 0.0 copy-done.3
  20.6 0.0 copy-start.2
  20.6 1.5 %shard_map.96.guide_ref.early_ref = f32[640,1024]{1,0:T(8,128)S(1)} custom-call(s32[1,9]{1,0:T(1,128)} %route_ref.3, bf16[640,1024]{1,0:T(8,128)(2,1)S(1)} %get-tuple-element.37.xt_ref, f32[320,1024]{1,0:T(8,128)S(1)} %get-tuple-element.40.inner_ref, f32[320,1024]{1,0:T(8,128)S(1)} %get-tuple-element.46.edge_ref, f32[1,80]{1,0:T(1,128)S(1)} %bitcast.4, ...), custom_call_target="tpu_custom_call" | custom-call | tf_op jit(solution)/shard_map/pallas_call | solution.py:578
  22.1 0.0 copy-start.4
  22.1 0.0 collective-permute-done.7.refs_0_
  22.2 0.0 collective-permute-done.8.refs_1_
  22.2 0.0 copy-done.2
  22.2 1.2 %shard_map.97 = (bf16[2,2,80,128]{3,2,1,0:T(8,128)(2,1)S(1)}, bf16[160,1024]{1,0:T(8,128)(2,1)S(1)}, bf16[160,1024]{1,0:T(8,128)(2,1)S(1)}) custom-call(s32[1,9]{1,0:T(1,128)S(1)} %copy-done.2, bf16[640,1024]{1,0:T(8,128)(2,1)S(1)} %get-tuple-element.37.xt_ref, f32[320,1024]{1,0:T(8,128)S(1)} %get-tuple-element.40.inner_ref, ...), custom_call_target="tpu_custom_call" | custom-call | tf_op jit(solution)/shard_map/pallas_call | solution.py:587
  23.4 0.1 collective-permute-start.9
  23.5 1.4 %collective-permute-start.10 = (bf16[160,1024]{1,0:T(8,128)(2,1)S(1)}, bf16[160,1024]{1,0:T(8,128)(2,1)S(1)}, u32[]{:S(2)}, u32[]{:S(2)}) collective-permute-start(bf16[160,1024]{1,0:T(8,128)(2,1)S(1)} %get-tuple-element.54), channel_id=1, source_target_pairs={{0,16},{1,2},{2,1},{3,4},{4,3},{5,6},{6,5},{7,8},{8,7},{9,10},{10,... | collective-permute-start | bytes 983048 | tf_op jit(solution)/shard_map/ppermute | solution.py:503
  24.9 0.0 copy-done.4
  24.9 4.6 %shard_map.98 = (f32[320,1024]{1,0:T(8,128)S(1)}, f32[320,1024]{1,0:T(8,128)S(1)}, bf16[320,1024]{1,0:T(8,128)(2,1)S(1)}) custom-call(s32[1,9]{1,0:T(1,128)S(1)} %copy-done.2, f32[640,1024]{1,0:T(8,128)S(1)} %shard_map.96.guide_ref.early_ref, bf16[2,2,80,128]{3,2,1,0:T(8,128)(2,1)S(1)} %get-tuple-element.56.late_ref, ...), custom_call_target="tpu_custom_call" | custom-call | tf_op jit(solution)/shard_map/pallas_call | solution.py:601
  29.6 0.0 collective-permute-done.9.a_ref
  29.6 4.0 %collective-permute-done.10.b_ref = bf16[160,1024]{1,0:T(8,128)(2,1)S(1)} collective-permute-done((bf16[160,1024]{1,0:T(8,128)(2,1)S(1)}, bf16[160,1024]{1,0:T(8,128)(2,1)S(1)}, u32[]{:S(2)}, u32[]{:S(2)}) %collective-permute-start.10) | collective-permute-done | bytes 327712 | tf_op jit(solution)/shard_map/ppermute | solution.py:503
  33.6 2.5 %shard_map.99 = bf16[640,1024]{1,0:T(8,128)(2,1)} custom-call(bf16[160,1024]{1,0:T(8,128)(2,1)S(1)} %collective-permute-done.9.a_ref, bf16[160,1024]{1,0:T(8,128)(2,1)S(1)} %collective-permute-done.10.b_ref, f32[320,1024]{1,0:T(8,128)S(1)} %get-tuple-element.55.slope_ref, f32[320,1024]{1,0:T(8,128)S(1)} %get-tuple-element.60.part_adj_ref, ...), custom_call_target="tpu_custom_call" | custom-call | tf_op jit(solution)/shard_map/pallas_call | solution.py:610
Async XLA Ops:
  1.6 9.8 %copy-start = (bf16[3,3,80,80]{3,2,1,0:T(8,128)(2,1)S(1)}, bf16[3,3,80,80]{3,2,1,0:T(8,128)(2,1)}, u32[]{:S(2)}) copy-start(bf16[3,3,80,80]{3,2,1,0:T(8,128)(2,1)} %raw1_ref.3) | copy-start | bytes 345604
  1.6 9.7 %copy-start.1 = (bf16[3,3,80,80]{3,2,1,0:T(8,128)(2,1)S(1)}, bf16[3,3,80,80]{3,2,1,0:T(8,128)(2,1)}, u32[]{:S(2)}) copy-start(bf16[3,3,80,80]{3,2,1,0:T(8,128)(2,1)} %raw2_ref.3) | copy-start | bytes 345604
  1.6 12.7 %collective-permute-start.5 = (bf16[4,336,128]{2,1,0:T(8,128)(2,1)S(1)}, bf16[4,336,128]{2,1,0:T(8,128)(2,1)S(1)}, u32[]{:S(2)}, u32[]{:S(2)}) collective-permute-start(bf16[4,336,128]{2,1,0:T(8,128)(2,1)S(1)} %get-tuple-element.48), channel_id=1, source_target_pairs={{0,16},{1,17},{2,18},{3,19},{4,8},{5,9},{6,10},{7,11},{8,4},{9,5},... | collective-permute-start | bytes 1032200 | tf_op jit(solution)/shard_map/ppermute | solution.py:503
  1.9 12.4 %collective-permute-start.4 = (bf16[4,336,128]{2,1,0:T(8,128)(2,1)S(1)}, bf16[4,336,128]{2,1,0:T(8,128)(2,1)S(1)}, u32[]{:S(2)}, u32[]{:S(2)}) collective-permute-start(bf16[4,336,128]{2,1,0:T(8,128)(2,1)S(1)} %get-tuple-element.36.after_ref), channel_id=1, source_target_pairs={{0,4},{1,5},{2,6},{3,7},{4,0},{5,1},{6,2},{7,3},{8,12},{9,13},{10,... | collective-permute-start | bytes 1032200 | tf_op jit(solution)/shard_map/ppermute | solution.py:503
  4.2 3.6 %collective-permute-start = (bf16[336,128]{1,0:T(8,128)(2,1)S(1)}, bf16[336,128]{1,0:T(8,128)(2,1)S(1)}, u32[]{:S(2)}, u32[]{:S(2)}) collective-permute-start(bf16[336,128]{1,0:T(8,128)(2,1)S(1)} %get-tuple-element.38), channel_id=1, source_target_pairs={{0,2},{1,3},{2,0},{3,1},{4,6},{5,7},{6,4},{7,5},{8,10},{9,11},{10,... | collective-permute-start | bytes 258056 | tf_op jit(solution)/shard_map/ppermute | solution.py:503
  5.4 5.9 %collective-permute-start.1 = (bf16[336,128]{1,0:T(8,128)(2,1)S(1)}, bf16[336,128]{1,0:T(8,128)(2,1)S(1)}, u32[]{:S(2)}, u32[]{:S(2)}) collective-permute-start(bf16[336,128]{1,0:T(8,128)(2,1)S(1)} %get-tuple-element.39), channel_id=1, source_target_pairs={{0,3},{1,2},{2,1},{3,0},{4,7},{5,6},{6,5},{7,4},{8,11},{9,10},{10,... | collective-permute-start | bytes 258056 | tf_op jit(solution)/shard_map/ppermute | solution.py:503
  7.6 10.9 %collective-permute-start.3 = (bf16[160,1024]{1,0:T(8,128)(2,1)S(1)}, bf16[160,1024]{1,0:T(8,128)(2,1)S(1)}, u32[]{:S(2)}, u32[]{:S(2)}) collective-permute-start(bf16[160,1024]{1,0:T(8,128)(2,1)S(1)} %get-tuple-element.42), channel_id=1, source_target_pairs={{0,16},{1,2},{2,1},{3,4},{4,3},{5,6},{6,5},{7,8},{8,7},{9,10},{10,... | collective-permute-start | bytes 983048 | tf_op jit(solution)/shard_map/ppermute | solution.py:503
  13.8 4.7 %collective-permute-start.2 = (bf16[160,1024]{1,0:T(8,128)(2,1)S(1)}, bf16[160,1024]{1,0:T(8,128)(2,1)S(1)}, u32[]{:S(2)}, u32[]{:S(2)}) collective-permute-start(bf16[160,1024]{1,0:T(8,128)(2,1)S(1)} %get-tuple-element.41), channel_id=1, source_target_pairs={{0,1},{1,0},{2,3},{3,2},{4,5},{5,4},{6,7},{7,6},{8,9},{9,8},{10,11... | collective-permute-start | bytes 983048 | tf_op jit(solution)/shard_map/ppermute | solution.py:503
  14.4 6.3 %collective-permute-start.6 = (bf16[2,336,128]{2,1,0:T(8,128)(2,1)S(1)}, bf16[2,336,128]{2,1,0:T(8,128)(2,1)S(1)}, u32[]{:S(2)}, u32[]{:S(2)}) collective-permute-start(bf16[2,336,128]{2,1,0:T(8,128)(2,1)S(1)} %get-tuple-element.50), channel_id=1, source_target_pairs={{0,1},{1,0},{2,3},{3,2},{4,5},{5,4},{6,7},{7,6},{8,9},{9,8},{10,11... | collective-permute-start | bytes 516104 | tf_op jit(solution)/shard_map/ppermute | solution.py:503
  14.5 7.6 %collective-permute-start.7 = (bf16[336,128]{1,0:T(8,128)(2,1)S(1)}, bf16[336,128]{1,0:T(8,128)(2,1)S(1)}, u32[]{:S(2)}, u32[]{:S(2)}) collective-permute-start(bf16[336,128]{1,0:T(8,128)(2,1)S(1)} %get-tuple-element.51), channel_id=1, source_target_pairs={{0,2},{1,3},{2,0},{3,1},{4,6},{5,7},{6,4},{7,5},{8,10},{9,11},{10,... | collective-permute-start | bytes 258056 | tf_op jit(solution)/shard_map/ppermute | solution.py:503
  16.7 5.5 %collective-permute-start.8 = (bf16[336,128]{1,0:T(8,128)(2,1)S(1)}, bf16[336,128]{1,0:T(8,128)(2,1)S(1)}, u32[]{:S(2)}, u32[]{:S(2)}) collective-permute-start(bf16[336,128]{1,0:T(8,128)(2,1)S(1)} %get-tuple-element.52), channel_id=1, source_target_pairs={{0,3},{1,2},{2,1},{3,0},{4,7},{5,6},{6,5},{7,4},{8,11},{9,10},{10,... | collective-permute-start | bytes 258056 | tf_op jit(solution)/shard_map/ppermute | solution.py:503
  18.5 2.1 %copy-start.3 = (f32[80]{0:T(128)S(1)}, f32[80]{0:T(128)}, u32[]{:S(2)}) copy-start(f32[80]{0:T(128)} %param.13) | copy-start | bytes 964
  20.6 1.5 %copy-start.2 = (s32[1,9]{1,0:T(1,128)S(1)}, s32[1,9]{1,0:T(1,128)}, u32[]{:S(2)}) copy-start(s32[1,9]{1,0:T(1,128)} %route_ref.3) | copy-start | bytes 112
  22.1 2.8 %copy-start.4 = (f32[80]{0:T(128)S(1)}, f32[80]{0:T(128)}, u32[]{:S(2)}) copy-start(f32[80]{0:T(128)} %param.12) | copy-start | bytes 964
  23.4 6.1 %collective-permute-start.9 = (bf16[160,1024]{1,0:T(8,128)(2,1)S(1)}, bf16[160,1024]{1,0:T(8,128)(2,1)S(1)}, u32[]{:S(2)}, u32[]{:S(2)}) collective-permute-start(bf16[160,1024]{1,0:T(8,128)(2,1)S(1)} %get-tuple-element.53), channel_id=1, source_target_pairs={{0,1},{1,0},{2,3},{3,2},{4,5},{5,4},{6,7},{7,6},{8,9},{9,8},{10,11... | collective-permute-start | bytes 983048 | tf_op jit(solution)/shard_map/ppermute | solution.py:503
  23.5 10.1 %collective-permute-start.10 = (bf16[160,1024]{1,0:T(8,128)(2,1)S(1)}, bf16[160,1024]{1,0:T(8,128)(2,1)S(1)}, u32[]{:S(2)}, u32[]{:S(2)}) collective-permute-start(bf16[160,1024]{1,0:T(8,128)(2,1)S(1)} %get-tuple-element.54), channel_id=1, source_target_pairs={{0,16},{1,2},{2,1},{3,4},{4,3},{5,6},{6,5},{7,8},{8,7},{9,10},{10,... | collective-permute-start | bytes 983048 | tf_op jit(solution)/shard_map/ppermute | solution.py:503

commit v6 on v5

--- a/solution.py
+++ b/solution.py
@@ -60,7 +60,8 @@
     return me % span, (me // span) % 2, me % 2
 
 
-def pack_tile(k, dst, w_ref, obs_ref, count_ref, slots, channels):
+def pack_tile(k, dst, w_ref, obs_ref, count_ref, channels):
+    slots = w_ref.shape[1]
     live = lax.broadcasted_iota(jnp.int32, (slots, BLK_LON), 0) < count_ref[0, k]
     zero = jnp.zeros((slots, BLK_LON), BF16)
     for i in range(BLK_LAT):
@@ -87,11 +88,11 @@
         dst[...] = src_ref[rows((height - HALO) * odd, HALO, channels), :]
 
 
-def pack_kernel(
+def pack_near_kernel(
     channels, span,
     count_hbm, w_hbm, obs_hbm, x_hbm,
-    za_ref, zb_ref, own_ref, near_ref, y2_ref, y3_ref, x_ref,
-    count_ref, w_ref, obs_ref, sems,
+    own_ref, near_ref, y2_ref, y3_ref, x_ref, w_ref, obs_ref,
+    count_ref, sems,
 ):
     copies = [
         pltpu.make_async_copy(count_hbm, count_ref, sems.at[0]),
@@ -103,23 +104,21 @@
         copy.start()
     for copy in copies[:3]:
         copy.wait()
-    p, z_odd, _ = place_in_plane(span)
-    slots = w_ref.shape[1]
-    pack = functools.partial(
-        pack_tile, w_ref=w_ref, obs_ref=obs_ref, count_ref=count_ref, slots=slots, channels=channels
-    )
-    for j in range(span):
-        up = jnp.maximum(p - j, 0)
-        down = jnp.minimum(2 * span + p - j, 2 * span)
-        pack(jnp.where(z_odd == 1, down, up), za_ref.at[j])
-        pack(jnp.where(z_odd == 1, up, down), zb_ref.at[j])
-    pack(span, own_ref)
+    p, _, _ = place_in_plane(span)
+    pack_tile(span, own_ref, w_ref, obs_ref, count_ref, channels)
     for j, dst in enumerate((near_ref, y2_ref, y3_ref), 1):
-        pack(span + p - lax.bitwise_xor(p, j), dst)
+        pack_tile(span + p - lax.bitwise_xor(p, j), dst, w_ref, obs_ref, count_ref, channels)
     copies[3].wait()
 
 
-def prepare_kernel(channels, height, x_ref, after_ref, xt_ref, hb_ref):
+def prepare_kernel(
+    channels, height, span,
+    count_hbm, w_ref, obs_ref, x_ref,
+    za_ref, zb_ref, xt_ref, hb_ref,
+    count_ref, sem,
+):
+    copy = pltpu.make_async_copy(count_hbm, count_ref, sem)
+    copy.start()
     for start, size in channel_groups(channels):
         n = size * height
         moved = jnp.dot(
@@ -132,10 +131,18 @@
                 moved[r * size : (r + 1) * size, :]
             )
     second_rows(xt_ref, hb_ref, height, channels)
-
-
-def relay_kernel(span, za_ref, zb_ref, near_ref, *refs):
-    near_out, *far_outs = refs[-span + 1 :]
+    copy.wait()
+    p, z_odd, _ = place_in_plane(span)
+    for j in range(span):
+        up = jnp.maximum(p - j, 0)
+        down = jnp.minimum(2 * span + p - j, 2 * span)
+        for k, dst in ((jnp.where(z_odd == 1, down, up), za_ref), (jnp.where(z_odd == 1, up, down), zb_ref)):
+            pack_tile(k, dst.at[j], w_ref, obs_ref, count_ref, channels)
+
+
+def relay_kernel(channels, height, span, za_ref, zb_ref, near_ref, xt_ref, *refs):
+    ha_ref, near_out, *far_outs = refs[-span:]
+    first_rows(xt_ref, ha_ref, height, channels)
     p, z_odd, _ = place_in_plane(span)
     near_out[0] = near_ref[...]
     for m, out in enumerate([near_out.at[1]] + far_outs, 1):
@@ -230,17 +237,16 @@
         bottom[edge : 2 * edge, :] = a_ref[...]
 
 
-def forward_inner_kernel(
-    channels, height,
-    xt_ref, raw1_ref, raw2_ref, after2_ref, after3_ref,
-    hid_ref, slope_ref, res_ref, w1_ref, w2_ref, ha_ref,
-):
-    first_rows(xt_ref, ha_ref, height, channels)
+def hidden_inner_kernel(channels, height, xt_ref, raw1_ref, hid_ref, slope_ref, w1_ref):
     stack_forward(raw1_ref, w1_ref)
-    stack_forward(raw2_ref, w2_ref)
     for i in range(height - 2):
         act = conv_row(w1_ref, xt_ref, i, channels)
         hid_ref[rows(i, 1, channels), :], slope_ref[rows(i, 1, channels), :] = silu_and_slope(act)
+
+
+def residual_inner_kernel(channels, height, hid_ref, raw2_ref, *refs):
+    res_ref, w2_ref = refs[-2:]
+    stack_forward(raw2_ref, w2_ref)
     for i in range(height - 4):
         res_ref[rows(i, 1, channels), :] = conv_row(w2_ref, hid_ref, i, channels)
 
@@ -510,17 +516,12 @@
         return pltpu.with_memory_space_constraint(x, pltpu.HBM)
 
     tile = shape((pack_rows, BLK_LON))
-    za_send, zb_send, own, near, *far, x = pl.pallas_call(
-        functools.partial(pack_kernel, channels, span),
-        out_shape=(packed, packed) + (tile,) * span + (field(height),),
+    own, near, *far, x, tw, ob = pl.pallas_call(
+        functools.partial(pack_near_kernel, channels, span),
+        out_shape=(tile,) * span + (field(height), shape(tile_weights.shape[1:]), shape(observations.shape[1:])),
         in_specs=[HB] * 4,
-        out_specs=[VM] * (3 + span),
-        scratch_shapes=[
-            pltpu.SMEM(counts.shape, jnp.int32),
-            pltpu.VMEM(tile_weights.shape[1:], BF16),
-            pltpu.VMEM(observations.shape[1:], BF16),
-            pltpu.SemaphoreType.DMA((4,)),
-        ],
+        out_specs=[VM] * (span + 3),
+        scratch_shapes=[pltpu.SMEM(counts.shape, jnp.int32), pltpu.SemaphoreType.DMA((4,))],
         compiler_params=params(),
     )(
         in_hbm(counts),
@@ -528,41 +529,42 @@
         in_hbm(observations),
         in_hbm(noisy_state.reshape(channels * height, columns)),
     )
-    za, zb = swap(za_send, span, 0), swap(zb_send, span, 1)
     far = [exchange(buf, lambda i, m=m: i ^ m) for m, buf in enumerate(far, 2)]
-    xt, hb = pl.pallas_call(
-        functools.partial(prepare_kernel, channels, height),
-        out_shape=(field(height), field(HALO)),
-        in_specs=[VM, AN],
+    za, zb, xt, hb = pl.pallas_call(
+        functools.partial(prepare_kernel, channels, height, span),
+        out_shape=(packed, packed, field(height), field(HALO)),
+        in_specs=[HB] + [VM] * 3,
+        out_specs=[VM] * 4,
+        scratch_shapes=[pltpu.SMEM(counts.shape, jnp.int32), pltpu.SemaphoreType.DMA],
+        compiler_params=params(),
+    )(in_hbm(counts), tw, ob, x)
+    za, zb, hb = swap(za, span, 0), swap(zb, span, 1), swap(hb, 1, 1)
+
+    weight = shape((taps * channels, taps * channels))
+    hid, slope_in, w1 = pl.pallas_call(
+        functools.partial(hidden_inner_kernel, channels, height),
+        out_shape=(field(height - 2), field(height - 2, F32), weight),
+        in_specs=[VM] * 2,
+        out_specs=[VM] * 3,
+        compiler_params=params(),
+    )(xt, w_first)
+    res_in, w2 = pl.pallas_call(
+        functools.partial(residual_inner_kernel, channels, height),
+        out_shape=(field(height - 4, F32), weight),
+        in_specs=[VM] * 2 + [AN] * len(far),
         out_specs=[VM] * 2,
         compiler_params=params(),
-    )(x, za_send)
-    hb = swap(hb, 1, 1)
-
-    weight = shape((taps * channels, taps * channels))
-    hid, slope_in, res_in, w1, w2, ha = pl.pallas_call(
-        functools.partial(forward_inner_kernel, channels, height),
-        out_shape=(
-            field(height - 2),
-            field(height - 2, F32),
-            field(height - 4, F32),
-            weight,
-            weight,
-            field(HALO),
-        ),
-        in_specs=[VM] * 3 + [AN] * len(far),
-        out_specs=[VM] * 6,
-        compiler_params=params(),
-    )(xt, w_first, w_second, *far)
+        cost_estimate=pl.CostEstimate(flops=20_000_000_000, bytes_accessed=1 << 22, transcendentals=0),
+    )(hid, w_second, *far)
+
+    ha, *relayed = pl.pallas_call(
+        functools.partial(relay_kernel, channels, height, span),
+        out_shape=(field(HALO), shape((2, pack_rows, BLK_LON))) + (tile,) * (span - 2),
+        in_specs=[VM] * 4 + [AN],
+        out_specs=[VM] * span,
+        compiler_params=params(),
+    )(za, zb, near, xt, w2)
     ha = swap(ha, 1, 0)
-
-    relayed = pl.pallas_call(
-        functools.partial(relay_kernel, span),
-        out_shape=(shape((2, pack_rows, BLK_LON)),) + (tile,) * (span - 2),
-        in_specs=[VM] * 3 + [AN],
-        out_specs=[VM] * (span - 1),
-        compiler_params=params(),
-    )(za, zb, near, w1)
     near, *last = [exchange(buf, lambda i, m=m: i ^ m) for m, buf in enumerate(relayed, 1)]
 
     slope_ed, res_ed, w1t, w2t, col1, col2 = pl.pallas_call(

time: 36.4 us -> 41.1 us (1.13)
  the two profiles are of different devices: /device:TPU:17 before, /device:TPU:9 now
where the time goes in v6:
time: 41.1 us; the launch traced here: 40.9 us
  Pallas kernels  17.6 us (43%)
  starting transfers between devices  12.5 us (30%)
  waiting for transfers between devices  10.5 us (26%)
    ppermute x11, starting transfers between devices, exchange(): lax.ppermute(x, ('grp', 'lat'), pairs(lax.axis_size('grp'), count, partner))  12.5 us
    ppermute x11, waiting for transfers between devices, exchange(): lax.ppermute(x, ('grp', 'lat'), pairs(lax.axis_size('grp'), count, partner))  10.5 us
    pallas_call x1, Pallas kernels, local(): pl.pallas_call(functools.partial(backward_inner_kernel, channels, height,...  4.74 us
    pallas_call x1, Pallas kernels, local(): pl.pallas_call(functools.partial(backward_edge_kernel, channels, height),...  2.52 us
    pallas_call x1, Pallas kernels, local(): pl.pallas_call(functools.partial(forward_edge_kernel, channels, height),...  2.15 us
    pallas_call x1, Pallas kernels, local(): pl.pallas_call(functools.partial(hidden_inner_kernel, channels, height),...  1.71 us
    pallas_call x1, Pallas kernels, local(): pl.pallas_call(functools.partial(pack_near_kernel, channels, span), out_s...  1.59 us
    pallas_call x1, Pallas kernels, local(): pl.pallas_call(functools.partial(early_tile_kernel, channels, height, col...  1.48 us
  transfers between devices with their start and end apart: 11, of which 4 were waited for; matrix products, arithmetic and copies ran while one was open for 0% of the time, Pallas kernels for 30%

profile of v6, /device:TPU:9, one launch (start us, length us, event | category | flops | bytes accessed | tf_op | source)
XLA Modules:
  0.0 40.9 jit_solution(694178119101145370)
XLA Ops:
  0.0 1.6 %shard_map.91 = (bf16[336,128]{1,0:T(8,128)(2,1)S(1)}, bf16[336,128]{1,0:T(8,128)(2,1)S(1)}, bf16[336,128]{1,0:T(8,128)(2,1)S(1)}, bf16[336,128]{1,0:T(8,128)(2,...) custom-call(s32[1,9]{1,0:T(1,128)} %count_hbm.3, ...), custom_call_target="tpu_custom_call" | custom-call | tf_op jit(solution)/shard_map/pallas_call | solution.py:519
  1.6 0.0 copy-start
  1.6 1.3 %collective-permute-start = (bf16[336,128]{1,0:T(8,128)(2,1)S(1)}, bf16[336,128]{1,0:T(8,128)(2,1)S(1)}, u32[]{:S(2)}, u32[]{:S(2)}) collective-permute-start(bf16[336,128]{1,0:T(8,128)(2,1)S(1)} %get-tuple-element.42), channel_id=1, source_target_pairs={{0,2},{1,3},{2,0},{3,1},{4,6},{5,7},{6,4},{7,5},{8,10},{9,11},{10,... | collective-permute-start | bytes 258056 | tf_op jit(solution)/shard_map/ppermute | solution.py:509
  2.9 1.1 %collective-permute-start.1 = (bf16[336,128]{1,0:T(8,128)(2,1)S(1)}, bf16[336,128]{1,0:T(8,128)(2,1)S(1)}, u32[]{:S(2)}, u32[]{:S(2)}) collective-permute-start(bf16[336,128]{1,0:T(8,128)(2,1)S(1)} %get-tuple-element.43), channel_id=1, source_target_pairs={{0,3},{1,2},{2,1},{3,0},{4,7},{5,6},{6,5},{7,4},{8,11},{9,10},{10,... | collective-permute-start | bytes 258056 | tf_op jit(solution)/shard_map/ppermute | solution.py:509
  4.0 0.0 copy-start.1
  4.0 1.0 %shard_map.92 = (bf16[4,336,128]{2,1,0:T(8,128)(2,1)S(1)}, bf16[4,336,128]{2,1,0:T(8,128)(2,1)S(1)}, bf16[640,1024]{1,0:T(8,128)(2,1)S(1)}, bf16[160,1024]{1,0:T(8,128)(2,1)S(1)}) custom-call(s32[1,9]{1,0:T(1,128)} %count_hbm.3, bf16[9,128,256]{2,1,0:T(8,128)(2,1)S(1)} %get-tuple-element.37.w_ref, bf16[9,80,128]{2,1,0:T(8,128)(2,1)S(1)} %get-tuple-element.38.obs_ref, ...), custom_call_target="tpu_custom_call" | custom-call | tf_op jit(solution)/shard_map/pallas_call | solution.py:533
  5.0 0.7 %collective-permute-start.5 = (bf16[160,1024]{1,0:T(8,128)(2,1)S(1)}, bf16[160,1024]{1,0:T(8,128)(2,1)S(1)}, u32[]{:S(2)}, u32[]{:S(2)}) collective-permute-start(bf16[160,1024]{1,0:T(8,128)(2,1)S(1)} %get-tuple-element.50), channel_id=1, source_target_pairs={{0,16},{1,2},{2,1},{3,4},{4,3},{5,6},{6,5},{7,8},{8,7},{9,10},{10,... | collective-permute-start | bytes 983048 | tf_op jit(solution)/shard_map/ppermute | solution.py:509
  5.7 0.2 collective-permute-start.2
  5.9 2.4 %collective-permute-start.3 = (bf16[4,336,128]{2,1,0:T(8,128)(2,1)S(1)}, bf16[4,336,128]{2,1,0:T(8,128)(2,1)S(1)}, u32[]{:S(2)}, u32[]{:S(2)}) collective-permute-start(bf16[4,336,128]{2,1,0:T(8,128)(2,1)S(1)} %get-tuple-element.46), channel_id=1, source_target_pairs={{0,16},{1,17},{2,18},{3,19},{4,8},{5,9},{6,10},{7,11},{8,4},{9,5},... | collective-permute-start | bytes 1032200 | tf_op jit(solution)/shard_map/ppermute | solution.py:509
  8.3 0.0 copy-done
  8.3 1.7 %shard_map.93 = (bf16[480,1024]{1,0:T(8,128)(2,1)S(1)}, f32[480,1024]{1,0:T(8,128)S(1)}, bf16[240,240]{1,0:T(8,128)(2,1)S(1)}) custom-call(bf16[640,1024]{1,0:T(8,128)(2,1)S(1)} %get-tuple-element.40.xt_ref, bf16[3,3,80,80]{3,2,1,0:T(8,128)(2,1)S(1)} %copy-done), custom_call_target="tpu_custom_call" | custom-call | tf_op jit(solution)/shard_map/pallas_call | solution.py:544
  10.0 0.0 collective-permute-done.refs_0_
  10.0 0.0 collective-permute-done.1.refs_1_
  10.0 0.0 copy-done.1
  10.1 1.1 %shard_map.94 = (f32[320,1024]{1,0:T(8,128)S(1)}, bf16[240,240]{1,0:T(8,128)(2,1)S(1)}) custom-call(bf16[480,1024]{1,0:T(8,128)(2,1)S(1)} %get-tuple-element.41.hid_ref, bf16[3,3,80,80]{3,2,1,0:T(8,128)(2,1)S(1)} %copy-done.1, bf16[336,128]{1,0:T(8,128)(2,1)S(1)} %collective-permute-done.refs_0_, bf16[336,128]{1,0:T(8,128)(2,1)S(1)} %collective-permute-done.1.refs_1_), custom_call_target="tpu_custom_call" | custom-call | flops 20000000000 | bytes 4194304 | tf_op jit(solution)/shard_map/pallas_call | solution.py:551
  11.2 3.3 %collective-permute-done.2.za_ref = bf16[4,336,128]{2,1,0:T(8,128)(2,1)S(1)} collective-permute-done((bf16[4,336,128]{2,1,0:T(8,128)(2,1)S(1)}, bf16[4,336,128]{2,1,0:T(8,128)(2,1)S(1)}, u32[]{:S(2)}, u32[]{:S(2)}) %collective-permute-start.2) | collective-permute-done | bytes 344096 | tf_op jit(solution)/shard_map/ppermute | solution.py:509
  14.4 2.5 %collective-permute-done.3.zb_ref = bf16[4,336,128]{2,1,0:T(8,128)(2,1)S(1)} collective-permute-done((bf16[4,336,128]{2,1,0:T(8,128)(2,1)S(1)}, bf16[4,336,128]{2,1,0:T(8,128)(2,1)S(1)}, u32[]{:S(2)}, u32[]{:S(2)}) %collective-permute-start.3) | collective-permute-done | bytes 344096 | tf_op jit(solution)/shard_map/ppermute | solution.py:509
  16.9 0.1 shard_map.95
  17.0 3.7 %collective-permute-start.4 = (bf16[160,1024]{1,0:T(8,128)(2,1)S(1)}, bf16[160,1024]{1,0:T(8,128)(2,1)S(1)}, u32[]{:S(2)}, u32[]{:S(2)}) collective-permute-start(bf16[160,1024]{1,0:T(8,128)(2,1)S(1)} %get-tuple-element.49), channel_id=1, source_target_pairs={{0,1},{1,0},{2,3},{3,2},{4,5},{5,4},{6,7},{7,6},{8,9},{9,8},{10,11... | collective-permute-start | bytes 983048 | tf_op jit(solution)/shard_map/ppermute | solution.py:509
  20.7 0.1 collective-permute-start.6
  20.8 0.0 collective-permute-start.7
  20.8 2.1 %collective-permute-start.8 = (bf16[336,128]{1,0:T(8,128)(2,1)S(1)}, bf16[336,128]{1,0:T(8,128)(2,1)S(1)}, u32[]{:S(2)}, u32[]{:S(2)}) collective-permute-start(bf16[336,128]{1,0:T(8,128)(2,1)S(1)} %get-tuple-element.56), channel_id=1, source_target_pairs={{0,3},{1,2},{2,1},{3,0},{4,7},{5,6},{6,5},{7,4},{8,11},{9,10},{10,... | collective-permute-start | bytes 258056 | tf_op jit(solution)/shard_map/ppermute | solution.py:509
  22.8 0.0 collective-permute-done.5.b_ref
  22.8 0.0 collective-permute-done.4.a_ref
  22.8 0.0 copy-start.3
  22.8 2.2 %shard_map.96 = (f32[320,1024]{1,0:T(8,128)S(1)}, f32[320,1024]{1,0:T(8,128)S(1)}, bf16[240,240]{1,0:T(8,128)(2,1)S(1)}, bf16[240,240]{1,0:T(8,128)(2,1)S(1)}, b...) custom-call(bf16[640,1024]{1,0:T(8,128)(2,1)S(1)} %get-tuple-element.40.xt_ref, ...), custom_call_target="tpu_custom_call" | custom-call | tf_op jit(solution)/shard_map/pallas_call | solution.py:570
  25.0 0.0 collective-permute-done.6.near_ref
  25.0 0.0 copy-done.3
  25.0 0.0 copy-start.2
  25.0 1.5 %shard_map.97.guide_ref.early_ref = f32[640,1024]{1,0:T(8,128)S(1)} custom-call(s32[1,9]{1,0:T(1,128)} %route_ref.3, bf16[640,1024]{1,0:T(8,128)(2,1)S(1)} %get-tuple-element.40.xt_ref, f32[320,1024]{1,0:T(8,128)S(1)} %get-tuple-element.44.inner_ref, f32[320,1024]{1,0:T(8,128)S(1)} %get-tuple-element.52.edge_ref, f32[1,80]{1,0:T(1,128)S(1)} %bitcast.4, ...), custom_call_target="tpu_custom_call" | custom-call | tf_op jit(solution)/shard_map/pallas_call | solution.py:580
  26.5 0.0 copy-start.4
  26.5 0.0 collective-permute-done.7.refs_0_
  26.5 0.3 collective-permute-done.8.refs_1_
  26.9 0.0 copy-done.2
  26.9 1.2 %shard_map.98 = (bf16[2,2,80,128]{3,2,1,0:T(8,128)(2,1)S(1)}, bf16[160,1024]{1,0:T(8,128)(2,1)S(1)}, bf16[160,1024]{1,0:T(8,128)(2,1)S(1)}) custom-call(s32[1,9]{1,0:T(1,128)S(1)} %copy-done.2, bf16[640,1024]{1,0:T(8,128)(2,1)S(1)} %get-tuple-element.40.xt_ref, f32[320,1024]{1,0:T(8,128)S(1)} %get-tuple-element.44.inner_ref, ...), custom_call_target="tpu_custom_call" | custom-call | tf_op jit(solution)/shard_map/pallas_call | solution.py:589
  28.1 0.1 collective-permute-start.9
  28.2 0.8 %collective-permute-start.10 = (bf16[160,1024]{1,0:T(8,128)(2,1)S(1)}, bf16[160,1024]{1,0:T(8,128)(2,1)S(1)}, u32[]{:S(2)}, u32[]{:S(2)}) collective-permute-start(bf16[160,1024]{1,0:T(8,128)(2,1)S(1)} %get-tuple-element.58), channel_id=1, source_target_pairs={{0,16},{1,2},{2,1},{3,4},{4,3},{5,6},{6,5},{7,8},{8,7},{9,10},{10,... | collective-permute-start | bytes 983048 | tf_op jit(solution)/shard_map/ppermute | solution.py:509
  29.0 0.0 copy-done.4
  29.0 4.7 %shard_map.99 = (f32[320,1024]{1,0:T(8,128)S(1)}, f32[320,1024]{1,0:T(8,128)S(1)}, bf16[320,1024]{1,0:T(8,128)(2,1)S(1)}) custom-call(s32[1,9]{1,0:T(1,128)S(1)} %copy-done.2, f32[640,1024]{1,0:T(8,128)S(1)} %shard_map.97.guide_ref.early_ref, bf16[2,2,80,128]{3,2,1,0:T(8,128)(2,1)S(1)} %get-tuple-element.60.late_ref, ...), custom_call_target="tpu_custom_call" | custom-call | tf_op jit(solution)/shard_map/pallas_call | solution.py:603
  33.8 0.0 collective-permute-done.9.a_ref
  33.8 4.5 %collective-permute-done.10.b_ref = bf16[160,1024]{1,0:T(8,128)(2,1)S(1)} collective-permute-done((bf16[160,1024]{1,0:T(8,128)(2,1)S(1)}, bf16[160,1024]{1,0:T(8,128)(2,1)S(1)}, u32[]{:S(2)}, u32[]{:S(2)}) %collective-permute-start.10) | collective-permute-done | bytes 327712 | tf_op jit(solution)/shard_map/ppermute | solution.py:509
  38.3 2.5 %shard_map.100 = bf16[640,1024]{1,0:T(8,128)(2,1)} custom-call(bf16[160,1024]{1,0:T(8,128)(2,1)S(1)} %collective-permute-done.9.a_ref, bf16[160,1024]{1,0:T(8,128)(2,1)S(1)} %collective-permute-done.10.b_ref, f32[320,1024]{1,0:T(8,128)S(1)} %get-tuple-element.59.slope_ref, f32[320,1024]{1,0:T(8,128)S(1)} %get-tuple-element.64.part_adj_ref, ...), custom_call_target="tpu_custom_call" | custom-call | tf_op jit(solution)/shard_map/pallas_call | solution.py:612
Async XLA Ops:
  1.6 6.7 %copy-start = (bf16[3,3,80,80]{3,2,1,0:T(8,128)(2,1)S(1)}, bf16[3,3,80,80]{3,2,1,0:T(8,128)(2,1)}, u32[]{:S(2)}) copy-start(bf16[3,3,80,80]{3,2,1,0:T(8,128)(2,1)} %raw1_ref.3) | copy-start | bytes 345604
  1.6 8.4 %collective-permute-start = (bf16[336,128]{1,0:T(8,128)(2,1)S(1)}, bf16[336,128]{1,0:T(8,128)(2,1)S(1)}, u32[]{:S(2)}, u32[]{:S(2)}) collective-permute-start(bf16[336,128]{1,0:T(8,128)(2,1)S(1)} %get-tuple-element.42), channel_id=1, source_target_pairs={{0,2},{1,3},{2,0},{3,1},{4,6},{5,7},{6,4},{7,5},{8,10},{9,11},{10,... | collective-permute-start | bytes 258056 | tf_op jit(solution)/shard_map/ppermute | solution.py:509
  2.9 7.1 %collective-permute-start.1 = (bf16[336,128]{1,0:T(8,128)(2,1)S(1)}, bf16[336,128]{1,0:T(8,128)(2,1)S(1)}, u32[]{:S(2)}, u32[]{:S(2)}) collective-permute-start(bf16[336,128]{1,0:T(8,128)(2,1)S(1)} %get-tuple-element.43), channel_id=1, source_target_pairs={{0,3},{1,2},{2,1},{3,0},{4,7},{5,6},{6,5},{7,4},{8,11},{9,10},{10,... | collective-permute-start | bytes 258056 | tf_op jit(solution)/shard_map/ppermute | solution.py:509
  4.0 6.1 %copy-start.1 = (bf16[3,3,80,80]{3,2,1,0:T(8,128)(2,1)S(1)}, bf16[3,3,80,80]{3,2,1,0:T(8,128)(2,1)}, u32[]{:S(2)}) copy-start(bf16[3,3,80,80]{3,2,1,0:T(8,128)(2,1)} %raw2_ref.3) | copy-start | bytes 345604
  5.0 17.9 %collective-permute-start.5 = (bf16[160,1024]{1,0:T(8,128)(2,1)S(1)}, bf16[160,1024]{1,0:T(8,128)(2,1)S(1)}, u32[]{:S(2)}, u32[]{:S(2)}) collective-permute-start(bf16[160,1024]{1,0:T(8,128)(2,1)S(1)} %get-tuple-element.50), channel_id=1, source_target_pairs={{0,16},{1,2},{2,1},{3,4},{4,3},{5,6},{6,5},{7,8},{8,7},{9,10},{10,... | collective-permute-start | bytes 983048 | tf_op jit(solution)/shard_map/ppermute | solution.py:509
  5.7 8.7 %collective-permute-start.2 = (bf16[4,336,128]{2,1,0:T(8,128)(2,1)S(1)}, bf16[4,336,128]{2,1,0:T(8,128)(2,1)S(1)}, u32[]{:S(2)}, u32[]{:S(2)}) collective-permute-start(bf16[4,336,128]{2,1,0:T(8,128)(2,1)S(1)} %get-tuple-element.45), channel_id=1, source_target_pairs={{0,4},{1,5},{2,6},{3,7},{4,0},{5,1},{6,2},{7,3},{8,12},{9,13},{10,... | collective-permute-start | bytes 1032200 | tf_op jit(solution)/shard_map/ppermute | solution.py:509
  5.9 11.0 %collective-permute-start.3 = (bf16[4,336,128]{2,1,0:T(8,128)(2,1)S(1)}, bf16[4,336,128]{2,1,0:T(8,128)(2,1)S(1)}, u32[]{:S(2)}, u32[]{:S(2)}) collective-permute-start(bf16[4,336,128]{2,1,0:T(8,128)(2,1)S(1)} %get-tuple-element.46), channel_id=1, source_target_pairs={{0,16},{1,17},{2,18},{3,19},{4,8},{5,9},{6,10},{7,11},{8,4},{9,5},... | collective-permute-start | bytes 1032200 | tf_op jit(solution)/shard_map/ppermute | solution.py:509
  17.0 5.8 %collective-permute-start.4 = (bf16[160,1024]{1,0:T(8,128)(2,1)S(1)}, bf16[160,1024]{1,0:T(8,128)(2,1)S(1)}, u32[]{:S(2)}, u32[]{:S(2)}) collective-permute-start(bf16[160,1024]{1,0:T(8,128)(2,1)S(1)} %get-tuple-element.49), channel_id=1, source_target_pairs={{0,1},{1,0},{2,3},{3,2},{4,5},{5,4},{6,7},{7,6},{8,9},{9,8},{10,11... | collective-permute-start | bytes 983048 | tf_op jit(solution)/shard_map/ppermute | solution.py:509
  20.7 4.3 %collective-permute-start.6 = (bf16[2,336,128]{2,1,0:T(8,128)(2,1)S(1)}, bf16[2,336,128]{2,1,0:T(8,128)(2,1)S(1)}, u32[]{:S(2)}, u32[]{:S(2)}) collective-permute-start(bf16[2,336,128]{2,1,0:T(8,128)(2,1)S(1)} %get-tuple-element.54), channel_id=1, source_target_pairs={{0,1},{1,0},{2,3},{3,2},{4,5},{5,4},{6,7},{7,6},{8,9},{9,8},{10,11... | collective-permute-start | bytes 516104 | tf_op jit(solution)/shard_map/ppermute | solution.py:509
  20.8 5.8 %collective-permute-start.7 = (bf16[336,128]{1,0:T(8,128)(2,1)S(1)}, bf16[336,128]{1,0:T(8,128)(2,1)S(1)}, u32[]{:S(2)}, u32[]{:S(2)}) collective-permute-start(bf16[336,128]{1,0:T(8,128)(2,1)S(1)} %get-tuple-element.55), channel_id=1, source_target_pairs={{0,2},{1,3},{2,0},{3,1},{4,6},{5,7},{6,4},{7,5},{8,10},{9,11},{10,... | collective-permute-start | bytes 258056 | tf_op jit(solution)/shard_map/ppermute | solution.py:509
  20.8 6.1 %collective-permute-start.8 = (bf16[336,128]{1,0:T(8,128)(2,1)S(1)}, bf16[336,128]{1,0:T(8,128)(2,1)S(1)}, u32[]{:S(2)}, u32[]{:S(2)}) collective-permute-start(bf16[336,128]{1,0:T(8,128)(2,1)S(1)} %get-tuple-element.56), channel_id=1, source_target_pairs={{0,3},{1,2},{2,1},{3,0},{4,7},{5,6},{6,5},{7,4},{8,11},{9,10},{10,... | collective-permute-start | bytes 258056 | tf_op jit(solution)/shard_map/ppermute | solution.py:509
  22.8 2.2 %copy-start.3 = (f32[80]{0:T(128)S(1)}, f32[80]{0:T(128)}, u32[]{:S(2)}) copy-start(f32[80]{0:T(128)} %param.13) | copy-start | bytes 964
  25.0 1.9 %copy-start.2 = (s32[1,9]{1,0:T(1,128)S(1)}, s32[1,9]{1,0:T(1,128)}, u32[]{:S(2)}) copy-start(s32[1,9]{1,0:T(1,128)} %route_ref.3) | copy-start | bytes 112
  26.5 2.5 %copy-start.4 = (f32[80]{0:T(128)S(1)}, f32[80]{0:T(128)}, u32[]{:S(2)}) copy-start(f32[80]{0:T(128)} %param.12) | copy-start | bytes 964
  28.1 5.7 %collective-permute-start.9 = (bf16[160,1024]{1,0:T(8,128)(2,1)S(1)}, bf16[160,1024]{1,0:T(8,128)(2,1)S(1)}, u32[]{:S(2)}, u32[]{:S(2)}) collective-permute-start(bf16[160,1024]{1,0:T(8,128)(2,1)S(1)} %get-tuple-element.57), channel_id=1, source_target_pairs={{0,1},{1,0},{2,3},{3,2},{4,5},{5,4},{6,7},{7,6},{8,9},{9,8},{10,11... | collective-permute-start | bytes 983048 | tf_op jit(solution)/shard_map/ppermute | solution.py:509
  28.2 10.1 %collective-permute-start.10 = (bf16[160,1024]{1,0:T(8,128)(2,1)S(1)}, bf16[160,1024]{1,0:T(8,128)(2,1)S(1)}, u32[]{:S(2)}, u32[]{:S(2)}) collective-permute-start(bf16[160,1024]{1,0:T(8,128)(2,1)S(1)} %get-tuple-element.58), channel_id=1, source_target_pairs={{0,16},{1,2},{2,1},{3,4},{4,3},{5,6},{6,5},{7,8},{8,7},{9,10},{10,... | collective-permute-start | bytes 983048 | tf_op jit(solution)/shard_map/ppermute | solution.py:509

commit v7 on v5

--- a/solution.py
+++ b/solution.py
@@ -439,13 +439,16 @@
 ):
     odd = lax.axis_index("lat") % 2
     a, b = a_ref[...], b_ref[...]
+    adjoint = []
     for at, window, above in ((0, jnp.where(odd == 1, a, b), True), (HALO, jnp.where(odd == 1, b, a), False)):
         here = [rows(at + i, 1, channels) for i in range(HALO)]
         share = halo_share(w2_ref, window[:channels], window[channels:], above, channels)
-        adj = [
+        rows_here = [
             (slope_ref[place, :] * (part_adj_ref[place, :] + back)).astype(BF16)
             for place, back in zip(here, share)
         ]
+        adjoint.append((here, rows_here, above))
+    for here, adj, above in adjoint:
         for place, back in zip(here, halo_share(w1_ref, adj[0], adj[1], above, channels)):
             edge_ref[place, :] = (part_score_ref[place, :] + back).astype(BF16)
     copies = []
@@ -596,7 +599,7 @@
         scratch_shapes=[buffer(3 * HALO, F32), buffer(2 * HALO)],
         compiler_params=params(),
     )(block_route, xt, res_in, res_ed, observed, early, *last)
-    ga, gb = swap(ga, 1, 0), swap(gb, 1, 1)
+    gb, ga = swap(gb, 1, 1), swap(ga, 1, 0)
 
     part_adj, part_score, score = pl.pallas_call(
         functools.partial(backward_inner_kernel, channels, height, columns, span),

time: 36.4 us -> 36.3 us (level)
  no operation moved by 1% of the time
where the time goes in v7:
time: 36.3 us; the launch traced here: 36.1 us
  Pallas kernels  16.5 us (45%)
  starting transfers between devices  9.99 us (28%)
  waiting for transfers between devices  9.3 us (26%)
    ppermute x11, starting transfers between devices, exchange(): lax.ppermute(x, ('grp', 'lat'), pairs(lax.axis_size('grp'), count, partner))  9.99 us
    ppermute x11, waiting for transfers between devices, exchange(): lax.ppermute(x, ('grp', 'lat'), pairs(lax.axis_size('grp'), count, partner))  9.3 us
    pallas_call x1, Pallas kernels, local(): pl.pallas_call(functools.partial(backward_inner_kernel, channels, height,...  4.64 us
    pallas_call x1, Pallas kernels, local(): pl.pallas_call(functools.partial(forward_inner_kernel, channels, height),...  2.44 us
    pallas_call x1, Pallas kernels, local(): pl.pallas_call(functools.partial(backward_edge_kernel, channels, height),...  2.4 us
    pallas_call x1, Pallas kernels, local(): pl.pallas_call(functools.partial(forward_edge_kernel, channels, height),...  2.13 us
    pallas_call x1, Pallas kernels, local(): pl.pallas_call(functools.partial(pack_kernel, channels, span), out_shape=...  1.59 us
    pallas_call x1, Pallas kernels, local(): pl.pallas_call(functools.partial(early_tile_kernel, channels, height, col...  1.48 us
  transfers between devices with their start and end apart: 11, of which 3 were waited for; matrix products, arithmetic and copies ran while one was open for 0% of the time, Pallas kernels for 31%

profile of v7, /device:TPU:17, one launch (start us, length us, event | category | flops | bytes accessed | tf_op | source)
XLA Modules:
  0.0 36.1 jit_solution(7139822978923921968)
XLA Ops:
  0.0 1.6 %shard_map.91 = (bf16[4,336,128]{2,1,0:T(8,128)(2,1)S(1)}, bf16[4,336,128]{2,1,0:T(8,128)(2,1)S(1)}, bf16[336,128]{1,0:T(8,128)(2,1)S(1)}, bf16[336,128]{1,0:T(8...) custom-call(s32[1,9]{1,0:T(1,128)} %count_hbm.1, ...), custom_call_target="tpu_custom_call" | custom-call | tf_op jit(solution)/shard_map/pallas_call | solution.py:516
  1.6 0.0 copy-start
  1.6 0.0 copy-start.1
  1.6 0.2 collective-permute-start.5
  1.9 2.3 %collective-permute-start.4 = (bf16[4,336,128]{2,1,0:T(8,128)(2,1)S(1)}, bf16[4,336,128]{2,1,0:T(8,128)(2,1)S(1)}, u32[]{:S(2)}, u32[]{:S(2)}) collective-permute-start(bf16[4,336,128]{2,1,0:T(8,128)(2,1)S(1)} %get-tuple-element.36.after_ref), channel_id=1, source_target_pairs={{0,4},{1,5},{2,6},{3,7},{4,0},{5,1},{6,2},{7,3},{8,12},{9,13},{10,... | collective-permute-start | bytes 1032200 | tf_op jit(solution)/shard_map/ppermute | solution.py:506
  4.2 1.2 %collective-permute-start = (bf16[336,128]{1,0:T(8,128)(2,1)S(1)}, bf16[336,128]{1,0:T(8,128)(2,1)S(1)}, u32[]{:S(2)}, u32[]{:S(2)}) collective-permute-start(bf16[336,128]{1,0:T(8,128)(2,1)S(1)} %get-tuple-element.38), channel_id=1, source_target_pairs={{0,2},{1,3},{2,0},{3,1},{4,6},{5,7},{6,4},{7,5},{8,10},{9,11},{10,... | collective-permute-start | bytes 258056 | tf_op jit(solution)/shard_map/ppermute | solution.py:506
  5.4 1.6 %collective-permute-start.1 = (bf16[336,128]{1,0:T(8,128)(2,1)S(1)}, bf16[336,128]{1,0:T(8,128)(2,1)S(1)}, u32[]{:S(2)}, u32[]{:S(2)}) collective-permute-start(bf16[336,128]{1,0:T(8,128)(2,1)S(1)} %get-tuple-element.39), channel_id=1, source_target_pairs={{0,3},{1,2},{2,1},{3,0},{4,7},{5,6},{6,5},{7,4},{8,11},{9,10},{10,... | collective-permute-start | bytes 258056 | tf_op jit(solution)/shard_map/ppermute | solution.py:506
  7.1 0.5 %shard_map.92 = (bf16[640,1024]{1,0:T(8,128)(2,1)S(1)}, bf16[160,1024]{1,0:T(8,128)(2,1)S(1)}) custom-call(bf16[640,1024]{1,0:T(8,128)(2,1)S(1)} %get-tuple-element.35.x_ref, bf16[4,336,128]{2,1,0:T(8,128)(2,1)S(1)} %get-tuple-element.36.after_ref), custom_call_target="tpu_custom_call" | custom-call | tf_op jit(solution)/shard_map/pallas_call | solution.py:536
  7.6 0.2 collective-permute-start.3
  7.8 0.0 collective-permute-done.after2_ref.refs_0_
  7.8 3.5 %collective-permute-done.1.after3_ref.refs_1_ = bf16[336,128]{1,0:T(8,128)(2,1)S(1)} collective-permute-done((bf16[336,128]{1,0:T(8,128)(2,1)S(1)}, bf16[336,128]{1,0:T(8,128)(2,1)S(1)}, u32[]{:S(2)}, u32[]{:S(2)}) %collective-permute-start.1) | collective-permute-done | bytes 86048 | tf_op jit(solution)/shard_map/ppermute | solution.py:506
  11.4 0.0 copy-done
  11.4 0.0 copy-done.1
  11.4 2.4 %shard_map.93 = (bf16[480,1024]{1,0:T(8,128)(2,1)S(1)}, f32[480,1024]{1,0:T(8,128)S(1)}, f32[320,1024]{1,0:T(8,128)S(1)}, bf16[240,240]{1,0:T(8,128)(2,1)S(1)}, ...) custom-call(bf16[640,1024]{1,0:T(8,128)(2,1)S(1)} %get-tuple-element.37.xt_ref, ...), custom_call_target="tpu_custom_call" | custom-call | tf_op jit(solution)/shard_map/pallas_call | solution.py:546
  13.8 0.5 %collective-permute-start.2 = (bf16[160,1024]{1,0:T(8,128)(2,1)S(1)}, bf16[160,1024]{1,0:T(8,128)(2,1)S(1)}, u32[]{:S(2)}, u32[]{:S(2)}) collective-permute-start(bf16[160,1024]{1,0:T(8,128)(2,1)S(1)} %get-tuple-element.41), channel_id=1, source_target_pairs={{0,1},{1,0},{2,3},{3,2},{4,5},{5,4},{6,7},{7,6},{8,9},{9,8},{10,11... | collective-permute-start | bytes 983048 | tf_op jit(solution)/shard_map/ppermute | solution.py:506
  14.3 0.0 collective-permute-done.5.zb_ref
  14.3 0.0 collective-permute-done.4.za_ref
  14.3 0.1 shard_map.95
  14.4 0.2 collective-permute-start.6
  14.5 2.2 %collective-permute-start.7 = (bf16[336,128]{1,0:T(8,128)(2,1)S(1)}, bf16[336,128]{1,0:T(8,128)(2,1)S(1)}, u32[]{:S(2)}, u32[]{:S(2)}) collective-permute-start(bf16[336,128]{1,0:T(8,128)(2,1)S(1)} %get-tuple-element.51), channel_id=1, source_target_pairs={{0,2},{1,3},{2,0},{3,1},{4,6},{5,7},{6,4},{7,5},{8,10},{9,11},{10,... | collective-permute-start | bytes 258056 | tf_op jit(solution)/shard_map/ppermute | solution.py:506
  16.7 0.0 collective-permute-start.8
  16.7 1.7 %collective-permute-done.3.b_ref = bf16[160,1024]{1,0:T(8,128)(2,1)S(1)} collective-permute-done((bf16[160,1024]{1,0:T(8,128)(2,1)S(1)}, bf16[160,1024]{1,0:T(8,128)(2,1)S(1)}, u32[]{:S(2)}, u32[]{:S(2)}) %collective-permute-start.3) | collective-permute-done | bytes 327712 | tf_op jit(solution)/shard_map/ppermute | solution.py:506
  18.5 0.0 collective-permute-done.2.a_ref
  18.5 0.0 copy-start.3
  18.5 2.1 %shard_map.94 = (f32[320,1024]{1,0:T(8,128)S(1)}, f32[320,1024]{1,0:T(8,128)S(1)}, bf16[240,240]{1,0:T(8,128)(2,1)S(1)}, bf16[240,240]{1,0:T(8,128)(2,1)S(1)}, b...) custom-call(bf16[640,1024]{1,0:T(8,128)(2,1)S(1)} %get-tuple-element.37.xt_ref, ...), custom_call_target="tpu_custom_call" | custom-call | tf_op jit(solution)/shard_map/pallas_call | solution.py:571
  20.6 0.0 collective-permute-done.6.near_ref
  20.6 0.0 copy-done.3
  20.6 0.0 copy-start.2
  20.6 1.5 %shard_map.96.guide_ref.early_ref = f32[640,1024]{1,0:T(8,128)S(1)} custom-call(s32[1,9]{1,0:T(1,128)} %route_ref.3, bf16[640,1024]{1,0:T(8,128)(2,1)S(1)} %get-tuple-element.37.xt_ref, f32[320,1024]{1,0:T(8,128)S(1)} %get-tuple-element.40.inner_ref, f32[320,1024]{1,0:T(8,128)S(1)} %get-tuple-element.46.edge_ref, f32[1,80]{1,0:T(1,128)S(1)} %bitcast.4, ...), custom_call_target="tpu_custom_call" | custom-call | tf_op jit(solution)/shard_map/pallas_call | solution.py:581
  22.1 0.0 copy-start.4
  22.2 0.0 collective-permute-done.7.refs_0_
  22.2 0.0 collective-permute-done.8.refs_1_
  22.2 0.0 copy-done.2
  22.2 1.2 %shard_map.97 = (bf16[2,2,80,128]{3,2,1,0:T(8,128)(2,1)S(1)}, bf16[160,1024]{1,0:T(8,128)(2,1)S(1)}, bf16[160,1024]{1,0:T(8,128)(2,1)S(1)}) custom-call(s32[1,9]{1,0:T(1,128)S(1)} %copy-done.2, bf16[640,1024]{1,0:T(8,128)(2,1)S(1)} %get-tuple-element.37.xt_ref, f32[320,1024]{1,0:T(8,128)S(1)} %get-tuple-element.40.inner_ref, ...), custom_call_target="tpu_custom_call" | custom-call | tf_op jit(solution)/shard_map/pallas_call | solution.py:590
  23.4 0.1 collective-permute-start.9
  23.5 1.4 %collective-permute-start.10 = (bf16[160,1024]{1,0:T(8,128)(2,1)S(1)}, bf16[160,1024]{1,0:T(8,128)(2,1)S(1)}, u32[]{:S(2)}, u32[]{:S(2)}) collective-permute-start(bf16[160,1024]{1,0:T(8,128)(2,1)S(1)} %get-tuple-element.54), channel_id=1, source_target_pairs={{0,16},{1,2},{2,1},{3,4},{4,3},{5,6},{6,5},{7,8},{8,7},{9,10},{10,... | collective-permute-start | bytes 983048 | tf_op jit(solution)/shard_map/ppermute | solution.py:506
  24.9 0.0 copy-done.4
  24.9 4.6 %shard_map.98 = (f32[320,1024]{1,0:T(8,128)S(1)}, f32[320,1024]{1,0:T(8,128)S(1)}, bf16[320,1024]{1,0:T(8,128)(2,1)S(1)}) custom-call(s32[1,9]{1,0:T(1,128)S(1)} %copy-done.2, f32[640,1024]{1,0:T(8,128)S(1)} %shard_map.96.guide_ref.early_ref, bf16[2,2,80,128]{3,2,1,0:T(8,128)(2,1)S(1)} %get-tuple-element.56.late_ref, ...), custom_call_target="tpu_custom_call" | custom-call | tf_op jit(solution)/shard_map/pallas_call | solution.py:604
  29.6 0.0 collective-permute-done.9.a_ref
  29.6 4.0 %collective-permute-done.10.b_ref = bf16[160,1024]{1,0:T(8,128)(2,1)S(1)} collective-permute-done((bf16[160,1024]{1,0:T(8,128)(2,1)S(1)}, bf16[160,1024]{1,0:T(8,128)(2,1)S(1)}, u32[]{:S(2)}, u32[]{:S(2)}) %collective-permute-start.10) | collective-permute-done | bytes 327712 | tf_op jit(solution)/shard_map/ppermute | solution.py:506
  33.6 2.4 %shard_map.99 = bf16[640,1024]{1,0:T(8,128)(2,1)} custom-call(bf16[160,1024]{1,0:T(8,128)(2,1)S(1)} %collective-permute-done.9.a_ref, bf16[160,1024]{1,0:T(8,128)(2,1)S(1)} %collective-permute-done.10.b_ref, f32[320,1024]{1,0:T(8,128)S(1)} %get-tuple-element.55.slope_ref, f32[320,1024]{1,0:T(8,128)S(1)} %get-tuple-element.60.part_adj_ref, ...), custom_call_target="tpu_custom_call" | custom-call | tf_op jit(solution)/shard_map/pallas_call | solution.py:613
Async XLA Ops:
  1.6 9.8 %copy-start = (bf16[3,3,80,80]{3,2,1,0:T(8,128)(2,1)S(1)}, bf16[3,3,80,80]{3,2,1,0:T(8,128)(2,1)}, u32[]{:S(2)}) copy-start(bf16[3,3,80,80]{3,2,1,0:T(8,128)(2,1)} %raw1_ref.3) | copy-start | bytes 345604
  1.6 9.7 %copy-start.1 = (bf16[3,3,80,80]{3,2,1,0:T(8,128)(2,1)S(1)}, bf16[3,3,80,80]{3,2,1,0:T(8,128)(2,1)}, u32[]{:S(2)}) copy-start(bf16[3,3,80,80]{3,2,1,0:T(8,128)(2,1)} %raw2_ref.3) | copy-start | bytes 345604
  1.6 12.7 %collective-permute-start.5 = (bf16[4,336,128]{2,1,0:T(8,128)(2,1)S(1)}, bf16[4,336,128]{2,1,0:T(8,128)(2,1)S(1)}, u32[]{:S(2)}, u32[]{:S(2)}) collective-permute-start(bf16[4,336,128]{2,1,0:T(8,128)(2,1)S(1)} %get-tuple-element.48), channel_id=1, source_target_pairs={{0,16},{1,17},{2,18},{3,19},{4,8},{5,9},{6,10},{7,11},{8,4},{9,5},... | collective-permute-start | bytes 1032200 | tf_op jit(solution)/shard_map/ppermute | solution.py:506
  1.9 12.4 %collective-permute-start.4 = (bf16[4,336,128]{2,1,0:T(8,128)(2,1)S(1)}, bf16[4,336,128]{2,1,0:T(8,128)(2,1)S(1)}, u32[]{:S(2)}, u32[]{:S(2)}) collective-permute-start(bf16[4,336,128]{2,1,0:T(8,128)(2,1)S(1)} %get-tuple-element.36.after_ref), channel_id=1, source_target_pairs={{0,4},{1,5},{2,6},{3,7},{4,0},{5,1},{6,2},{7,3},{8,12},{9,13},{10,... | collective-permute-start | bytes 1032200 | tf_op jit(solution)/shard_map/ppermute | solution.py:506
  4.2 3.6 %collective-permute-start = (bf16[336,128]{1,0:T(8,128)(2,1)S(1)}, bf16[336,128]{1,0:T(8,128)(2,1)S(1)}, u32[]{:S(2)}, u32[]{:S(2)}) collective-permute-start(bf16[336,128]{1,0:T(8,128)(2,1)S(1)} %get-tuple-element.38), channel_id=1, source_target_pairs={{0,2},{1,3},{2,0},{3,1},{4,6},{5,7},{6,4},{7,5},{8,10},{9,11},{10,... | collective-permute-start | bytes 258056 | tf_op jit(solution)/shard_map/ppermute | solution.py:506
  5.4 5.9 %collective-permute-start.1 = (bf16[336,128]{1,0:T(8,128)(2,1)S(1)}, bf16[336,128]{1,0:T(8,128)(2,1)S(1)}, u32[]{:S(2)}, u32[]{:S(2)}) collective-permute-start(bf16[336,128]{1,0:T(8,128)(2,1)S(1)} %get-tuple-element.39), channel_id=1, source_target_pairs={{0,3},{1,2},{2,1},{3,0},{4,7},{5,6},{6,5},{7,4},{8,11},{9,10},{10,... | collective-permute-start | bytes 258056 | tf_op jit(solution)/shard_map/ppermute | solution.py:506
  7.6 10.9 %collective-permute-start.3 = (bf16[160,1024]{1,0:T(8,128)(2,1)S(1)}, bf16[160,1024]{1,0:T(8,128)(2,1)S(1)}, u32[]{:S(2)}, u32[]{:S(2)}) collective-permute-start(bf16[160,1024]{1,0:T(8,128)(2,1)S(1)} %get-tuple-element.42), channel_id=1, source_target_pairs={{0,16},{1,2},{2,1},{3,4},{4,3},{5,6},{6,5},{7,8},{8,7},{9,10},{10,... | collective-permute-start | bytes 983048 | tf_op jit(solution)/shard_map/ppermute | solution.py:506
  13.8 4.7 %collective-permute-start.2 = (bf16[160,1024]{1,0:T(8,128)(2,1)S(1)}, bf16[160,1024]{1,0:T(8,128)(2,1)S(1)}, u32[]{:S(2)}, u32[]{:S(2)}) collective-permute-start(bf16[160,1024]{1,0:T(8,128)(2,1)S(1)} %get-tuple-element.41), channel_id=1, source_target_pairs={{0,1},{1,0},{2,3},{3,2},{4,5},{5,4},{6,7},{7,6},{8,9},{9,8},{10,11... | collective-permute-start | bytes 983048 | tf_op jit(solution)/shard_map/ppermute | solution.py:506
  14.4 6.3 %collective-permute-start.6 = (bf16[2,336,128]{2,1,0:T(8,128)(2,1)S(1)}, bf16[2,336,128]{2,1,0:T(8,128)(2,1)S(1)}, u32[]{:S(2)}, u32[]{:S(2)}) collective-permute-start(bf16[2,336,128]{2,1,0:T(8,128)(2,1)S(1)} %get-tuple-element.50), channel_id=1, source_target_pairs={{0,1},{1,0},{2,3},{3,2},{4,5},{5,4},{6,7},{7,6},{8,9},{9,8},{10,11... | collective-permute-start | bytes 516104 | tf_op jit(solution)/shard_map/ppermute | solution.py:506
  14.5 7.6 %collective-permute-start.7 = (bf16[336,128]{1,0:T(8,128)(2,1)S(1)}, bf16[336,128]{1,0:T(8,128)(2,1)S(1)}, u32[]{:S(2)}, u32[]{:S(2)}) collective-permute-start(bf16[336,128]{1,0:T(8,128)(2,1)S(1)} %get-tuple-element.51), channel_id=1, source_target_pairs={{0,2},{1,3},{2,0},{3,1},{4,6},{5,7},{6,4},{7,5},{8,10},{9,11},{10,... | collective-permute-start | bytes 258056 | tf_op jit(solution)/shard_map/ppermute | solution.py:506
  16.7 5.5 %collective-permute-start.8 = (bf16[336,128]{1,0:T(8,128)(2,1)S(1)}, bf16[336,128]{1,0:T(8,128)(2,1)S(1)}, u32[]{:S(2)}, u32[]{:S(2)}) collective-permute-start(bf16[336,128]{1,0:T(8,128)(2,1)S(1)} %get-tuple-element.52), channel_id=1, source_target_pairs={{0,3},{1,2},{2,1},{3,0},{4,7},{5,6},{6,5},{7,4},{8,11},{9,10},{10,... | collective-permute-start | bytes 258056 | tf_op jit(solution)/shard_map/ppermute | solution.py:506
  18.5 2.1 %copy-start.3 = (f32[80]{0:T(128)S(1)}, f32[80]{0:T(128)}, u32[]{:S(2)}) copy-start(f32[80]{0:T(128)} %param.13) | copy-start | bytes 964
  20.6 1.5 %copy-start.2 = (s32[1,9]{1,0:T(1,128)S(1)}, s32[1,9]{1,0:T(1,128)}, u32[]{:S(2)}) copy-start(s32[1,9]{1,0:T(1,128)} %route_ref.3) | copy-start | bytes 112
  22.1 2.8 %copy-start.4 = (f32[80]{0:T(128)S(1)}, f32[80]{0:T(128)}, u32[]{:S(2)}) copy-start(f32[80]{0:T(128)} %param.12) | copy-start | bytes 964
  23.4 6.2 %collective-permute-start.9 = (bf16[160,1024]{1,0:T(8,128)(2,1)S(1)}, bf16[160,1024]{1,0:T(8,128)(2,1)S(1)}, u32[]{:S(2)}, u32[]{:S(2)}) collective-permute-start(bf16[160,1024]{1,0:T(8,128)(2,1)S(1)} %get-tuple-element.53), channel_id=1, source_target_pairs={{0,1},{1,0},{2,3},{3,2},{4,5},{5,4},{6,7},{7,6},{8,9},{9,8},{10,11... | collective-permute-start | bytes 983048 | tf_op jit(solution)/shard_map/ppermute | solution.py:506
  23.5 10.1 %collective-permute-start.10 = (bf16[160,1024]{1,0:T(8,128)(2,1)S(1)}, bf16[160,1024]{1,0:T(8,128)(2,1)S(1)}, u32[]{:S(2)}, u32[]{:S(2)}) collective-permute-start(bf16[160,1024]{1,0:T(8,128)(2,1)S(1)} %get-tuple-element.54), channel_id=1, source_target_pairs={{0,16},{1,2},{2,1},{3,4},{4,3},{5,6},{6,5},{7,8},{8,7},{9,10},{10,... | collective-permute-start | bytes 983048 | tf_op jit(solution)/shard_map/ppermute | solution.py:506

commit v8 on v7

--- a/solution.py
+++ b/solution.py
@@ -289,20 +289,19 @@
     return jnp.where(step > 0, step, 2 * span + step), ref
 
 
-def early_jobs(span, own_ref, za_ref, zb_ref, near_ref, far_refs):
+def early_jobs(span, own_ref, za_ref, zb_ref, far_refs):
     p, z_odd, _ = place_in_plane(span)
     jobs = [
         (span, own_ref),
         (jnp.where(z_odd == 1, 0, 2 * span), za_ref.at[p]),
         (jnp.where(z_odd == 1, 2 * span, 0), zb_ref.at[p]),
-        direct_job(span, 1, near_ref.at[0]),
-        relayed_job(span, 1, near_ref.at[1]),
     ]
     return jobs + [direct_job(span, m, ref) for m, ref in enumerate(far_refs, 2)]
 
 
-def late_jobs(span, far_refs):
-    return [relayed_job(span, m, ref) for m, ref in enumerate(far_refs, 2)]
+def late_jobs(span, near_ref, far_refs):
+    near = [direct_job(span, 1, near_ref.at[0]), relayed_job(span, 1, near_ref.at[1])]
+    return near + [relayed_job(span, m, ref) for m, ref in enumerate(far_refs, 2)]
 
 
 def tile_terms(jobs, route_ref, xt_ref, inner_ref, edge_ref, obs_weight, channels, height, columns):
@@ -351,14 +350,14 @@
 
 def early_tile_kernel(
     channels, height, columns, span,
-    route_hbm, xt_ref, inner_ref, edge_ref, ow_ref, own_ref, za_ref, zb_ref, near_ref, *refs,
+    route_hbm, xt_ref, inner_ref, edge_ref, ow_ref, own_ref, za_ref, zb_ref, *refs,
 ):
     far_refs, (guide_ref, route_ref, sem) = refs[: span - 2], refs[span - 2 :]
     copy = pltpu.make_async_copy(route_hbm, route_ref, sem)
     copy.start()
     guide_ref[...] = jnp.zeros_like(guide_ref)
     copy.wait()
-    jobs = early_jobs(span, own_ref, za_ref, zb_ref, near_ref, far_refs)
+    jobs = early_jobs(span, own_ref, za_ref, zb_ref, far_refs)
     places, terms = tile_terms(
         jobs, route_ref, xt_ref, inner_ref, edge_ref, as_column(ow_ref[...]), channels, height, columns
     )
@@ -371,12 +370,13 @@
     channels, height, columns, span,
     route_ref, xt_ref, inner_ref, edge_ref, ow_ref, guide_ref, *refs,
 ):
-    far_refs, (late_ref, ga_ref, gb_ref, sums, low) = refs[: span - 2], refs[span - 2 :]
+    near_ref, *far_refs = refs[: span - 1]
+    late_ref, ga_ref, gb_ref, sums, low = refs[span - 1 :]
     edge = HALO * channels
     last = (height - HALO) * channels
     sums[0:edge, :] = guide_ref[0:edge, :]
     sums[edge : 2 * edge, :] = guide_ref[last : last + edge, :]
-    jobs = late_jobs(span, far_refs)
+    jobs = late_jobs(span, near_ref, far_refs)
     places, terms = tile_terms(
         jobs, route_ref, xt_ref, inner_ref, edge_ref, as_column(ow_ref[...]), channels, height, columns
     )
@@ -399,7 +399,7 @@
 ):
     guide[...] = early_ref[...]
     across = columns // BLK_LON
-    jobs = late_jobs(span, [late_ref] * (span - 2))
+    jobs = late_jobs(span, late_ref, [late_ref] * (span - 2))
     for index, (k, _) in enumerate(jobs):
         n = route_ref[0, k]
         lanes = pl.ds(pl.multiple_of((n % across) * BLK_LON, BLK_LON), BLK_LON)
@@ -566,7 +566,7 @@
         out_specs=[VM] * (span - 1),
         compiler_params=params(),
     )(za, zb, near, w1)
-    near, *last = [exchange(buf, lambda i, m=m: i ^ m) for m, buf in enumerate(relayed, 1)]
+    last = [exchange(relayed[m - 1], lambda i, m=m: i ^ m) for m in range(span - 1, 0, -1)][::-1]
 
     slope_ed, res_ed, w1t, w2t, col1, col2 = pl.pallas_call(
         functools.partial(forward_edge_kernel, channels, height),
@@ -581,20 +581,20 @@
     early = pl.pallas_call(
         functools.partial(early_tile_kernel, channels, height, columns, span),
         out_shape=field(height, F32),
-        in_specs=[HB] + [VM] * (8 + span - 2),
+        in_specs=[HB] + [VM] * (7 + span - 2),
         out_specs=VM,
         scratch_shapes=[pltpu.SMEM(block_route.shape, jnp.int32), pltpu.SemaphoreType.DMA],
         compiler_params=params(),
-    )(in_hbm(block_route), xt, res_in, res_ed, observed, own, za, zb, near, *far)
+    )(in_hbm(block_route), xt, res_in, res_ed, observed, own, za, zb, *far)
 
     late, ga, gb = pl.pallas_call(
         functools.partial(late_tile_kernel, channels, height, columns, span),
         out_shape=(
-            shape((span - 2, BLK_LAT, channels, BLK_LON)),
+            shape((span, BLK_LAT, channels, BLK_LON)),
             field(HALO),
             field(HALO),
         ),
-        in_specs=[SM] + [VM] * (5 + span - 2),
+        in_specs=[SM] + [VM] * (5 + span - 1),
         out_specs=[VM] * 3,
         scratch_shapes=[buffer(3 * HALO, F32), buffer(2 * HALO)],
         compiler_params=params(),

time: 36.3 us -> 36.3 us (level)
  no operation moved by 1% of the time
where the time goes in v8:
time: 36.3 us; the launch traced here: 36.1 us
  Pallas kernels  16.6 us (46%)
  starting transfers between devices  10 us (28%)
  waiting for transfers between devices  9.2 us (25%)
    ppermute x11, starting transfers between devices, exchange(): lax.ppermute(x, ('grp', 'lat'), pairs(lax.axis_size('grp'), count, partner))  10 us
    ppermute x11, waiting for transfers between devices, exchange(): lax.ppermute(x, ('grp', 'lat'), pairs(lax.axis_size('grp'), count, partner))  9.2 us
    pallas_call x1, Pallas kernels, local(): pl.pallas_call(functools.partial(backward_inner_kernel, channels, height,...  4.66 us
    pallas_call x1, Pallas kernels, local(): pl.pallas_call(functools.partial(forward_inner_kernel, channels, height),...  2.46 us
    pallas_call x1, Pallas kernels, local(): pl.pallas_call(functools.partial(backward_edge_kernel, channels, height),...  2.39 us
    pallas_call x1, Pallas kernels, local(): pl.pallas_call(functools.partial(forward_edge_kernel, channels, height),...  2.13 us
    pallas_call x1, Pallas kernels, local(): pl.pallas_call(functools.partial(pack_kernel, channels, span), out_shape=...  1.59 us
    pallas_call x1, Pallas kernels, local(): pl.pallas_call(functools.partial(early_tile_kernel, channels, height, col...  1.37 us
  transfers between devices with their start and end apart: 11, of which 3 were waited for; matrix products, arithmetic and copies ran while one was open for 0% of the time, Pallas kernels for 31%

profile of v8, /device:TPU:17, one launch (start us, length us, event | category | flops | bytes accessed | tf_op | source)
XLA Modules:
  0.0 36.1 jit_solution(10223613841571820138)
XLA Ops:
  0.0 1.6 %shard_map.91 = (bf16[4,336,128]{2,1,0:T(8,128)(2,1)S(1)}, bf16[4,336,128]{2,1,0:T(8,128)(2,1)S(1)}, bf16[336,128]{1,0:T(8,128)(2,1)S(1)}, bf16[336,128]{1,0:T(8...) custom-call(s32[1,9]{1,0:T(1,128)} %count_hbm.1, ...), custom_call_target="tpu_custom_call" | custom-call | tf_op jit(solution)/shard_map/pallas_call | solution.py:516
  1.6 0.0 copy-start
  1.6 0.0 copy-start.1
  1.6 0.2 collective-permute-start.5
  1.9 2.3 %collective-permute-start.4 = (bf16[4,336,128]{2,1,0:T(8,128)(2,1)S(1)}, bf16[4,336,128]{2,1,0:T(8,128)(2,1)S(1)}, u32[]{:S(2)}, u32[]{:S(2)}) collective-permute-start(bf16[4,336,128]{2,1,0:T(8,128)(2,1)S(1)} %get-tuple-element.36.after_ref), channel_id=1, source_target_pairs={{0,4},{1,5},{2,6},{3,7},{4,0},{5,1},{6,2},{7,3},{8,12},{9,13},{10,... | collective-permute-start | bytes 1032200 | tf_op jit(solution)/shard_map/ppermute | solution.py:506
  4.2 1.2 %collective-permute-start = (bf16[336,128]{1,0:T(8,128)(2,1)S(1)}, bf16[336,128]{1,0:T(8,128)(2,1)S(1)}, u32[]{:S(2)}, u32[]{:S(2)}) collective-permute-start(bf16[336,128]{1,0:T(8,128)(2,1)S(1)} %get-tuple-element.38), channel_id=1, source_target_pairs={{0,2},{1,3},{2,0},{3,1},{4,6},{5,7},{6,4},{7,5},{8,10},{9,11},{10,... | collective-permute-start | bytes 258056 | tf_op jit(solution)/shard_map/ppermute | solution.py:506
  5.4 1.6 %collective-permute-start.1 = (bf16[336,128]{1,0:T(8,128)(2,1)S(1)}, bf16[336,128]{1,0:T(8,128)(2,1)S(1)}, u32[]{:S(2)}, u32[]{:S(2)}) collective-permute-start(bf16[336,128]{1,0:T(8,128)(2,1)S(1)} %get-tuple-element.39), channel_id=1, source_target_pairs={{0,3},{1,2},{2,1},{3,0},{4,7},{5,6},{6,5},{7,4},{8,11},{9,10},{10,... | collective-permute-start | bytes 258056 | tf_op jit(solution)/shard_map/ppermute | solution.py:506
  7.1 0.5 %shard_map.92 = (bf16[640,1024]{1,0:T(8,128)(2,1)S(1)}, bf16[160,1024]{1,0:T(8,128)(2,1)S(1)}) custom-call(bf16[640,1024]{1,0:T(8,128)(2,1)S(1)} %get-tuple-element.35.x_ref, bf16[4,336,128]{2,1,0:T(8,128)(2,1)S(1)} %get-tuple-element.36.after_ref), custom_call_target="tpu_custom_call" | custom-call | tf_op jit(solution)/shard_map/pallas_call | solution.py:536
  7.6 0.2 collective-permute-start.3
  7.8 0.0 collective-permute-done.after2_ref.refs_0_
  7.8 3.5 %collective-permute-done.1.after3_ref.refs_1_ = bf16[336,128]{1,0:T(8,128)(2,1)S(1)} collective-permute-done((bf16[336,128]{1,0:T(8,128)(2,1)S(1)}, bf16[336,128]{1,0:T(8,128)(2,1)S(1)}, u32[]{:S(2)}, u32[]{:S(2)}) %collective-permute-start.1) | collective-permute-done | bytes 86048 | tf_op jit(solution)/shard_map/ppermute | solution.py:506
  11.4 0.0 copy-done
  11.4 0.0 copy-done.1
  11.4 2.5 %shard_map.93 = (bf16[480,1024]{1,0:T(8,128)(2,1)S(1)}, f32[480,1024]{1,0:T(8,128)S(1)}, f32[320,1024]{1,0:T(8,128)S(1)}, bf16[240,240]{1,0:T(8,128)(2,1)S(1)}, ...) custom-call(bf16[640,1024]{1,0:T(8,128)(2,1)S(1)} %get-tuple-element.37.xt_ref, ...), custom_call_target="tpu_custom_call" | custom-call | tf_op jit(solution)/shard_map/pallas_call | solution.py:546
  13.8 0.5 %collective-permute-start.2 = (bf16[160,1024]{1,0:T(8,128)(2,1)S(1)}, bf16[160,1024]{1,0:T(8,128)(2,1)S(1)}, u32[]{:S(2)}, u32[]{:S(2)}) collective-permute-start(bf16[160,1024]{1,0:T(8,128)(2,1)S(1)} %get-tuple-element.41), channel_id=1, source_target_pairs={{0,1},{1,0},{2,3},{3,2},{4,5},{5,4},{6,7},{7,6},{8,9},{9,8},{10,11... | collective-permute-start | bytes 983048 | tf_op jit(solution)/shard_map/ppermute | solution.py:506
  14.3 0.0 collective-permute-done.5.zb_ref
  14.3 0.0 collective-permute-done.4.za_ref
  14.3 0.1 shard_map.96
  14.4 0.2 collective-permute-start.6
  14.5 2.2 %collective-permute-start.7 = (bf16[336,128]{1,0:T(8,128)(2,1)S(1)}, bf16[336,128]{1,0:T(8,128)(2,1)S(1)}, u32[]{:S(2)}, u32[]{:S(2)}) collective-permute-start(bf16[336,128]{1,0:T(8,128)(2,1)S(1)} %get-tuple-element.51), channel_id=1, source_target_pairs={{0,2},{1,3},{2,0},{3,1},{4,6},{5,7},{6,4},{7,5},{8,10},{9,11},{10,... | collective-permute-start | bytes 258056 | tf_op jit(solution)/shard_map/ppermute | solution.py:506
  16.7 0.0 collective-permute-start.8
  16.8 1.7 %collective-permute-done.3.b_ref = bf16[160,1024]{1,0:T(8,128)(2,1)S(1)} collective-permute-done((bf16[160,1024]{1,0:T(8,128)(2,1)S(1)}, bf16[160,1024]{1,0:T(8,128)(2,1)S(1)}, u32[]{:S(2)}, u32[]{:S(2)}) %collective-permute-start.3) | collective-permute-done | bytes 327712 | tf_op jit(solution)/shard_map/ppermute | solution.py:506
  18.5 0.0 collective-permute-done.2.a_ref
  18.5 0.0 copy-start.3
  18.5 2.1 %shard_map.94 = (f32[320,1024]{1,0:T(8,128)S(1)}, f32[320,1024]{1,0:T(8,128)S(1)}, bf16[240,240]{1,0:T(8,128)(2,1)S(1)}, bf16[240,240]{1,0:T(8,128)(2,1)S(1)}, b...) custom-call(bf16[640,1024]{1,0:T(8,128)(2,1)S(1)} %get-tuple-element.37.xt_ref, ...), custom_call_target="tpu_custom_call" | custom-call | tf_op jit(solution)/shard_map/pallas_call | solution.py:571
  20.6 0.0 copy-done.3
  20.6 0.0 copy-start.2
  20.6 1.4 %shard_map.95.guide_ref.early_ref = f32[640,1024]{1,0:T(8,128)S(1)} custom-call(s32[1,9]{1,0:T(1,128)} %route_ref.3, bf16[640,1024]{1,0:T(8,128)(2,1)S(1)} %get-tuple-element.37.xt_ref, f32[320,1024]{1,0:T(8,128)S(1)} %get-tuple-element.40.inner_ref, f32[320,1024]{1,0:T(8,128)S(1)} %get-tuple-element.46.edge_ref, f32[1,80]{1,0:T(1,128)S(1)} %bitcast.4, ...), custom_call_target="tpu_custom_call" | custom-call | tf_op jit(solution)/shard_map/pallas_call | solution.py:581
  22.0 0.0 copy-start.4
  22.0 0.0 collective-permute-done.7.refs_1_
  22.0 0.0 collective-permute-done.8.refs_2_
  22.0 0.0 collective-permute-done.6.refs_0_
  22.0 0.0 copy-done.2
  22.0 1.4 %shard_map.97 = (bf16[4,2,80,128]{3,2,1,0:T(8,128)(2,1)S(1)}, bf16[160,1024]{1,0:T(8,128)(2,1)S(1)}, bf16[160,1024]{1,0:T(8,128)(2,1)S(1)}) custom-call(s32[1,9]{1,0:T(1,128)S(1)} %copy-done.2, bf16[640,1024]{1,0:T(8,128)(2,1)S(1)} %get-tuple-element.37.xt_ref, f32[320,1024]{1,0:T(8,128)S(1)} %get-tuple-element.40.inner_ref, ...), custom_call_target="tpu_custom_call" | custom-call | tf_op jit(solution)/shard_map/pallas_call | solution.py:590
  23.4 0.1 collective-permute-start.9
  23.5 1.4 %collective-permute-start.10 = (bf16[160,1024]{1,0:T(8,128)(2,1)S(1)}, bf16[160,1024]{1,0:T(8,128)(2,1)S(1)}, u32[]{:S(2)}, u32[]{:S(2)}) collective-permute-start(bf16[160,1024]{1,0:T(8,128)(2,1)S(1)} %get-tuple-element.54), channel_id=1, source_target_pairs={{0,16},{1,2},{2,1},{3,4},{4,3},{5,6},{6,5},{7,8},{8,7},{9,10},{10,... | collective-permute-start | bytes 983048 | tf_op jit(solution)/shard_map/ppermute | solution.py:506
  24.9 0.0 copy-done.4
  24.9 4.7 %shard_map.98 = (f32[320,1024]{1,0:T(8,128)S(1)}, f32[320,1024]{1,0:T(8,128)S(1)}, bf16[320,1024]{1,0:T(8,128)(2,1)S(1)}) custom-call(s32[1,9]{1,0:T(1,128)S(1)} %copy-done.2, f32[640,1024]{1,0:T(8,128)S(1)} %shard_map.95.guide_ref.early_ref, bf16[4,2,80,128]{3,2,1,0:T(8,128)(2,1)S(1)} %get-tuple-element.56.late_ref, ...), custom_call_target="tpu_custom_call" | custom-call | tf_op jit(solution)/shard_map/pallas_call | solution.py:604
  29.6 0.0 collective-permute-done.9.a_ref
  29.6 3.9 %collective-permute-done.10.b_ref = bf16[160,1024]{1,0:T(8,128)(2,1)S(1)} collective-permute-done((bf16[160,1024]{1,0:T(8,128)(2,1)S(1)}, bf16[160,1024]{1,0:T(8,128)(2,1)S(1)}, u32[]{:S(2)}, u32[]{:S(2)}) %collective-permute-start.10) | collective-permute-done | bytes 327712 | tf_op jit(solution)/shard_map/ppermute | solution.py:506
  33.6 2.4 %shard_map.99 = bf16[640,1024]{1,0:T(8,128)(2,1)} custom-call(bf16[160,1024]{1,0:T(8,128)(2,1)S(1)} %collective-permute-done.9.a_ref, bf16[160,1024]{1,0:T(8,128)(2,1)S(1)} %collective-permute-done.10.b_ref, f32[320,1024]{1,0:T(8,128)S(1)} %get-tuple-element.55.slope_ref, f32[320,1024]{1,0:T(8,128)S(1)} %get-tuple-element.60.part_adj_ref, ...), custom_call_target="tpu_custom_call" | custom-call | tf_op jit(solution)/shard_map/pallas_call | solution.py:613
Async XLA Ops:
  1.6 9.8 %copy-start = (bf16[3,3,80,80]{3,2,1,0:T(8,128)(2,1)S(1)}, bf16[3,3,80,80]{3,2,1,0:T(8,128)(2,1)}, u32[]{:S(2)}) copy-start(bf16[3,3,80,80]{3,2,1,0:T(8,128)(2,1)} %raw1_ref.3) | copy-start | bytes 345604
  1.6 9.7 %copy-start.1 = (bf16[3,3,80,80]{3,2,1,0:T(8,128)(2,1)S(1)}, bf16[3,3,80,80]{3,2,1,0:T(8,128)(2,1)}, u32[]{:S(2)}) copy-start(bf16[3,3,80,80]{3,2,1,0:T(8,128)(2,1)} %raw2_ref.3) | copy-start | bytes 345604
  1.6 12.7 %collective-permute-start.5 = (bf16[4,336,128]{2,1,0:T(8,128)(2,1)S(1)}, bf16[4,336,128]{2,1,0:T(8,128)(2,1)S(1)}, u32[]{:S(2)}, u32[]{:S(2)}) collective-permute-start(bf16[4,336,128]{2,1,0:T(8,128)(2,1)S(1)} %get-tuple-element.48), channel_id=1, source_target_pairs={{0,16},{1,17},{2,18},{3,19},{4,8},{5,9},{6,10},{7,11},{8,4},{9,5},... | collective-permute-start | bytes 1032200 | tf_op jit(solution)/shard_map/ppermute | solution.py:506
  1.9 12.5 %collective-permute-start.4 = (bf16[4,336,128]{2,1,0:T(8,128)(2,1)S(1)}, bf16[4,336,128]{2,1,0:T(8,128)(2,1)S(1)}, u32[]{:S(2)}, u32[]{:S(2)}) collective-permute-start(bf16[4,336,128]{2,1,0:T(8,128)(2,1)S(1)} %get-tuple-element.36.after_ref), channel_id=1, source_target_pairs={{0,4},{1,5},{2,6},{3,7},{4,0},{5,1},{6,2},{7,3},{8,12},{9,13},{10,... | collective-permute-start | bytes 1032200 | tf_op jit(solution)/shard_map/ppermute | solution.py:506
  4.2 3.6 %collective-permute-start = (bf16[336,128]{1,0:T(8,128)(2,1)S(1)}, bf16[336,128]{1,0:T(8,128)(2,1)S(1)}, u32[]{:S(2)}, u32[]{:S(2)}) collective-permute-start(bf16[336,128]{1,0:T(8,128)(2,1)S(1)} %get-tuple-element.38), channel_id=1, source_target_pairs={{0,2},{1,3},{2,0},{3,1},{4,6},{5,7},{6,4},{7,5},{8,10},{9,11},{10,... | collective-permute-start | bytes 258056 | tf_op jit(solution)/shard_map/ppermute | solution.py:506
  5.4 5.9 %collective-permute-start.1 = (bf16[336,128]{1,0:T(8,128)(2,1)S(1)}, bf16[336,128]{1,0:T(8,128)(2,1)S(1)}, u32[]{:S(2)}, u32[]{:S(2)}) collective-permute-start(bf16[336,128]{1,0:T(8,128)(2,1)S(1)} %get-tuple-element.39), channel_id=1, source_target_pairs={{0,3},{1,2},{2,1},{3,0},{4,7},{5,6},{6,5},{7,4},{8,11},{9,10},{10,... | collective-permute-start | bytes 258056 | tf_op jit(solution)/shard_map/ppermute | solution.py:506
  7.6 10.8 %collective-permute-start.3 = (bf16[160,1024]{1,0:T(8,128)(2,1)S(1)}, bf16[160,1024]{1,0:T(8,128)(2,1)S(1)}, u32[]{:S(2)}, u32[]{:S(2)}) collective-permute-start(bf16[160,1024]{1,0:T(8,128)(2,1)S(1)} %get-tuple-element.42), channel_id=1, source_target_pairs={{0,16},{1,2},{2,1},{3,4},{4,3},{5,6},{6,5},{7,8},{8,7},{9,10},{10,... | collective-permute-start | bytes 983048 | tf_op jit(solution)/shard_map/ppermute | solution.py:506
  13.8 4.6 %collective-permute-start.2 = (bf16[160,1024]{1,0:T(8,128)(2,1)S(1)}, bf16[160,1024]{1,0:T(8,128)(2,1)S(1)}, u32[]{:S(2)}, u32[]{:S(2)}) collective-permute-start(bf16[160,1024]{1,0:T(8,128)(2,1)S(1)} %get-tuple-element.41), channel_id=1, source_target_pairs={{0,1},{1,0},{2,3},{3,2},{4,5},{5,4},{6,7},{7,6},{8,9},{9,8},{10,11... | collective-permute-start | bytes 983048 | tf_op jit(solution)/shard_map/ppermute | solution.py:506
  14.4 7.6 %collective-permute-start.6 = (bf16[2,336,128]{2,1,0:T(8,128)(2,1)S(1)}, bf16[2,336,128]{2,1,0:T(8,128)(2,1)S(1)}, u32[]{:S(2)}, u32[]{:S(2)}) collective-permute-start(bf16[2,336,128]{2,1,0:T(8,128)(2,1)S(1)} %get-tuple-element.50), channel_id=1, source_target_pairs={{0,1},{1,0},{2,3},{3,2},{4,5},{5,4},{6,7},{7,6},{8,9},{9,8},{10,11... | collective-permute-start | bytes 516104 | tf_op jit(solution)/shard_map/ppermute | solution.py:506
  14.5 7.5 %collective-permute-start.7 = (bf16[336,128]{1,0:T(8,128)(2,1)S(1)}, bf16[336,128]{1,0:T(8,128)(2,1)S(1)}, u32[]{:S(2)}, u32[]{:S(2)}) collective-permute-start(bf16[336,128]{1,0:T(8,128)(2,1)S(1)} %get-tuple-element.51), channel_id=1, source_target_pairs={{0,2},{1,3},{2,0},{3,1},{4,6},{5,7},{6,4},{7,5},{8,10},{9,11},{10,... | collective-permute-start | bytes 258056 | tf_op jit(solution)/shard_map/ppermute | solution.py:506
  16.7 5.3 %collective-permute-start.8 = (bf16[336,128]{1,0:T(8,128)(2,1)S(1)}, bf16[336,128]{1,0:T(8,128)(2,1)S(1)}, u32[]{:S(2)}, u32[]{:S(2)}) collective-permute-start(bf16[336,128]{1,0:T(8,128)(2,1)S(1)} %get-tuple-element.52), channel_id=1, source_target_pairs={{0,3},{1,2},{2,1},{3,0},{4,7},{5,6},{6,5},{7,4},{8,11},{9,10},{10,... | collective-permute-start | bytes 258056 | tf_op jit(solution)/shard_map/ppermute | solution.py:506
  18.5 2.1 %copy-start.3 = (f32[80]{0:T(128)S(1)}, f32[80]{0:T(128)}, u32[]{:S(2)}) copy-start(f32[80]{0:T(128)} %param.13) | copy-start | bytes 964
  20.6 1.4 %copy-start.2 = (s32[1,9]{1,0:T(1,128)S(1)}, s32[1,9]{1,0:T(1,128)}, u32[]{:S(2)}) copy-start(s32[1,9]{1,0:T(1,128)} %route_ref.3) | copy-start | bytes 112
  22.0 2.9 %copy-start.4 = (f32[80]{0:T(128)S(1)}, f32[80]{0:T(128)}, u32[]{:S(2)}) copy-start(f32[80]{0:T(128)} %param.12) | copy-start | bytes 964
  23.4 6.2 %collective-permute-start.9 = (bf16[160,1024]{1,0:T(8,128)(2,1)S(1)}, bf16[160,1024]{1,0:T(8,128)(2,1)S(1)}, u32[]{:S(2)}, u32[]{:S(2)}) collective-permute-start(bf16[160,1024]{1,0:T(8,128)(2,1)S(1)} %get-tuple-element.53), channel_id=1, source_target_pairs={{0,1},{1,0},{2,3},{3,2},{4,5},{5,4},{6,7},{7,6},{8,9},{9,8},{10,11... | collective-permute-start | bytes 983048 | tf_op jit(solution)/shard_map/ppermute | solution.py:506
  23.5 10.0 %collective-permute-start.10 = (bf16[160,1024]{1,0:T(8,128)(2,1)S(1)}, bf16[160,1024]{1,0:T(8,128)(2,1)S(1)}, u32[]{:S(2)}, u32[]{:S(2)}) collective-permute-start(bf16[160,1024]{1,0:T(8,128)(2,1)S(1)} %get-tuple-element.54), channel_id=1, source_target_pairs={{0,16},{1,2},{2,1},{3,4},{4,3},{5,6},{6,5},{7,8},{8,7},{9,10},{10,... | collective-permute-start | bytes 983048 | tf_op jit(solution)/shard_map/ppermute | solution.py:506
